TPU v7x, 512 devices: a whole 4x4x16 slice. The times are simulated.
512 devices in a mesh: sector: 32 (over z, core), slab: 16 (over x, y).
Axes of the slice: x: 4, y: 4, z: 16, core: 2. Of those that a mesh axis runs over, the one named last changes fastest.
Arguments:
- image: float32 [48, 64, 128], P('slab', 'sector'), may hold values from 0.2 to 2
- sensitivity: float32 [48, 64, 128], P('slab', 'sector'), may hold values from 0.01 to 0.1
- tile_values: bfloat16 [32, 192, 104, 256], P('sector', 'slab'), may hold values from 0.049804688 to 1
- tile_rows: int32 [32, 192], P('sector', 'slab'), may hold values from 0 to 31
- tile_cols: int32 [32, 192], P('sector', 'slab'), may hold values from 0 to 95
- tile_count: int32 [32, 16], P('sector', 'slab'), may hold values from 2 to 12, as said below
- measured: float32 [32, 32, 104], P('sector'), may hold values from 0 to 3
- background: float32 [32, 32, 104], P('sector'), may hold values from 0.2 to 1
- w_in: bfloat16 [32, 1, 3, 3, 3], replicated, may hold values from -1.25 to 1.25
- w_mid: bfloat16 [3, 32, 32, 3, 3, 3], replicated, may hold values from -0.21875 to 0.21875
- w_out: bfloat16 [1, 32, 3, 3, 3], replicated, may hold values from -0.21875 to 0.21875
- cotangent: float32 [48, 64, 128], P('slab', 'sector'), may hold values from -36 to 36
Outputs:
- new_image: float32 [48, 64, 128], P('slab', 'sector')
- em_grad: float32 [48, 64, 128], P('slab', 'sector')
- grad_in: float32 [32, 1, 3, 3, 3], replicated
- grad_mid: float32 [3, 32, 32, 3, 3, 3], replicated
- grad_out: float32 [1, 32, 3, 3, 3], replicated
Inputs may be any that keep to these rules, and one draw needn't show every extreme that they name: `tile_rows`: row block of a sector, of 32. `tile_cols`: voxel block of a slab, of 96. The first tile_count slots of a device are used; some device uses all 12 in every draw.
All inputs are finite; a program needn't handle non-finite values.
Results may differ from a plain program's by a relative error of at most 0.0085.
The roundings to bfloat16 on the way count: a program that leaves them out, or rounds other values in their place, can miss the bound.
Values may be sent and summed in bfloat16 or wider, within the bound.
No kernel may reach another device: no remote copies, remote signals or barrier semaphores. Data moves between devices by JAX's collectives and lax.ppermute only.
A program may use at most 64 MiB of HBM per device.

v0:
```python
import math

import jax
import jax.numpy as jnp
from jax import lax
from jax.sharding import PartitionSpec as P


def extended(cells, sides, width):
    for axis, dim in sides:
        count = lax.axis_size(axis)
        ends = count - 1
        head = lax.slice_in_dim(cells, 0, width, axis=dim)
        tail = lax.slice_in_dim(cells, cells.shape[dim] - width, cells.shape[dim], axis=dim)
        cells = jnp.concatenate(
            [
                lax.ppermute(tail, axis, [(i, (i + 1) % count) for i in range(ends)]),
                cells,
                lax.ppermute(head, axis, [((i + 1) % count, i) for i in range(ends)]),
            ],
            axis=dim,
        )
    return cells


def conv_valid(padded, kernel):
    result = lax.conv_general_dilated(
        padded[None],
        kernel,
        (1, 1, 1),
        "VALID",
        dimension_numbers=("NCDHW", "OIDHW", "NCDHW"),
        preferred_element_type=jnp.float32,
    )
    return result[0]


def flipped(kernel):
    return jnp.transpose(jnp.flip(kernel, (2, 3, 4)), (1, 0, 2, 3, 4))


def weight_grad(padded, cotan):
    result = lax.conv_general_dilated(
        padded[:, None],
        cotan[:, None],
        (1, 1, 1),
        "VALID",
        dimension_numbers=("NCDHW", "OIDHW", "NCDHW"),
        preferred_element_type=jnp.float32,
    )
    return jnp.transpose(result, (1, 0, 2, 3, 4))


def silu_slope(preact):
    sigma = jax.nn.sigmoid(preact)
    return sigma * (1.0 + preact * (1.0 - sigma))


def extend_rims(field):
    widened = extended(field, (("sector", 2), ("slab", 1)), 1)
    return jnp.pad(widened, ((0, 0), (0, 0), (0, 0), (1, 1)))


def network(em_image, w_in, w_mid, w_out, cotangent):
    kernels = [w_in] + [w_mid[layer] for layer in range(w_mid.shape[0])]
    layer_count = len(kernels)
    current = em_image.astype(jnp.bfloat16)[None]
    padded = []
    preacts = []
    padded.append(extend_rims(current))
    for kernel in kernels:
        preact = conv_valid(padded[-1], kernel)
        preacts.append(preact)
        padded.append(extend_rims(jax.nn.silu(preact).astype(jnp.bfloat16)))
    new_image = em_image + conv_valid(padded[-1], w_out)[0]
    cotan = cotangent.astype(jnp.bfloat16)[None]
    grad_out = weight_grad(padded[-1], cotan)
    back_kernel = w_out
    grads = []
    for layer in range(layer_count - 1, -1, -1):
        inward = conv_valid(extend_rims(cotan), flipped(back_kernel))
        cotan = (silu_slope(preacts[layer]) * inward).astype(jnp.bfloat16)
        grads.append(weight_grad(padded[layer], cotan))
        back_kernel = kernels[layer]
    em_grad = cotangent + conv_valid(extend_rims(cotan), flipped(w_in))[0]
    grads = grads[::-1]
    return (new_image, em_grad, grads[0], jnp.stack(grads[1:]), grad_out)


def shards(
    image,
    sensitivity,
    tile_values,
    tile_rows,
    tile_cols,
    tile_count,
    measured,
    background,
    w_in,
    w_mid,
    w_out,
    cotangent,
):
    sectors = lax.axis_size("sector")
    slabs = lax.axis_size("slab")
    highest = lax.Precision.HIGHEST
    depth_len, rows_len, cols_len = image.shape
    block_len = rows_len * cols_len
    line_blocks = measured.shape[1]
    slot_count = tile_rows.shape[1]
    values_here = tile_values[0]
    rows_here = tile_rows[0]
    cols_here = tile_cols[0]
    weights_here = (jnp.arange(slot_count) < tile_count[0, 0]).astype(jnp.float32) / block_len
    slab_image = lax.all_gather(image.astype(jnp.bfloat16), "sector", axis=1, tiled=True)
    slab_blocks = slab_image.reshape(depth_len * sectors, block_len)
    forward = (
        jnp.einsum(
            "krv,kv->kr", values_here, slab_blocks[cols_here], preferred_element_type=jnp.float32
        )
        * weights_here[:, None]
    )
    placing = (rows_here[None, :] == jnp.arange(line_blocks)[:, None]).astype(jnp.float32)
    partial_rows = jnp.dot(placing, forward, precision=highest)
    own_rows = line_blocks // slabs
    start_row = lax.axis_index("slab") * own_rows
    projection = lax.psum_scatter(partial_rows, "slab", scatter_dimension=0, tiled=True)
    measured_own = lax.dynamic_slice_in_dim(measured[0], start_row, own_rows, 0)
    background_own = lax.dynamic_slice_in_dim(background[0], start_row, own_rows, 0)
    ratio_own = (measured_own / (projection + background_own)).astype(jnp.bfloat16)
    ratio = lax.all_gather(ratio_own, "slab", axis=0, tiled=True)
    backward = (
        jnp.einsum("krv,kr->kv", values_here, ratio[rows_here], preferred_element_type=jnp.float32)
        * weights_here[:, None]
    )
    every_back, every_cols = (
        lax.all_gather(backward, "sector", axis=0, tiled=True),
        lax.all_gather(cols_here, "sector", axis=0, tiled=True),
    )
    wanted = jnp.arange(depth_len) * sectors + lax.axis_index("sector")
    owning = (every_cols[None, :] == wanted[:, None]).astype(jnp.float32)
    back_image = jnp.dot(owning, every_back, precision=highest).reshape(
        depth_len, rows_len, cols_len
    )
    em_image = image * back_image / sensitivity
    new_image, em_grad, grad_in, grad_mid, grad_out = network(
        em_image, w_in, w_mid, w_out, cotangent
    )
    summed = lax.psum((grad_in, grad_mid, grad_out), ("sector", "slab"))
    factor = 1.0 / math.sqrt(depth_len * slabs * rows_len * sectors * cols_len)
    return (new_image, em_grad, summed[0] * factor, summed[1] * factor, summed[2] * factor)


def solution(mesh):
    placed = (
        P("slab", "sector", None),
        P("slab", "sector", None),
        P("sector", "slab", None, None),
        P("sector", "slab"),
        P("sector", "slab"),
        P("sector", "slab"),
        P("sector", None, None),
        P("sector", None, None),
        P(),
        P(),
        P(),
        P("slab", "sector", None),
    )
    return jax.shard_map(
        shards,
        mesh=mesh,
        in_specs=placed,
        out_specs=(P("slab", "sector", None), P("slab", "sector", None), P(), P(), P()),
        check_vma=False,
    )
```

profile of v0, /device:TPU:1, one launch (start us, length us, event | category | flops | bytes accessed | tf_op | source)
XLA Modules:
  0.0 881.3 jit_solution(14488568226628041290)
XLA Ops:
  8.0 37.7 %all_gather.13 = bf16[3,64,128]{2,0,1:T(4,128)(2,1)S(1)} all-gather(bf16[3,2,128]{2,0,1:T(4,128)(2,1)S(1)} %copy.334), channel_id=1, replica_groups=mesh['sector'=32,'slab'=16] {'sector'}, dimensions={1}, use_global_device_ids=true | all-gather | bytes 50688 | tf_op jit(solution)/shard_map/all_gather | solution.py:115
  49.5 60.7 %all-reduce.11 = f32[32,104]{1,0:T(8,128)S(1)} all-reduce(f32[32,104]{1,0:T(8,128)S(1)} %fusion.150), channel_id=3, replica_groups=mesh['sector'=32,'slab'=16] {'slab'}, use_global_device_ids=true, to_apply=%region_0.0.clone | all-reduce | flops 3328 | bytes 26624
  112.8 13.0 %all-gather.1 = bf16[16,2,104]{2,1,0:T(2,128)(2,1)S(1)} all-gather(bf16[1,2,104]{2,1,0:T(2,128)(2,1)S(1)} %fusion.176), channel_id=1, replica_groups=mesh['sector'=32,'slab'=16] {'slab'}, dimensions={0}, use_global_device_ids=true | all-gather | bytes 7072 | tf_op jit(solution)/shard_map/all_gather | solution.py:131
  126.6 46.2 %all-gather.2 = f32[32,12,256]{2,1,0:T(8,128)S(1)} all-gather(f32[1,12,256]{2,1,0:T(8,128)S(1)} %fusion.149), channel_id=1, replica_groups=mesh['sector'=32,'slab'=16] {'sector'}, dimensions={0}, use_global_device_ids=true | all-gather | bytes 405504 | tf_op jit(solution)/shard_map/all_gather | solution.py:137
  174.9 15.9 %all-reduce.10 = s32[384]{0:T(512)S(1)} all-reduce(s32[384]{0:T(512)S(1)} %bitcast_dynamic-update-slice_fusion), channel_id=2, replica_groups=mesh['sector'=32,'slab'=16] {'sector'}, use_global_device_ids=true, to_apply=%add.10 | all-reduce | flops 384 | bytes 3072
  191.7 5.5 collective-permute-start.1
  197.2 2.4 collective-permute-start
  201.7 4.5 collective-permute-start.2
  209.0 2.9 collective-permute-start.5
  211.9 4.0 collective-permute-start.4
  216.0 1.9 collective-permute-start.21
  217.9 3.6 collective-permute-start.20
  224.1 4.5 collective-permute-start.6
  230.0 4.3 collective-permute-start.22
  236.3 1.9 convolution_select_fusion.7
  238.7 1.9 collective-permute-start.9
  240.6 3.6 collective-permute-start.8
  246.5 4.4 collective-permute-start.10
  253.8 1.9 convolution_select_fusion.6
  256.3 1.9 collective-permute-start.13
  258.2 5.1 collective-permute-start.12
  265.5 6.8 collective-permute-start.14
  272.9 3.0 copy.384
  277.2 2.4 copy.388
  282.6 1.9 convolution_select_fusion.5
  286.2 1.9 collective-permute-start.17
  288.2 4.5 collective-permute-start.16
  293.3 1.9 collective-permute-start.25
  295.2 3.6 collective-permute-start.24
  298.8 2.8 copy.390
  303.4 7.8 convolution_bitcast_fusion
  313.3 6.1 collective-permute-start.26
  321.5 6.6 collective-permute-start.18
  340.7 3.6 collective-permute-start.28
  345.4 7.9 convolution_bitcast_fusion.1
  356.1 7.1 collective-permute-start.30
  363.8 2.4 copy.392
  370.3 1.9 collective-permute-start.33
  372.2 3.6 collective-permute-start.32
  376.3 5.8 convolution_bitcast_fusion.2
  383.5 6.1 collective-permute-start.34
  394.7 1.9 collective-permute-start.37
  396.6 3.6 collective-permute-start.36
  402.5 6.4 collective-permute-start.38
  408.9 11.0 %convolution_bitcast_fusion.4 = f32[32,1,3,3,3]{0,1,4,3,2:T(1,128)S(1)} fusion(bf16[1,1,5,4,130]{1,0,4,3,2:T(2,128)(2,1)S(1)} %copy-done.5, bf16[32,1,3,2,128]{0,1,4,3,2:T(2,128)(2,1)S(1)} %copy.385), kind=kOutput, calls=%fused_computation.26 | convolution fusion | flops 1327104 | bytes 57808 | tf_op jit(solution)/shard_map/conv_general_dilated | solution.py:43
  424.8 6.0 convolution_bitcast_fusion.3
  430.7 120.2 %all-reduce.12 = (f32[32,1,3,3,3]{0,1,4,3,2:T(1,128)S(1)}, f32[1,32,3,3,3]{1,0,4,3,2:T(1,128)S(1)}) all-reduce(f32[32,1,3,3,3]{0,1,4,3,2:T(1,128)S(1)} %convolution_bitcast_fusion.4, f32[1,32,3,3,3]{1,0,4,3,2:T(1,128)S(1)} %convolution_bitcast_fusion.3), channel_id=1, replica_groups=mesh['sector'=32,'slab'=16] {'sector','slab'}, use_global_device_ids=true, to_apply=%region_1.2 | all-reduce | flops 1728 | bytes 13824 | tf_op jit(solution)/shard_map/psum | solution.py:149
  552.2 319.1 %all-reduce.15.cloned.1.call-done = f32[3,32,32,3,3,3]{1,2,5,4,3,0:T(8,128)} async-done(((f32[3,32,32,3,3,3]{1,2,5,4,3,0:T(8,128)}), f32[3,32,32,3,3,3]{1,2,5,4,3,0:T(8,128)}) %all-reduce.15.cloned.1.call-update) | async-done | bytes 331792 | tf_op jit(solution)/shard_map/psum | solution.py:149
  (287 shorter events, 79.2 us)
Async XLA Ops:
  7.2 41.2 %copy-start = (bf16[1,12,104,256]{3,2,1,0:T(8,128)(2,1)S(1)}, bf16[1,12,104,256]{3,2,1,0:T(8,128)(2,1)}, u32[]{:S(2)}) copy-start(bf16[1,12,104,256]{3,2,1,0:T(8,128)(2,1)} %param.14) | copy-start | bytes 1916932
  7.2 864.1 %all-reduce.15.cloned.1.call-start = ((), (), s32[]{:S(2)}) async-start(), calls=%async_computation | async-start | bytes 2654208 | tf_op jit(solution)/shard_map/psum | solution.py:149
  48.6 126.2 %copy-start.33 = (s32[1,12]{1,0:T(1,128)S(1)}, s32[1,12]{1,0:T(1,128)}, u32[]{:S(2)}) copy-start(s32[1,12]{1,0:T(1,128)} %param.16) | copy-start | bytes 148
  110.2 81.0 %copy-start.18 = (f32[3,2,128]{2,1,0:T(2,128)S(1)}, f32[3,2,128]{2,1,0:T(2,128)}, u32[]{:S(2)}) copy-start(f32[3,2,128]{2,1,0:T(2,128)} %param.12) | copy-start | bytes 9220
  110.2 81.0 %copy-start.31 = (f32[3,2,128]{2,1,0:T(2,128)S(1)}, f32[3,2,128]{2,1,0:T(2,128)}, u32[]{:S(2)}) copy-start(f32[3,2,128]{2,1,0:T(2,128)} %param.13) | copy-start | bytes 9220
  125.8 80.4 %copy-start.20 = (f32[3,2,128]{2,1,0:T(2,128)S(1)}, f32[3,2,128]{2,1,0:T(2,128)}, u32[]{:S(2)}) copy-start(f32[3,2,128]{2,1,0:T(2,128)} %param.23) | copy-start | bytes 9220
  126.6 81.0 %copy-start.22 = (bf16[32,1,3,3,3]{0,4,3,2,1:T(4,128)(2,1)S(1)}, bf16[32,1,3,3,3]{0,4,3,2,1:T(4,128)(2,1)}, u32[]{:S(2)}) copy-start(bf16[32,1,3,3,3]{0,4,3,2,1:T(4,128)(2,1)} %param.20) | copy-start | bytes 5188
  126.6 81.0 %copy-start.34 = (pred[8,17]{0,1:T(8,128)(4,1)S(1)}, pred[8,17]{0,1:T(8,128)(4,1)}, u32[]{:S(2)}) copy-start(pred[8,17]{0,1:T(8,128)(4,1)} %constant.109) | copy-start | bytes 412
  191.7 7.9 collective-permute-start.1
  197.2 3.1 collective-permute-start
  200.4 5.9 collective-permute-start.3
  201.7 5.3 collective-permute-start.2
  209.0 13.8 %collective-permute-start.5 = (bf16[32,3,1,128]{3,0,2,1:T(8,128)(2,1)S(1)}, bf16[32,3,1,128]{3,0,2,1:T(8,128)(2,1)S(1)}, u32[]{:S(2)}, u32[]{:S(2)}) collective-permute-start(bf16[32,3,1,128]{3,0,2,1:T(8,128)(2,1)S(1)} %get-tuple-element.85), channel_id=1, source_target_pairs={{16,0},{32,16},{48,32},{64,48},{80,64},{96,80},{112,96},{128,112},... | collective-permute-start | bytes 73736 | tf_op jit(solution)/shard_map/ppermute | solution.py:19
  211.9 10.9 %collective-permute-start.4 = (bf16[32,3,1,128]{3,0,2,1:T(8,128)(2,1)S(1)}, bf16[32,3,1,128]{3,0,2,1:T(8,128)(2,1)S(1)}, u32[]{:S(2)}, u32[]{:S(2)}) collective-permute-start(bf16[32,3,1,128]{3,0,2,1:T(8,128)(2,1)S(1)} %get-tuple-element.84), channel_id=1, source_target_pairs={{0,16},{16,32},{32,48},{48,64},{64,80},{80,96},{96,112},{112,128},... | collective-permute-start | bytes 73736 | tf_op jit(solution)/shard_map/ppermute | solution.py:17
  216.0 12.7 %collective-permute-start.21 = (bf16[1,3,1,128]{3,2,1,0:T(2,128)(2,1)S(1)}, bf16[1,3,1,128]{3,2,1,0:T(2,128)(2,1)S(1)}, u32[]{:S(2)}, u32[]{:S(2)}) collective-permute-start(bf16[1,3,1,128]{3,2,1,0:T(2,128)(2,1)S(1)} %get-tuple-element.93), channel_id=1, source_target_pairs={{16,0},{32,16},{48,32},{64,48},{80,64},{96,80},{112,96},{128,112},... | collective-permute-start | bytes 2312 | tf_op jit(solution)/shard_map/ppermute | solution.py:19
  217.9 10.8 %collective-permute-start.20 = (bf16[1,3,1,128]{3,2,1,0:T(2,128)(2,1)S(1)}, bf16[1,3,1,128]{3,2,1,0:T(2,128)(2,1)S(1)}, u32[]{:S(2)}, u32[]{:S(2)}) collective-permute-start(bf16[1,3,1,128]{3,2,1,0:T(2,128)(2,1)S(1)} %get-tuple-element.92), channel_id=1, source_target_pairs={{0,16},{16,32},{32,48},{48,64},{64,80},{80,96},{96,112},{112,128},... | collective-permute-start | bytes 2312 | tf_op jit(solution)/shard_map/ppermute | solution.py:17
  222.8 11.4 %collective-permute-start.7 = (bf16[32,1,4,128]{3,0,2,1:T(8,128)(2,1)S(1)}, bf16[32,1,4,128]{3,0,2,1:T(8,128)(2,1)S(1)}, u32[]{:S(2)}, u32[]{:S(2)}) collective-permute-start(bf16[32,1,4,128]{3,0,2,1:T(8,128)(2,1)S(1)} %get-tuple-element.69), channel_id=1, source_target_pairs={{1,0},{2,1},{3,2},{4,3},{5,4},{6,5},{7,6},{8,7},{9,8},{10,9},{11,1... | collective-permute-start | bytes 98312 | tf_op jit(solution)/shard_map/ppermute | solution.py:19
  224.1 10.2 %collective-permute-start.6 = (bf16[32,1,4,128]{3,0,2,1:T(8,128)(2,1)S(1)}, bf16[32,1,4,128]{3,0,2,1:T(8,128)(2,1)S(1)}, u32[]{:S(2)}, u32[]{:S(2)}) collective-permute-start(bf16[32,1,4,128]{3,0,2,1:T(8,128)(2,1)S(1)} %get-tuple-element.68), channel_id=1, source_target_pairs={{0,1},{1,2},{2,3},{3,4},{4,5},{5,6},{6,7},{7,8},{8,9},{9,10},{10,1... | collective-permute-start | bytes 98312 | tf_op jit(solution)/shard_map/ppermute | solution.py:17
  228.7 15.5 %collective-permute-start.23 = (bf16[1,1,4,128]{3,2,1,0:T(4,128)(2,1)S(1)}, bf16[1,1,4,128]{3,2,1,0:T(4,128)(2,1)S(1)}, u32[]{:S(2)}, u32[]{:S(2)}) collective-permute-start(bf16[1,1,4,128]{3,2,1,0:T(4,128)(2,1)S(1)} %get-tuple-element.87), channel_id=1, source_target_pairs={{1,0},{2,1},{3,2},{4,3},{5,4},{6,5},{7,6},{8,7},{9,8},{10,9},{11,1... | collective-permute-start | bytes 3080 | tf_op jit(solution)/shard_map/ppermute | solution.py:19
  230.0 14.3 %collective-permute-start.22 = (bf16[1,1,4,128]{3,2,1,0:T(4,128)(2,1)S(1)}, bf16[1,1,4,128]{3,2,1,0:T(4,128)(2,1)S(1)}, u32[]{:S(2)}, u32[]{:S(2)}) collective-permute-start(bf16[1,1,4,128]{3,2,1,0:T(4,128)(2,1)S(1)} %get-tuple-element.86), channel_id=1, source_target_pairs={{0,1},{1,2},{2,3},{3,4},{4,5},{5,6},{6,7},{7,8},{8,9},{9,10},{10,1... | collective-permute-start | bytes 3080 | tf_op jit(solution)/shard_map/ppermute | solution.py:17
  238.7 5.8 collective-permute-start.9
  240.6 4.6 collective-permute-start.8
  245.2 6.1 collective-permute-start.11
  246.5 5.4 collective-permute-start.10
  256.3 7.9 collective-permute-start.13
  258.2 6.0 collective-permute-start.12
  264.2 15.4 %collective-permute-start.15 = (bf16[32,1,4,128]{3,0,2,1:T(8,128)(2,1)S(1)}, bf16[32,1,4,128]{3,0,2,1:T(8,128)(2,1)S(1)}, u32[]{:S(2)}, u32[]{:S(2)}) collective-permute-start(bf16[32,1,4,128]{3,0,2,1:T(8,128)(2,1)S(1)} %get-tuple-element.65), channel_id=1, source_target_pairs={{1,0},{2,1},{3,2},{4,3},{5,4},{6,5},{7,6},{8,7},{9,8},{10,9},{11,1... | collective-permute-start | bytes 98312 | tf_op jit(solution)/shard_map/ppermute | solution.py:19
  265.5 14.1 %collective-permute-start.14 = (bf16[32,1,4,128]{3,0,2,1:T(8,128)(2,1)S(1)}, bf16[32,1,4,128]{3,0,2,1:T(8,128)(2,1)S(1)}, u32[]{:S(2)}, u32[]{:S(2)}) collective-permute-start(bf16[32,1,4,128]{3,0,2,1:T(8,128)(2,1)S(1)} %get-tuple-element.64), channel_id=1, source_target_pairs={{0,1},{1,2},{2,3},{3,4},{4,5},{5,6},{6,7},{7,8},{8,9},{9,10},{10,1... | collective-permute-start | bytes 98312 | tf_op jit(solution)/shard_map/ppermute | solution.py:17
  286.2 33.1 %collective-permute-start.17 = (bf16[32,3,1,128]{3,0,2,1:T(8,128)(2,1)}, bf16[32,3,1,128]{3,0,2,1:T(8,128)(2,1)}, u32[]{:S(2)}, u32[]{:S(2)}) collective-permute-start(bf16[32,3,1,128]{3,0,2,1:T(8,128)(2,1)} %get-tuple-element.79), channel_id=1, source_target_pairs={{16,0},{32,16},{48,32},{64,48},{80,64},{96,80},{112,96},{128,112},... | collective-permute-start | bytes 73736 | tf_op jit(solution)/shard_map/ppermute | solution.py:19
  288.2 31.2 %collective-permute-start.16 = (bf16[32,3,1,128]{3,0,2,1:T(8,128)(2,1)}, bf16[32,3,1,128]{3,0,2,1:T(8,128)(2,1)}, u32[]{:S(2)}, u32[]{:S(2)}) collective-permute-start(bf16[32,3,1,128]{3,0,2,1:T(8,128)(2,1)} %get-tuple-element.78), channel_id=1, source_target_pairs={{0,16},{16,32},{32,48},{48,64},{64,80},{80,96},{96,112},{112,128},... | collective-permute-start | bytes 73736 | tf_op jit(solution)/shard_map/ppermute | solution.py:17
  293.3 17.9 %collective-permute-start.25 = (bf16[32,3,1,128]{3,0,2,1:T(8,128)(2,1)}, bf16[32,3,1,128]{3,0,2,1:T(8,128)(2,1)}, u32[]{:S(2)}, u32[]{:S(2)}) collective-permute-start(bf16[32,3,1,128]{3,0,2,1:T(8,128)(2,1)} %get-tuple-element.77), channel_id=1, source_target_pairs={{16,0},{32,16},{48,32},{64,48},{80,64},{96,80},{112,96},{128,112},... | collective-permute-start | bytes 73736 | tf_op jit(solution)/shard_map/ppermute | solution.py:19
  295.2 16.0 %collective-permute-start.24 = (bf16[32,3,1,128]{3,0,2,1:T(8,128)(2,1)}, bf16[32,3,1,128]{3,0,2,1:T(8,128)(2,1)}, u32[]{:S(2)}, u32[]{:S(2)}) collective-permute-start(bf16[32,3,1,128]{3,0,2,1:T(8,128)(2,1)} %get-tuple-element.76), channel_id=1, source_target_pairs={{0,16},{16,32},{32,48},{48,64},{64,80},{80,96},{96,112},{112,128},... | collective-permute-start | bytes 73736 | tf_op jit(solution)/shard_map/ppermute | solution.py:17
  312.0 16.1 %collective-permute-start.27 = (bf16[32,1,4,128]{3,0,2,1:T(8,128)(2,1)S(1)}, bf16[32,1,4,128]{3,0,2,1:T(8,128)(2,1)S(1)}, u32[]{:S(2)}, u32[]{:S(2)}) collective-permute-start(bf16[32,1,4,128]{3,0,2,1:T(8,128)(2,1)S(1)} %get-tuple-element.59), channel_id=1, source_target_pairs={{1,0},{2,1},{3,2},{4,3},{5,4},{6,5},{7,6},{8,7},{9,8},{10,9},{11,1... | collective-permute-start | bytes 98312 | tf_op jit(solution)/shard_map/ppermute | solution.py:19
  313.3 14.8 %collective-permute-start.26 = (bf16[32,1,4,128]{3,0,2,1:T(8,128)(2,1)S(1)}, bf16[32,1,4,128]{3,0,2,1:T(8,128)(2,1)S(1)}, u32[]{:S(2)}, u32[]{:S(2)}) collective-permute-start(bf16[32,1,4,128]{3,0,2,1:T(8,128)(2,1)S(1)} %get-tuple-element.58), channel_id=1, source_target_pairs={{0,1},{1,2},{2,3},{3,4},{4,5},{5,6},{6,7},{7,8},{8,9},{9,10},{10,1... | collective-permute-start | bytes 98312 | tf_op jit(solution)/shard_map/ppermute | solution.py:17
  320.2 13.0 %collective-permute-start.19 = (bf16[32,1,4,128]{3,0,2,1:T(8,128)(2,1)S(1)}, bf16[32,1,4,128]{3,0,2,1:T(8,128)(2,1)S(1)}, u32[]{:S(2)}, u32[]{:S(2)}) collective-permute-start(bf16[32,1,4,128]{3,0,2,1:T(8,128)(2,1)S(1)} %get-tuple-element.63), channel_id=1, source_target_pairs={{1,0},{2,1},{3,2},{4,3},{5,4},{6,5},{7,6},{8,7},{9,8},{10,9},{11,1... | collective-permute-start | bytes 98312 | tf_op jit(solution)/shard_map/ppermute | solution.py:19
  321.5 11.8 %collective-permute-start.18 = (bf16[32,1,4,128]{3,0,2,1:T(8,128)(2,1)S(1)}, bf16[32,1,4,128]{3,0,2,1:T(8,128)(2,1)S(1)}, u32[]{:S(2)}, u32[]{:S(2)}) collective-permute-start(bf16[32,1,4,128]{3,0,2,1:T(8,128)(2,1)S(1)} %get-tuple-element.62), channel_id=1, source_target_pairs={{0,1},{1,2},{2,3},{3,4},{4,5},{5,6},{6,7},{7,8},{8,9},{9,10},{10,1... | collective-permute-start | bytes 98312 | tf_op jit(solution)/shard_map/ppermute | solution.py:17
  338.8 16.0 %collective-permute-start.29 = (bf16[32,3,1,128]{3,0,2,1:T(8,128)(2,1)}, bf16[32,3,1,128]{3,0,2,1:T(8,128)(2,1)S(1)}, u32[]{:S(2)}, u32[]{:S(2)}) collective-permute-start(bf16[32,3,1,128]{3,0,2,1:T(8,128)(2,1)} %get-tuple-element.75), channel_id=1, source_target_pairs={{16,0},{32,16},{48,32},{64,48},{80,64},{96,80},{112,96},{128,112},... | collective-permute-start | bytes 73736 | tf_op jit(solution)/shard_map/ppermute | solution.py:19
  340.7 14.1 %collective-permute-start.28 = (bf16[32,3,1,128]{3,0,2,1:T(8,128)(2,1)}, bf16[32,3,1,128]{3,0,2,1:T(8,128)(2,1)S(1)}, u32[]{:S(2)}, u32[]{:S(2)}) collective-permute-start(bf16[32,3,1,128]{3,0,2,1:T(8,128)(2,1)} %get-tuple-element.74), channel_id=1, source_target_pairs={{0,16},{16,32},{32,48},{48,64},{64,80},{80,96},{96,112},{112,128},... | collective-permute-start | bytes 73736 | tf_op jit(solution)/shard_map/ppermute | solution.py:17
  354.8 11.4 %collective-permute-start.31 = (bf16[32,1,4,128]{3,0,2,1:T(8,128)(2,1)S(1)}, bf16[32,1,4,128]{3,0,2,1:T(8,128)(2,1)S(1)}, u32[]{:S(2)}, u32[]{:S(2)}) collective-permute-start(bf16[32,1,4,128]{3,0,2,1:T(8,128)(2,1)S(1)} %get-tuple-element.57), channel_id=1, source_target_pairs={{1,0},{2,1},{3,2},{4,3},{5,4},{6,5},{7,6},{8,7},{9,8},{10,9},{11,1... | collective-permute-start | bytes 98312 | tf_op jit(solution)/shard_map/ppermute | solution.py:19
  356.1 10.1 %collective-permute-start.30 = (bf16[32,1,4,128]{3,0,2,1:T(8,128)(2,1)S(1)}, bf16[32,1,4,128]{3,0,2,1:T(8,128)(2,1)S(1)}, u32[]{:S(2)}, u32[]{:S(2)}) collective-permute-start(bf16[32,1,4,128]{3,0,2,1:T(8,128)(2,1)S(1)} %get-tuple-element.56), channel_id=1, source_target_pairs={{0,1},{1,2},{2,3},{3,4},{4,5},{5,6},{6,7},{7,8},{8,9},{9,10},{10,1... | collective-permute-start | bytes 98312 | tf_op jit(solution)/shard_map/ppermute | solution.py:17
  370.3 11.8 %collective-permute-start.33 = (bf16[32,3,1,128]{3,0,2,1:T(8,128)(2,1)S(1)}, bf16[32,3,1,128]{3,0,2,1:T(8,128)(2,1)S(1)}, u32[]{:S(2)}, u32[]{:S(2)}) collective-permute-start(bf16[32,3,1,128]{3,0,2,1:T(8,128)(2,1)S(1)} %get-tuple-element.73), channel_id=1, source_target_pairs={{16,0},{32,16},{48,32},{64,48},{80,64},{96,80},{112,96},{128,112},... | collective-permute-start | bytes 73736 | tf_op jit(solution)/shard_map/ppermute | solution.py:19
  372.2 9.9 %collective-permute-start.32 = (bf16[32,3,1,128]{3,0,2,1:T(8,128)(2,1)S(1)}, bf16[32,3,1,128]{3,0,2,1:T(8,128)(2,1)S(1)}, u32[]{:S(2)}, u32[]{:S(2)}) collective-permute-start(bf16[32,3,1,128]{3,0,2,1:T(8,128)(2,1)S(1)} %get-tuple-element.72), channel_id=1, source_target_pairs={{0,16},{16,32},{32,48},{48,64},{64,80},{80,96},{96,112},{112,128},... | collective-permute-start | bytes 73736 | tf_op jit(solution)/shard_map/ppermute | solution.py:17
  382.2 8.6 collective-permute-start.35
  383.5 7.4 collective-permute-start.34
  394.7 6.0 collective-permute-start.37
  396.6 4.6 collective-permute-start.36
  401.2 18.7 %collective-permute-start.39 = (bf16[32,1,4,128]{3,0,2,1:T(8,128)(2,1)S(1)}, bf16[32,1,4,128]{3,0,2,1:T(8,128)(2,1)S(1)}, u32[]{:S(2)}, u32[]{:S(2)}) collective-permute-start(bf16[32,1,4,128]{3,0,2,1:T(8,128)(2,1)S(1)} %get-tuple-element.53), channel_id=1, source_target_pairs={{1,0},{2,1},{3,2},{4,3},{5,4},{6,5},{7,6},{8,7},{9,8},{10,9},{11,1... | collective-permute-start | bytes 98312 | tf_op jit(solution)/shard_map/ppermute | solution.py:19
  402.5 17.4 %collective-permute-start.38 = (bf16[32,1,4,128]{3,0,2,1:T(8,128)(2,1)S(1)}, bf16[32,1,4,128]{3,0,2,1:T(8,128)(2,1)S(1)}, u32[]{:S(2)}, u32[]{:S(2)}) collective-permute-start(bf16[32,1,4,128]{3,0,2,1:T(8,128)(2,1)S(1)} %get-tuple-element.52), channel_id=1, source_target_pairs={{0,1},{1,2},{2,3},{3,4},{4,5},{5,6},{6,7},{7,8},{8,9},{9,10},{10,1... | collective-permute-start | bytes 98312 | tf_op jit(solution)/shard_map/ppermute | solution.py:17
  (30 other events, 235.9 us)
Sparse Core Ops, SparseCore 0:
  390.9 480.3 all-reduce.14
where the time goes:
time: 891 us; the launch traced here: 881 us
  waiting for transfers between devices  322 us (36%)
  blocking collectives  294 us (33%)
  starting transfers between devices  131 us (15%)
  matrix products  53.1 us (6%)
  local copies, waits for them, and re-layouts  46.6 us (5%)
  between operations  18 us (2%)
  other arithmetic  16.4 us (2%)
    psum x1, waiting for transfers between devices, shards(): summed = lax.psum((grad_in, grad_mid, grad_out), ('sector', 'slab'))  319 us
    psum x1, blocking collectives, shards(): summed = lax.psum((grad_in, grad_mid, grad_out), ('sector', 'slab'))  120 us
    ppermute x20, starting transfers between devices, extended(): lax.ppermute(tail, axis, [(i, (i + 1) % count) for i in range(ends)])  94.6 us
    unnamed x2, blocking collectives  76.6 us
    all_gather x1, blocking collectives, shards(): lax.all_gather(backward, 'sector', axis=0, tiled=True)  46.2 us
    all_gather x1, blocking collectives, shards(): lax.all_gather(image.astype(jnp.bfloat16), 'sector', axis=1, tiled=True)  37.7 us
    ppermute x20, starting transfers between devices, extended(): lax.ppermute(head, axis, [((i + 1) % count, i) for i in range(ends)])  36.7 us
    transpose x3, matrix products, weight_grad(): return jnp.transpose(result, (1, 0, 2, 3, 4))  21.5 us
  transfers between devices with their start and end apart: 41, of which 6 were waited for; matrix products, arithmetic and copies ran while one was open for 9% of the time, Pallas kernels for 0%

commit v1 on v0

v1 whole, which is shorter than its diff:
```python
import math

import jax
import jax.numpy as jnp
from jax import lax
from jax.experimental import pallas as pl
from jax.experimental.pallas import tpu as pltpu
from jax.sharding import PartitionSpec as P

LANES = 128
VMEM_BYTES = 56 * 1024 * 1024


class Plan:
    def __init__(self, zs, xs, channels, layers):
        self.zs, self.xs, self.c, self.layers = zs, xs, channels, layers
        self.halo_u = [2 * layers - l + 1 for l in range(1, layers + 2)]
        self.halo_c = [l for l in range(1, layers + 1)]
        self.halo_in = 2 * layers
        self.halo_last = layers + 1
        self.lead_in = -(self.halo_in - 1) % 8
        self.lead_last = -(self.halo_last - 1) % 8
        self.rows_in = -(-(zs + 2 * self.halo_in + self.lead_in) // 8) * 8
        self.rows_last = -(-(zs + 2 * self.halo_last + self.lead_last) // 8) * 8

    def z(self, halo):
        return self.zs + 2 * halo

    def x(self, halo):
        return self.xs + 2 * halo

    def starts(self, planes):
        count = -(-planes // 6)
        size = -(-planes // count)
        return size, [min(k * size, planes - size) for k in range(count)]


def round_up(value, step):
    return -(-value // step) * step


def shifts(rows):
    lane = lax.broadcasted_iota(jnp.int32, rows.shape, 1)
    low = jnp.where(lane == 0, 0.0, pltpu.roll(rows, 1, 1))
    high = jnp.where(lane == LANES - 1, 0.0, pltpu.roll(rows, LANES - 1, 1))
    return low, rows, high


def prepare_kernel(plan, base_in, base_last, base_out, base_back, *refs):
    mids = 2 * (plan.layers - 1)
    bases, outs = refs[:mids], refs[mids:]
    w_first, w_top, w_out, w_back = outs[:4]
    toeplitz = outs[4:]
    c = plan.c
    for base, out, step, planes in (
        (base_in, w_first, 1, plan.z(plan.halo_u[1])),
        (base_last, w_top, 1, plan.z(plan.halo_c[-1])),
    ):
        rows = base[...].astype(jnp.float32)
        for k in range(planes):
            moved = rows if k == 0 else pltpu.roll(rows, k * step, 1)
            out[k * c : (k + 1) * c, :] = moved.astype(jnp.bfloat16)
    for base, out in ((base_out, w_out), (base_back, w_back)):
        rows = base[...].astype(jnp.float32)
        line = lax.broadcasted_iota(jnp.int32, rows.shape, 0)
        total = jnp.where(line == 0, rows, 0.0)
        for k in range(1, plan.zs):
            total = total + jnp.where(line == k, pltpu.roll(rows, k * c, 1), 0.0)
        out[...] = total.astype(jnp.bfloat16)
    for base, out in zip(bases, toeplitz):
        rows = base[...].astype(jnp.float32)
        for k in range(out.shape[0] // c):
            moved = rows if k == 0 else pltpu.roll(rows, k * c, 1)
            out[k * c : (k + 1) * c, :] = moved.astype(jnp.bfloat16)


def inside(first, count, c, bound):
    line = lax.broadcasted_iota(jnp.int32, (count * c, 1), 0)
    plane = first + lax.shift_right_arithmetic(line, int(math.log2(c)))
    return jnp.logical_and(plane >= 0, plane < bound)


def network_kernel(plan, grid, pos, u_first, c_last, em_own, cot_own, w_first, w_top, w_out, w_back, *refs):
    layers, c, zs, xs = plan.layers, plan.c, plan.zs, plan.xs
    mids = layers - 1
    w_fwd, w_bwd = refs[:mids], refs[mids : 2 * mids]
    new_image, em_grad, grads = refs[2 * mids : 2 * mids + 3]
    scratch = refs[2 * mids + 3 :]
    first_sh, last_sh = scratch[:2]
    u_sh = scratch[2 : 2 + layers]
    pre = scratch[2 + layers : 2 + 2 * layers]
    c_sh = scratch[2 + 2 * layers : 2 + 3 * layers]
    z_first, x_first = pos[0], pos[1]
    f32, bf16 = jnp.float32, jnp.bfloat16

    for source, target, count in (
        (u_first, first_sh, plan.x(plan.halo_in)),
        (c_last, last_sh, plan.x(plan.halo_last)),
    ):
        for k in range(count):
            span = slice(k * LANES, (k + 1) * LANES)
            for dy, rows in enumerate(shifts(source[:, span].astype(f32))):
                target[dy, :, span] = rows

    def store_shifted(target, value, rows, lane, x_at, keep):
        for half in range(2):
            part = value[:, half * LANES : (half + 1) * LANES]
            good = jnp.logical_and(x_at + half >= 0, x_at + half < grid[1])
            part = jnp.where(jnp.logical_and(keep, good), part, 0.0)
            for dy, moved in enumerate(shifts(part)):
                target[dy, rows, pl.ds(lane + half * LANES, LANES)] = moved.astype(bf16)

    def one_channel(source, weight, lane):
        pieces = [
            source[dy, :, pl.ds(lane + dx * LANES, 2 * LANES)] for dx in range(3) for dy in range(3)
        ]
        stacked = jnp.concatenate(pieces, axis=0).astype(bf16)
        return jnp.dot(weight[:, : stacked.shape[0]], stacked, preferred_element_type=f32)

    def many_channels(source, weight, first_plane, planes, lane):
        rows = slice(first_plane * c, (first_plane + planes + 2) * c)
        pieces = [
            source[dy, rows, pl.ds(lane + dx * LANES, 2 * LANES)]
            for dx in range(3)
            for dy in range(3)
        ]
        stacked = jnp.concatenate(pieces, axis=0)
        return jnp.dot(weight[:, : stacked.shape[0]], stacked, preferred_element_type=f32)

    def forward_tail(value, layer, first_plane, planes, pair, lane):
        halo = plan.halo_u[layer]
        rows = slice(first_plane * c, (first_plane + planes) * c)
        pre[layer - 1][rows, pl.ds(lane, 2 * LANES)] = value
        act = value * jax.nn.sigmoid(value)
        keep = inside(z_first - halo + first_plane, planes, c, grid[0])
        store_shifted(u_sh[layer - 1], act, rows, lane, x_first - halo + 2 * pair, keep)

    def backward_tail(value, layer, first_plane, planes, pair, lane):
        halo, halo_pre = plan.halo_c[layer - 1], plan.halo_u[layer]
        rows = slice(first_plane * c, (first_plane + planes) * c)
        from_plane = first_plane + halo_pre - halo
        preact = pre[layer - 1][
            from_plane * c : (from_plane + planes) * c,
            pl.ds(lane + (halo_pre - halo) * LANES, 2 * LANES),
        ]
        sigma = jax.nn.sigmoid(preact)
        slope = sigma * (1.0 + preact * (1.0 - sigma))
        keep = inside(z_first - halo + first_plane, planes, c, grid[0])
        store_shifted(
            c_sh[layer - 1], slope * value, rows, lane, x_first - halo + 2 * pair, keep
        )

    def over_pairs(count, body):
        def step(pair, carry):
            body(pair, pl.multiple_of(pair * 2 * LANES, 2 * LANES))
            return carry

        lax.fori_loop(0, count, step, 0)

    halo = plan.halo_u[1]

    def first_layer(pair, lane):
        value = one_channel(first_sh, w_first, lane)
        forward_tail(value, 1, 0, plan.z(halo), pair, lane)

    over_pairs(plan.x(halo) // 2, first_layer)
    for layer in range(2, layers + 1):
        halo = plan.halo_u[layer]
        size, starts = plan.starts(plan.z(halo))
        for start in starts:

            def middle(pair, lane, layer=layer, size=size, start=start):
                value = many_channels(u_sh[layer - 2], w_fwd[layer - 2], start, size, lane)
                forward_tail(value, layer, start, size, pair, lane)

            over_pairs(plan.x(halo) // 2, middle)

    def own_taps(source, halo):
        rows = slice((halo - 1) * c, (halo + zs + 1) * c)
        pieces = [
            source[dy, rows, (halo - 1 + dx) * LANES : (halo - 1 + dx + xs) * LANES]
            for dx in range(3)
            for dy in range(3)
        ]
        return jnp.concatenate(pieces, axis=0)

    top = plan.halo_u[layers]
    taps = own_taps(u_sh[layers - 1], top)
    last = jnp.dot(w_out[:, : taps.shape[0]], taps, preferred_element_type=f32)
    new_image[...] = em_own[...] + last[:zs, :]

    halo = plan.halo_c[-1]

    def top_layer(pair, lane):
        value = one_channel(last_sh, w_top, lane)
        backward_tail(value, layers, 0, plan.z(halo), pair, lane)

    over_pairs(plan.x(halo) // 2, top_layer)
    for layer in range(layers - 1, 0, -1):
        halo = plan.halo_c[layer - 1]
        size, starts = plan.starts(plan.z(halo))
        for start in starts:

            def middle_back(pair, lane, layer=layer, size=size, start=start):
                value = many_channels(c_sh[layer], w_bwd[layer - 1], start, size, lane)
                backward_tail(value, layer, start, size, pair, lane)

            over_pairs(plan.x(halo) // 2, middle_back)
    taps = own_taps(c_sh[0], plan.halo_c[0])
    down = jnp.dot(w_back[:, : taps.shape[0]], taps, preferred_element_type=f32)
    em_grad[...] = cot_own[...] + down[:zs, :]

    def own_rows(source, halo, plane):
        return source[1, (halo + plane) * c : (halo + plane + 1) * c, halo * LANES : (halo + xs) * LANES]

    def against(cells, taps):
        return lax.dot_general(cells, taps, (((1,), (1,)), ((), ())), preferred_element_type=f32)

    block = round_up(27 * c, LANES)
    grads[...] = jnp.zeros(grads.shape, f32)
    for layer in range(2, layers + 1):
        source, halo = u_sh[layer - 2], plan.halo_u[layer - 1]
        total = None
        for plane in range(zs):
            rows = slice((halo - 1 + plane) * c, (halo + 2 + plane) * c)
            pieces = [
                source[dy, rows, (halo - 1 + dx) * LANES : (halo - 1 + dx + xs) * LANES]
                for dx in range(3)
                for dy in range(3)
            ]
            cells = own_rows(c_sh[layer - 1], plan.halo_c[layer - 1], plane)
            term = against(cells, jnp.concatenate(pieces, axis=0))
            total = term if total is None else total + term
        grads[:, (layer - 2) * block : (layer - 2) * block + 27 * c] = total

    def thin(source, halo, lead, cells_of, at):
        row = lead + halo - 1
        pieces = [
            source[dy, row : row + 8, (halo - 1 + dx) * LANES : (halo - 1 + dx + xs) * LANES]
            for dx in range(3)
            for dy in range(3)
        ]
        pieces.append(jnp.zeros((LANES - 72, xs * LANES), f32))
        taps = jnp.concatenate(pieces, axis=0).astype(bf16)
        total = None
        for plane in range(zs):
            term = against(cells_of(plane), taps)
            if plane:
                term = pltpu.roll(term, LANES - plane, 1)
            total = term if total is None else total + term
        grads[:, at : at + LANES] = total

    thin(
        first_sh,
        plan.halo_in,
        plan.lead_in,
        lambda plane: own_rows(c_sh[0], plan.halo_c[0], plane),
        mids * block,
    )
    thin(
        last_sh,
        plan.halo_last,
        plan.lead_last,
        lambda plane: own_rows(u_sh[layers - 1], top, plane),
        mids * block + LANES,
    )


def toeplitz_bases(plan, w_in, w_mid, w_out):
    c, layers = plan.c, plan.layers
    mids = w_mid.shape[0]

    def spread(weights, planes, lead=0):
        moved = jnp.transpose(weights, (0, 2, 3, 1, 4))
        moved = jnp.pad(moved, ((0, 0), (0, 0), (0, 0), (lead, planes - 3 - lead), (0, 0)))
        flat = moved.reshape(weights.shape[0], 9 * planes * weights.shape[4])
        return jnp.pad(flat, ((0, 0), (0, round_up(flat.shape[1], LANES) - flat.shape[1])))

    first = jnp.transpose(w_in, (0, 2, 3, 4, 1))
    base_in = spread(first, plan.rows_in, plan.lead_in)
    last_back = jnp.transpose(jnp.flip(w_out, (2, 3, 4)), (1, 2, 3, 4, 0))
    base_last = spread(last_back, plan.rows_last, plan.lead_last)
    out_fwd = jnp.transpose(w_out, (0, 2, 3, 4, 1))
    in_back = jnp.transpose(jnp.flip(w_in, (2, 3, 4)), (1, 2, 3, 4, 0))
    base_out = jnp.broadcast_to(spread(out_fwd, plan.zs + 2), (8, round_up(9 * (plan.zs + 2) * c, LANES)))
    base_back = jnp.broadcast_to(spread(in_back, plan.zs + 2), base_out.shape)
    bases, sizes = [], []
    forward = jnp.transpose(w_mid, (0, 1, 3, 4, 5, 2))
    backward = jnp.transpose(jnp.flip(w_mid, (3, 4, 5)), (0, 2, 3, 4, 5, 1))
    for k in range(mids):
        size, _ = plan.starts(plan.z(plan.halo_u[k + 2]))
        bases.append(spread(forward[k], size + 2))
        sizes.append(size)
    for k in range(mids):
        size, _ = plan.starts(plan.z(plan.halo_c[k]))
        bases.append(spread(backward[k], size + 2))
        sizes.append(size)
    return (base_in, base_last, base_out, base_back, *bases), sizes


def prepared_weights(plan, w_in, w_mid, w_out):
    bases, sizes = toeplitz_bases(plan, w_in, w_mid, w_out)
    c, bf16 = plan.c, jnp.bfloat16
    shapes = [
        (plan.z(plan.halo_u[1]) * c, bases[0].shape[1]),
        (plan.z(plan.halo_c[-1]) * c, bases[1].shape[1]),
        bases[2].shape,
        bases[3].shape,
    ]
    shapes += [(size * c, base.shape[1]) for size, base in zip(sizes, bases[4:])]
    vmem = pl.BlockSpec(memory_space=pltpu.VMEM)
    return pl.pallas_call(
        lambda *refs: prepare_kernel(plan, *refs),
        out_shape=[jax.ShapeDtypeStruct(shape, bf16) for shape in shapes],
        in_specs=[vmem] * len(bases),
        out_specs=[vmem] * len(shapes),
        compiler_params=pltpu.CompilerParams(vmem_limit_bytes=VMEM_BYTES),
        name="prepare_weights",
    )(*bases)


def network(plan, grid, z_first, x_first, u_first, c_last, em_own, cot_own, weights):
    layers, c = plan.layers, plan.c
    f32, bf16 = jnp.float32, jnp.bfloat16
    block = round_up(27 * c, LANES)
    width = (layers - 1) * block + 2 * LANES
    own = jax.ShapeDtypeStruct((plan.zs, plan.xs * LANES), f32)
    scratch = [
        pltpu.VMEM((3, plan.rows_in, plan.x(plan.halo_in) * LANES), f32),
        pltpu.VMEM((3, plan.rows_last, plan.x(plan.halo_last) * LANES), f32),
    ]

    def region(halo, lead=()):
        return (*lead, plan.z(halo) * c, plan.x(halo) * LANES)

    scratch += [pltpu.VMEM(region(plan.halo_u[l], (3,)), bf16) for l in range(1, layers + 1)]
    scratch += [pltpu.VMEM(region(plan.halo_u[l]), f32) for l in range(1, layers + 1)]
    scratch += [pltpu.VMEM(region(plan.halo_c[l - 1], (3,)), bf16) for l in range(1, layers + 1)]
    vmem = pl.BlockSpec(memory_space=pltpu.VMEM)
    position = jnp.stack([z_first, x_first]).astype(jnp.int32)
    operands = (position, u_first, c_last, em_own, cot_own, *weights)
    return pl.pallas_call(
        lambda *refs: network_kernel(plan, grid, *refs),
        out_shape=[own, own, jax.ShapeDtypeStruct((c, width), f32)],
        in_specs=[pl.BlockSpec(memory_space=pltpu.SMEM)] + [vmem] * (len(operands) - 1),
        out_specs=[vmem] * 3,
        scratch_shapes=scratch,
        compiler_params=pltpu.CompilerParams(vmem_limit_bytes=VMEM_BYTES),
        name="network",
    )(*operands)


def unpack_grads(plan, packed):
    c, mids = plan.c, plan.layers - 1
    block = round_up(27 * c, LANES)
    mid = packed[:, : mids * block].reshape(c, mids, block)[:, :, : 27 * c]
    mid = mid.reshape(c, mids, 3, 3, 3, c)
    mid = jnp.transpose(mid, (1, 0, 5, 4, 2, 3))
    thin = packed[:, mids * block :].reshape(c, 2, LANES)[:, :, :72].reshape(c, 2, 3, 3, 8)[..., :3]
    thin = jnp.transpose(thin, (1, 0, 4, 2, 3))
    grad_in = thin[0][:, None]
    grad_out = jnp.flip(thin[1], (1, 2, 3))[None]
    return grad_in, mid, grad_out


def shards(
    image,
    sensitivity,
    tile_values,
    tile_rows,
    tile_cols,
    tile_count,
    measured,
    background,
    w_in,
    w_mid,
    w_out,
    cotangent,
):
    f32, bf16 = jnp.float32, jnp.bfloat16
    highest = lax.Precision.HIGHEST
    sectors, slabs = lax.axis_size("sector"), lax.axis_size("slab")
    sector, slab = lax.axis_index("sector"), lax.axis_index("slab")
    zs, xs, ys = image.shape
    block_len = xs * ys
    line_blocks, row_len = measured.shape[1:]
    slots = tile_rows.shape[1]
    plan = Plan(zs, xs, w_in.shape[0], w_mid.shape[0] + 1)
    grid = (zs * slabs, xs * sectors)

    weights = prepared_weights(plan, w_in, w_mid, w_out)

    cols_row = jnp.pad(tile_cols.astype(f32), ((0, 0), (0, block_len - slots))).reshape(1, xs, ys)
    sent = jnp.concatenate([image, sensitivity, cotangent, cols_row], axis=0)
    got = lax.all_gather(sent, "sector", axis=1, tiled=True)
    image_slab, sens_slab, cot_slab = got[:zs], got[zs : 2 * zs], got[2 * zs : 3 * zs]
    every_cols = got[3 * zs].reshape(sectors, block_len)[:, :slots].reshape(-1)

    values = tile_values[0]
    weight = (jnp.arange(slots) < tile_count[0, 0]).astype(f32) / block_len
    blocks = image_slab.astype(bf16).reshape(zs * sectors, block_len)
    forward = jnp.einsum("krv,kv->kr", values, blocks[tile_cols[0]], preferred_element_type=f32)
    forward = forward * weight[:, None]
    lined = jnp.concatenate([forward, tile_rows[0].astype(f32)[:, None]], axis=1)
    lined = jnp.pad(lined, ((0, 0), (0, LANES - row_len - 1)))
    every = lax.all_gather(lined, "slab", axis=0, tiled=True)
    every_rows = every[:, row_len]
    placing = (every_rows[None, :] == jnp.arange(line_blocks, dtype=f32)[:, None]).astype(f32)
    projection = jnp.dot(placing, every[:, :row_len], precision=highest)
    ratio = (measured[0] / (projection + background[0])).astype(bf16)

    backward = jnp.einsum("krv,kr->kv", values, ratio[tile_rows[0]], preferred_element_type=f32)
    backward = backward * weight[:, None]
    every_back = lax.all_gather(backward, "sector", axis=0, tiled=True)
    reach = -(-plan.halo_in // xs)
    near = sector - reach + jnp.arange(2 * reach + 1)
    wanted = (jnp.arange(zs)[:, None] * sectors + near[None, :]).astype(f32)
    good = jnp.logical_and(near >= 0, near < sectors)
    wanted = jnp.where(good[None, :], wanted, -1.0).reshape(-1)
    owning = (every_cols[None, :] == wanted[:, None]).astype(f32)
    halo = plan.halo_in
    back = jnp.dot(owning, every_back, precision=highest).reshape(zs, xs * (2 * reach + 1), ys)
    back = back[:, reach * xs - halo : reach * xs + xs + halo]

    def window(field, halo, fill):
        padded = jnp.pad(field, ((0, 0), (halo, halo), (0, 0)), constant_values=fill)
        return lax.dynamic_slice_in_dim(padded, sector * xs, xs + 2 * halo, 1)

    em = window(image_slab, halo, 0.0) * back / window(sens_slab, halo, 1.0)
    em_own = em[:, halo : halo + xs]

    cot_wide = window(cot_slab, plan.halo_last, 0.0).astype(bf16)
    both = jnp.concatenate([em.astype(bf16), cot_wide], axis=1)
    every_plane = lax.all_gather(both, "slab", axis=0, tiled=True)

    def planes(lo, count, halo, lead, rows):
        field = every_plane[:, lo : lo + count]
        padded = jnp.pad(field, ((halo + lead, rows), (0, 0), (0, 0)))
        taken = lax.dynamic_slice_in_dim(padded, slab * zs, rows, 0)
        line = jnp.arange(rows)[:, None, None]
        taken = jnp.where(jnp.logical_and(line >= lead, line < lead + plan.z(halo)), taken, 0)
        return taken.reshape(rows, count * ys)

    wide = plan.x(halo)
    u_first = planes(0, wide, halo, plan.lead_in, plan.rows_in)
    c_last = planes(wide, plan.x(plan.halo_last), plan.halo_last, plan.lead_last, plan.rows_last)
    new_image, em_grad, packed = network(
        plan,
        grid,
        slab * zs,
        sector * xs,
        u_first,
        c_last,
        em_own.reshape(zs, xs * ys),
        cotangent.reshape(zs, xs * ys),
        weights,
    )
    cells = grid[0] * grid[1] * ys
    packed = lax.psum(packed, ("sector", "slab")) * (1.0 / math.sqrt(cells))
    grad_in, grad_mid, grad_out = unpack_grads(plan, packed)
    return (
        new_image.reshape(zs, xs, ys),
        em_grad.reshape(zs, xs, ys),
        grad_in,
        grad_mid,
        grad_out,
    )


def solution(mesh):
    placed = (
        P("slab", "sector", None),
        P("slab", "sector", None),
        P("sector", "slab", None, None),
        P("sector", "slab"),
        P("sector", "slab"),
        P("sector", "slab"),
        P("sector", None, None),
        P("sector", None, None),
        P(),
        P(),
        P(),
        P("slab", "sector", None),
    )
    return jax.shard_map(
        shards,
        mesh=mesh,
        in_specs=placed,
        out_specs=(P("slab", "sector", None), P("slab", "sector", None), P(), P(), P()),
        check_vma=False,
    )
```

time: 891 us -> 663 us (0.74)
  blocking collectives: 294 us -> 109 us
  waiting for transfers between devices: 322 us -> 461 us
  starting transfers between devices: 131 us -> 0.04 us
  matrix products: 53.1 us -> 0.93 us
  Pallas kernels: 0 us -> 46.2 us
  local copies, waits for them, and re-layouts: 46.6 us -> 24 us
  other arithmetic: 16.4 us -> 4.94 us
    psum x1, waiting for transfers between devices: 319 us -> 461 us  [shards(): packed = lax.psum(packed, ('sector', 'slab')) * (1.0 / math.sqrt(cells))]
    ppermute x40 -> x0, starting transfers between devices: 131 us -> none  [the longest x20 94.6 us: extended(): lax.ppermute(tail, axis, [(i, (i + 1) % count) for i in range(ends)])]
    psum x1 -> x0, blocking collectives: 120 us -> none  [shards(): summed = lax.psum((grad_in, grad_mid, grad_out), ('sector', 'slab'))]
    unnamed x2 -> x0, blocking collectives: 76.6 us -> none
    pallas_call x0 -> x2, Pallas kernels: none -> 46.2 us  [the longest x1 42.6 us: network(): pl.pallas_call(lambda *refs: network_kernel(plan, grid, *refs), out_shape...]
    conv_general_dilated x12 -> x0, matrix products: 30.1 us -> none  [the longest x2 16.9 us: weight_grad(): lax.conv_general_dilated(padded[:, None], cotan[:, None], (1, 1, 1), 'VAL...]
    transpose x3 -> x0, matrix products: 21.5 us -> none  [weight_grad(): return jnp.transpose(result, (1, 0, 2, 3, 4))]
    broadcast_in_dim x15 -> x2, local copies, waits for them, and re-layouts: 14.9 us -> 1.21 us  [the longest x1 0.61 us: toeplitz_bases(): base_back = jnp.broadcast_to(spread(in_back, plan.zs + 2), base_out.shape)]
  transfers between devices with their start and end apart: 41 -> 1, of which waited for: 6 -> 1; matrix products, arithmetic and copies ran while one was open for 9% -> 0% of each run, Pallas kernels for 0% -> 0%
where the time goes in v1:
time: 663 us; the launch traced here: 662 us
  waiting for transfers between devices  461 us (70%)
  blocking collectives  109 us (16%)
  Pallas kernels  46.2 us (7%)
  local copies, waits for them, and re-layouts  24 us (4%)
  between operations  15.2 us (2%)
    psum x1, waiting for transfers between devices, shards(): packed = lax.psum(packed, ('sector', 'slab')) * (1.0 / math.sqrt(cells))  461 us
    pallas_call x1, Pallas kernels, network(): pl.pallas_call(lambda *refs: network_kernel(plan, grid, *refs), out_shape...  42.6 us
    all_gather x1, blocking collectives, shards(): got = lax.all_gather(sent, 'sector', axis=1, tiled=True)  39 us
    all_gather x1, blocking collectives, shards(): every_back = lax.all_gather(backward, 'sector', axis=0, tiled=True)  33.4 us
    all_gather x1, blocking collectives, shards(): every = lax.all_gather(lined, 'slab', axis=0, tiled=True)  18.7 us
    all_gather x1, blocking collectives, shards(): every_plane = lax.all_gather(both, 'slab', axis=0, tiled=True)  18.3 us
  transfers between devices with their start and end apart: 1, of which 1 were waited for; matrix products, arithmetic and copies ran while one was open for 0% of the time, Pallas kernels for 0%

profile of v1, /device:TPU:1, one launch (start us, length us, event | category | flops | bytes accessed | tf_op | source)
XLA Modules:
  0.0 661.5 jit_solution(7073115056066787915)
XLA Ops:
  7.3 0.7 convert_element_type.78
  8.0 0.7 fusion.21
  8.6 0.7 bitcast_convert_fusion
  9.3 0.7 fusion.22
  10.0 0.7 copy.92
  10.6 0.7 copy.93
  11.3 0.7 copy.94
  12.0 39.0 %all_gather.12 = f32[10,64,128]{2,0,1:T(8,128)S(1)} all-gather(f32[10,2,128]{2,0,1:T(8,128)S(1)} %pad_maximum_fusion.1), channel_id=1, replica_groups=mesh['sector'=32,'slab'=16] {'sector'}, dimensions={1}, use_global_device_ids=true | all-gather | bytes 337920 | tf_op jit(solution)/shard_map/all_gather | solution.py:395
  52.1 0.6 gather_fusion
  52.7 0.3 fusion.4
  53.1 18.7 %all-gather = f32[16,12,128]{2,1,0:T(8,128)S(1)} all-gather(f32[1,12,128]{2,1,0:T(8,128)S(1)} %fusion.19), channel_id=1, replica_groups=mesh['sector'=32,'slab'=16] {'slab'}, dimensions={0}, use_global_device_ids=true | all-gather | bytes 104448 | tf_op jit(solution)/shard_map/all_gather | solution.py:406
  72.2 0.6 gather_fusion.1
  72.8 0.2 fusion.2
  73.1 33.4 %all-gather.1 = f32[32,12,256]{2,1,0:T(8,128)S(1)} all-gather(f32[1,12,256]{2,1,0:T(8,128)S(1)} %fusion.16), channel_id=1, replica_groups=mesh['sector'=32,'slab'=16] {'sector'}, dimensions={0}, use_global_device_ids=true | all-gather | bytes 405504 | tf_op jit(solution)/shard_map/all_gather | solution.py:414
  106.8 0.3 fusion.9
  107.3 18.3 %all_gather.15 = bf16[48,30,128]{2,1,0:T(8,128)(2,1)S(1)} all-gather(bf16[3,30,128]{2,1,0:T(8,128)(2,1)S(1)} %pad_maximum_fusion), channel_id=1, replica_groups=mesh['sector'=32,'slab'=16] {'slab'}, dimensions={0}, use_global_device_ids=true | all-gather | bytes 391680 | tf_op jit(solution)/shard_map/all_gather | solution.py:434
  125.8 0.7 copy.150
  126.6 0.7 copy.151
  127.3 0.6 copy.154
  128.0 0.2 copy.131
  128.4 0.3 reshape.227
  128.7 0.7 pad.115.refs_7_
  129.7 0.3 reshape.229
  130.1 0.6 pad.119.refs_9_
  130.7 0.2 copy.132
  131.1 0.3 reshape.228
  131.4 0.7 pad.117.refs_8_
  132.4 0.3 reshape.224
  132.8 0.7 pad.110.refs_4_
  133.8 0.3 reshape.225
  134.1 0.7 pad.112.refs_5_
  135.1 1.0 reshape.226.refs_6_
  136.3 0.6 pad.104.refs_1_
  137.0 0.6 pad.102.refs_0_
  138.0 0.6 copy.153
  138.6 0.6 pad_add_fusion.refs_0_
  139.2 0.6 broadcast_in_dim.73.refs_3_
  139.8 0.6 broadcast_in_dim.71.refs_2_
  140.4 3.6 prepare_weights.1
  144.0 42.6 %network.1 = (f32[3,256]{1,0:T(4,128)}, f32[3,256]{1,0:T(4,128)}, f32[32,2944]{1,0:T(8,128)}) custom-call(s32[2]{0:T(128)} %pad_add_fusion.refs_0_, bf16[24,2304]{1,0:T(8,128)(2,1)} %bitcast.107, bf16[24,1536]{1,0:T(8,128)(2,1)} %bitcast.110, f32[3,256]{1,0:T(4,128)} %bitcast.121, f32[3,256]{1,0:T(4,128)} %bitcast.122, ...), custom_call_target="tpu_custom_call" | custom-call | tf_op jit(solution)/shard_map/network/pallas_call | solution.py:342
  186.6 1.3 reshape.230
  187.9 1.3 reshape.231
  189.2 460.7 %all-reduce.28.cloned.1.call-done = f32[32,2944]{1,0:T(8,128)} async-done(((f32[32,2944]{1,0:T(8,128)}), f32[32,2944]{1,0:T(8,128)}) %all-reduce.28.cloned.1.call-update) | async-done | bytes 376848 | tf_op jit(solution)/shard_map/psum | solution.py:459
  649.9 1.0 broadcast_multiply_fusion
  651.1 0.9 reshape.235
  652.0 1.2 copy.114
  653.5 0.6 copy.115
  654.1 0.6 copy.152
  (96 shorter events, 4.4 us)
Async XLA Ops:
  7.2 45.5 %copy-start = (bf16[1,12,104,256]{3,2,1,0:T(8,128)(2,1)S(1)}, bf16[1,12,104,256]{3,2,1,0:T(8,128)(2,1)}, u32[]{:S(2)}) copy-start(bf16[1,12,104,256]{3,2,1,0:T(8,128)(2,1)} %param.14) | copy-start | bytes 1916932
  7.2 64.8 %copy-start.6 = (f32[1,32,104]{2,1,0:T(8,128)S(1)}, f32[1,32,104]{2,1,0:T(8,128)}, u32[]{:S(2)}) copy-start(f32[1,32,104]{2,1,0:T(8,128)} %param.18) | copy-start | bytes 39940
  7.2 64.8 %copy-start.5 = (f32[1,32,104]{2,1,0:T(8,128)S(1)}, f32[1,32,104]{2,1,0:T(8,128)}, u32[]{:S(2)}) copy-start(f32[1,32,104]{2,1,0:T(8,128)} %param.19) | copy-start | bytes 39940
  7.2 642.7 %all-reduce.28.cloned.1.call-start = ((), (), s32[]{:S(2)}) async-start(), calls=%async_computation | async-start | bytes 753664 | tf_op jit(solution)/shard_map/psum | solution.py:459
  107.1 20.8 %copy-start.1 = (bf16[3,32,32,3,3,3]{2,1,5,4,3,0:T(8,128)(2,1)S(1)}, bf16[3,32,32,3,3,3]{2,1,5,4,3,0:T(8,128)(2,1)}, u32[]{:S(2)}) copy-start(bf16[3,32,32,3,3,3]{2,1,5,4,3,0:T(8,128)(2,1)} %param.21) | copy-start | bytes 497668
  133.7 2.4 copy-start.4
  133.8 3.1 copy-start.3
  133.8 4.2 copy-start.7
  650.9 1.1 copy-start.2
  652.0 1.3 slice-start
Sparse Core Ops, SparseCore 0:
  186.8 463.0 all-reduce.27

commit v2 on v1

--- a/solution.py
+++ b/solution.py
@@ -216,22 +216,29 @@
     def against(cells, taps):
         return lax.dot_general(cells, taps, (((1,), (1,)), ((), ())), preferred_element_type=f32)
 
-    block = round_up(27 * c, LANES)
-    grads[...] = jnp.zeros(grads.shape, f32)
+    block = round_up(27 * c, LANES) // LANES
     for layer in range(2, layers + 1):
         source, halo = u_sh[layer - 2], plan.halo_u[layer - 1]
         total = None
         for plane in range(zs):
-            rows = slice((halo - 1 + plane) * c, (halo + 2 + plane) * c)
+            first = halo - 1 + plane
             pieces = [
-                source[dy, rows, (halo - 1 + dx) * LANES : (halo - 1 + dx + xs) * LANES]
+                source[
+                    dy,
+                    (first + dz) * c : (first + dz + 1) * c,
+                    (halo - 1 + dx) * LANES : (halo - 1 + dx + xs) * LANES,
+                ]
+                for dz in range(3)
                 for dx in range(3)
                 for dy in range(3)
             ]
+            pieces.append(jnp.zeros((block * LANES - 27 * c, xs * LANES), bf16))
             cells = own_rows(c_sh[layer - 1], plan.halo_c[layer - 1], plane)
             term = against(cells, jnp.concatenate(pieces, axis=0))
             total = term if total is None else total + term
-        grads[:, (layer - 2) * block : (layer - 2) * block + 27 * c] = total
+        for k in range(block):
+            at = ((layer - 2) * block + k) * c
+            grads[at : at + c, :] = total[:, k * LANES : (k + 1) * LANES]
 
     def thin(source, halo, lead, cells_of, at):
         row = lead + halo - 1
@@ -248,22 +255,25 @@
             if plane:
                 term = pltpu.roll(term, LANES - plane, 1)
             total = term if total is None else total + term
-        grads[:, at : at + LANES] = total
+        grads[at : at + c, :] = total
 
     thin(
         first_sh,
         plan.halo_in,
         plan.lead_in,
         lambda plane: own_rows(c_sh[0], plan.halo_c[0], plane),
-        mids * block,
+        mids * block * c,
     )
     thin(
         last_sh,
         plan.halo_last,
         plan.lead_last,
         lambda plane: own_rows(u_sh[layers - 1], top, plane),
-        mids * block + LANES,
+        (mids * block + 1) * c,
     )
+    used = (mids * block + 2) * c
+    if used < grads.shape[0]:
+        grads[used:, :] = jnp.zeros((grads.shape[0] - used, LANES), f32)
 
 
 def toeplitz_bases(plan, w_in, w_mid, w_out):
@@ -319,11 +329,9 @@
     )(*bases)
 
 
-def network(plan, grid, z_first, x_first, u_first, c_last, em_own, cot_own, weights):
+def network(plan, grid, z_first, x_first, u_first, c_last, em_own, cot_own, weights, packed_rows):
     layers, c = plan.layers, plan.c
     f32, bf16 = jnp.float32, jnp.bfloat16
-    block = round_up(27 * c, LANES)
-    width = (layers - 1) * block + 2 * LANES
     own = jax.ShapeDtypeStruct((plan.zs, plan.xs * LANES), f32)
     scratch = [
         pltpu.VMEM((3, plan.rows_in, plan.x(plan.halo_in) * LANES), f32),
@@ -341,7 +349,7 @@
     operands = (position, u_first, c_last, em_own, cot_own, *weights)
     return pl.pallas_call(
         lambda *refs: network_kernel(plan, grid, *refs),
-        out_shape=[own, own, jax.ShapeDtypeStruct((c, width), f32)],
+        out_shape=[own, own, jax.ShapeDtypeStruct((packed_rows, LANES), f32)],
         in_specs=[pl.BlockSpec(memory_space=pltpu.SMEM)] + [vmem] * (len(operands) - 1),
         out_specs=[vmem] * 3,
         scratch_shapes=scratch,
@@ -350,17 +358,60 @@
     )(*operands)
 
 
+def grad_rows(plan):
+    return ((plan.layers - 1) * (round_up(27 * plan.c, LANES) // LANES) + 2) * plan.c
+
+
 def unpack_grads(plan, packed):
     c, mids = plan.c, plan.layers - 1
-    block = round_up(27 * c, LANES)
-    mid = packed[:, : mids * block].reshape(c, mids, block)[:, :, : 27 * c]
-    mid = mid.reshape(c, mids, 3, 3, 3, c)
-    mid = jnp.transpose(mid, (1, 0, 5, 4, 2, 3))
-    thin = packed[:, mids * block :].reshape(c, 2, LANES)[:, :, :72].reshape(c, 2, 3, 3, 8)[..., :3]
-    thin = jnp.transpose(thin, (1, 0, 4, 2, 3))
+    block = round_up(27 * c, LANES) // LANES
+    per = LANES // c
+    blocks = packed[: grad_rows(plan)].reshape(mids * block + 2, c, LANES)
+    mid = blocks[: mids * block].reshape(mids, block, c, per, c)
+    mid = jnp.transpose(mid, (0, 1, 3, 2, 4)).reshape(mids, block * per, c, c)[:, :27]
+    mid = jnp.transpose(mid.reshape(mids, 3, 3, 3, c, c), (0, 4, 5, 1, 2, 3))
+    thin = blocks[mids * block :, :, :72].reshape(2, c, 3, 3, 8)[..., :3]
+    thin = jnp.transpose(thin, (0, 1, 4, 2, 3))
     grad_in = thin[0][:, None]
     grad_out = jnp.flip(thin[1], (1, 2, 3))[None]
     return grad_in, mid, grad_out
+
+
+CORES = 2
+
+
+def along_chips(axis):
+    count = lax.axis_size(axis)
+    return [list(range(core, count, CORES)) for core in range(CORES)]
+
+
+def within_chip(axis):
+    count = lax.axis_size(axis)
+    return [list(range(first, first + CORES)) for first in range(0, count, CORES)]
+
+
+def to_all(value, axis, groups=None):
+    count = lax.axis_size(axis) if groups is None else len(groups[0])
+    copies = jnp.broadcast_to(value[None], (count, *value.shape))
+    return lax.all_to_all(copies, axis, 0, 0, tiled=True, axis_index_groups=groups)
+
+
+def pair_gather(value):
+    return lax.all_gather(value, "sector", axis_index_groups=within_chip("sector"))
+
+
+def summed_everywhere(packed, slabs):
+    chips = along_chips("sector")
+    core = lax.rem(lax.axis_index("sector"), CORES)
+    share = packed.shape[0] // slabs
+    parts = packed.reshape(slabs, share, LANES)
+    own = jnp.sum(lax.all_to_all(parts, "slab", 0, 0, tiled=True), axis=0)
+    both = pair_gather(own)
+    own = both[0] + both[1]
+    half = lax.dynamic_slice_in_dim(own, core * (share // CORES), share // CORES, 0)
+    half = jnp.sum(to_all(half, "sector", chips), axis=0)
+    halves = to_all(half, "slab")
+    return jnp.transpose(pair_gather(halves), (1, 0, 2, 3)).reshape(packed.shape)
 
 
 def shards(
@@ -390,11 +441,17 @@
 
     weights = prepared_weights(plan, w_in, w_mid, w_out)
 
-    cols_row = jnp.pad(tile_cols.astype(f32), ((0, 0), (0, block_len - slots))).reshape(1, xs, ys)
-    sent = jnp.concatenate([image, sensitivity, cotangent, cols_row], axis=0)
-    got = lax.all_gather(sent, "sector", axis=1, tiled=True)
-    image_slab, sens_slab, cot_slab = got[:zs], got[zs : 2 * zs], got[2 * zs : 3 * zs]
-    every_cols = got[3 * zs].reshape(sectors, block_len)[:, :slots].reshape(-1)
+    cells = zs * xs
+    sent = [image, sensitivity, cotangent]
+    sent = jnp.concatenate([field.reshape(cells, ys) for field in sent], axis=0)
+    cols_row = jnp.pad(tile_cols.astype(f32), ((0, round_up(3 * cells + 1, 8) - 3 * cells - 1), (0, ys - slots)))
+    sent = jnp.concatenate([sent, cols_row], axis=0)
+    from_chips = to_all(sent, "sector", along_chips("sector"))
+    every_cols = from_chips[:, 3 * cells, :slots].reshape(-1)
+    got = jnp.transpose(pair_gather(from_chips)[:, :, : 3 * cells], (2, 1, 0, 3))
+    got = got.reshape(3, zs, xs, sectors, ys)
+    got = jnp.transpose(got, (0, 1, 3, 2, 4)).reshape(3, zs, sectors * xs, ys)
+    image_slab, sens_slab, cot_slab = got[0], got[1], got[2]
 
     values = tile_values[0]
     weight = (jnp.arange(slots) < tile_count[0, 0]).astype(f32) / block_len
@@ -403,7 +460,7 @@
     forward = forward * weight[:, None]
     lined = jnp.concatenate([forward, tile_rows[0].astype(f32)[:, None]], axis=1)
     lined = jnp.pad(lined, ((0, 0), (0, LANES - row_len - 1)))
-    every = lax.all_gather(lined, "slab", axis=0, tiled=True)
+    every = to_all(lined, "slab").reshape(slabs * slots, LANES)
     every_rows = every[:, row_len]
     placing = (every_rows[None, :] == jnp.arange(line_blocks, dtype=f32)[:, None]).astype(f32)
     projection = jnp.dot(placing, every[:, :row_len], precision=highest)
@@ -411,16 +468,20 @@
 
     backward = jnp.einsum("krv,kr->kv", values, ratio[tile_rows[0]], preferred_element_type=f32)
     backward = backward * weight[:, None]
-    every_back = lax.all_gather(backward, "sector", axis=0, tiled=True)
-    reach = -(-plan.halo_in // xs)
-    near = sector - reach + jnp.arange(2 * reach + 1)
+    every_back = to_all(backward, "sector", along_chips("sector")).reshape(-1, block_len)
+    halo = plan.halo_in
+    reach = -(-halo // xs)
+    core = lax.rem(sector, CORES)
+    span = 2 * reach + CORES
+    near = sector - core - reach + jnp.arange(span)
     wanted = (jnp.arange(zs)[:, None] * sectors + near[None, :]).astype(f32)
     good = jnp.logical_and(near >= 0, near < sectors)
     wanted = jnp.where(good[None, :], wanted, -1.0).reshape(-1)
     owning = (every_cols[None, :] == wanted[:, None]).astype(f32)
-    halo = plan.halo_in
-    back = jnp.dot(owning, every_back, precision=highest).reshape(zs, xs * (2 * reach + 1), ys)
-    back = back[:, reach * xs - halo : reach * xs + xs + halo]
+    of_core = jnp.dot(owning, every_back, precision=highest)
+    of_cores = pair_gather(of_core)
+    back = (of_cores[0] + of_cores[1]).reshape(zs, span * xs, ys)
+    back = lax.dynamic_slice_in_dim(back, core * xs + reach * xs - halo, xs + 2 * halo, 1)
 
     def window(field, halo, fill):
         padded = jnp.pad(field, ((0, 0), (halo, halo), (0, 0)), constant_values=fill)
@@ -431,7 +492,7 @@
 
     cot_wide = window(cot_slab, plan.halo_last, 0.0).astype(bf16)
     both = jnp.concatenate([em.astype(bf16), cot_wide], axis=1)
-    every_plane = lax.all_gather(both, "slab", axis=0, tiled=True)
+    every_plane = to_all(both, "slab").reshape(zs * slabs, both.shape[1], ys)
 
     def planes(lo, count, halo, lead, rows):
         field = every_plane[:, lo : lo + count]
@@ -454,9 +515,9 @@
         em_own.reshape(zs, xs * ys),
         cotangent.reshape(zs, xs * ys),
         weights,
+        round_up(grad_rows(plan), slabs * CORES * 8),
     )
-    cells = grid[0] * grid[1] * ys
-    packed = lax.psum(packed, ("sector", "slab")) * (1.0 / math.sqrt(cells))
+    packed = summed_everywhere(packed, slabs) * (1.0 / math.sqrt(grid[0] * grid[1] * ys))
     grad_in, grad_mid, grad_out = unpack_grads(plan, packed)
     return (
         new_image.reshape(zs, xs, ys),

time: 663 us -> 207 us (0.31)
  waiting for transfers between devices: 461 us -> 41.9 us
  blocking collectives: 109 us -> 43.3 us
  starting transfers between devices: 0.04 us -> 40.9 us
  between operations: 15.2 us -> 1.9 us
    psum x1 -> x0, waiting for transfers between devices: 461 us -> none  [shards(): packed = lax.psum(packed, ('sector', 'slab')) * (1.0 / math.sqrt(cells))]
    all_gather x4, blocking collectives: 109 us -> 25.3 us  [pair_gather(): lax.all_gather(value, 'sector', axis_index_groups=within_chip('sector'))]
    all_to_all x0 -> x6, waiting for transfers between devices: none -> 41.9 us  [the longest x5 33.7 us: to_all(): lax.all_to_all(copies, axis, 0, 0, tiled=True, axis_index_groups=groups)]
    all_to_all x0 -> x6, starting transfers between devices: none -> 40.9 us  [the longest x5 34.4 us: to_all(): lax.all_to_all(copies, axis, 0, 0, tiled=True, axis_index_groups=groups)]
    all_to_all x0 -> x1, blocking collectives: none -> 18 us  [to_all(): lax.all_to_all(copies, axis, 0, 0, tiled=True, axis_index_groups=groups)]
  transfers between devices with their start and end apart: 1 -> 6, of which waited for: 1 -> 5; matrix products, arithmetic and copies ran while one was open for 0% -> 8% of each run, Pallas kernels for 0% -> 2%
where the time goes in v2:
time: 207 us; the launch traced here: 206 us
  Pallas kernels  46.3 us (22%)
  blocking collectives  43.3 us (21%)
  waiting for transfers between devices  41.9 us (20%)
  starting transfers between devices  40.9 us (20%)
  local copies, waits for them, and re-layouts  27.4 us (13%)
  other arithmetic  3.3 us (2%)
    pallas_call x1, Pallas kernels, network(): pl.pallas_call(lambda *refs: network_kernel(plan, grid, *refs), out_shape...  42.7 us
    all_to_all x5, starting transfers between devices, to_all(): lax.all_to_all(copies, axis, 0, 0, tiled=True, axis_index_groups=groups)  34.4 us
    all_to_all x5, waiting for transfers between devices, to_all(): lax.all_to_all(copies, axis, 0, 0, tiled=True, axis_index_groups=groups)  33.7 us
    all_gather x4, blocking collectives, pair_gather(): lax.all_gather(value, 'sector', axis_index_groups=within_chip('sector'))  25.3 us
    all_to_all x1, blocking collectives, to_all(): lax.all_to_all(copies, axis, 0, 0, tiled=True, axis_index_groups=groups)  18 us
    all_to_all x1, waiting for transfers between devices, summed_everywhere(): own = jnp.sum(lax.all_to_all(parts, 'slab', 0, 0, tiled=True), axis=0)  8.13 us
    all_to_all x1, starting transfers between devices, summed_everywhere(): own = jnp.sum(lax.all_to_all(parts, 'slab', 0, 0, tiled=True), axis=0)  6.53 us
    pad x9, local copies, waits for them, and re-layouts, spread(): jnp.pad(flat, ((0, 0), (0, round_up(flat.shape[1], LANES) - flat.shape[1])))  4.65 us
  transfers between devices with their start and end apart: 6, of which 5 were waited for; matrix products, arithmetic and copies ran while one was open for 8% of the time, Pallas kernels for 2%

profile of v2, /device:TPU:1, one launch (start us, length us, event | category | flops | bytes accessed | tf_op | source)
XLA Modules:
  0.0 205.9 jit_solution(17629473654217248935)
XLA Ops:
  0.7 0.8 reshape.260
  1.4 0.7 reshape.261
  2.1 0.7 reshape.262
  2.8 0.7 convert_element_type.82
  3.5 0.7 broadcast_in_dim.59
  4.2 15.7 %all-to-all-start = ((f32[16,24,128]{2,1,0:T(8,128)}), f32[16,24,128]{2,1,0:T(8,128)S(1)}, u32[]{:S(2)}, u32[]{:S(2)}) async-start(f32[16,24,128]{2,1,0:T(8,128)} %broadcast_in_dim.59), calls=%async_computation | async-start | bytes 393216 | tf_op jit(solution)/shard_map/all_to_all | solution.py:396
  20.0 0.7 fusion.18
  21.3 0.7 bitcast_convert_fusion
  21.9 1.1 reverse_bitcast_fusion
  23.3 9.1 %all-to-all-done = f32[16,24,128]{2,1,0:T(8,128)S(1)} async-done(((f32[16,24,128]{2,1,0:T(8,128)}), f32[16,24,128]{2,1,0:T(8,128)S(1)}, u32[]{:S(2)}, u32[]{:S(2)}) %all-to-all-start) | async-done | bytes 196640 | tf_op jit(solution)/shard_map/all_to_all | solution.py:396
  32.5 6.5 %all-gather = f32[32,24,128]{2,1,0:T(8,128)S(1)} all-gather(f32[16,24,128]{2,1,0:T(8,128)S(1)} %all-to-all-done), channel_id=2, replica_groups={{0,16},{32,48},{64,80},{96,112},{128,144},{160,176},{192,208},{224,240}..., dimensions={0}, use_global_device_ids=true | all-gather | bytes 589824 | tf_op jit(solution)/shard_map/all_gather | solution.py:400
  40.3 0.7 broadcast_in_dim.62
  41.0 6.8 %all-to-all-start.1 = ((f32[16,12,128]{2,1,0:T(8,128)}), f32[16,12,128]{2,1,0:T(8,128)S(1)}, u32[]{:S(2)}, u32[]{:S(2)}) async-start(f32[16,12,128]{2,1,0:T(8,128)} %broadcast_in_dim.62), calls=%async_computation.1 | async-start | bytes 262144 | tf_op jit(solution)/shard_map/all_to_all | solution.py:396
  47.8 6.7 %all-to-all-done.1 = f32[16,12,128]{2,1,0:T(8,128)S(1)} async-done(((f32[16,12,128]{2,1,0:T(8,128)}), f32[16,12,128]{2,1,0:T(8,128)S(1)}, u32[]{:S(2)}, u32[]{:S(2)}) %all-to-all-start.1) | async-done | bytes 98336 | tf_op jit(solution)/shard_map/all_to_all | solution.py:396
  55.7 0.7 broadcast_in_dim.63
  56.5 4.6 %all-to-all-start.2 = ((f32[16,12,256]{2,1,0:T(8,128)}), f32[16,12,256]{2,1,0:T(8,128)S(1)}, u32[]{:S(2)}, u32[]{:S(2)}) async-start(f32[16,12,256]{2,1,0:T(8,128)} %broadcast_in_dim.63), calls=%async_computation.2 | async-start | bytes 524288 | tf_op jit(solution)/shard_map/all_to_all | solution.py:396
  61.7 12.2 %all-to-all-done.2 = f32[16,12,256]{2,1,0:T(8,128)S(1)} async-done(((f32[16,12,256]{2,1,0:T(8,128)}), f32[16,12,256]{2,1,0:T(8,128)S(1)}, u32[]{:S(2)}, u32[]{:S(2)}) %all-to-all-start.2) | async-done | bytes 196640 | tf_op jit(solution)/shard_map/all_to_all | solution.py:396
  74.1 8.3 %all-gather.4 = f32[2,30,256]{2,1,0:T(8,128)S(1)} all-gather(f32[1,30,256]{2,1,0:T(8,128)S(1)} %convolution_bitcast_fusion), channel_id=3, replica_groups={{0,16},{32,48},{64,80},{96,112},{128,144},{160,176},{192,208},{224,240}..., dimensions={0}, use_global_device_ids=true | all-gather | bytes 92160 | tf_op jit(solution)/shard_map/all_gather | solution.py:400
  82.5 0.8 broadcast_in_dim.64
  83.3 3.7 %all-to-all-start.3 = ((bf16[16,3,30,128]{3,2,1,0:T(8,128)(2,1)}), bf16[16,3,30,128]{3,2,1,0:T(8,128)(2,1)S(1)}, u32[]{:S(2)}, u32[]{:S(2)}) async-start(bf16[16,3,30,128]{3,2,1,0:T(8,128)(2,1)} %broadcast_in_dim.64), calls=%async_computation.3 | async-start | bytes 786432 | tf_op jit(solution)/shard_map/all_to_all | solution.py:396
  87.8 0.7 pad.115.refs_7_
  89.2 0.7 pad.119.refs_9_
  90.5 0.7 pad.117.refs_8_
  91.8 0.7 pad.110.refs_4_
  93.2 0.7 pad.112.refs_5_
  94.2 1.0 reshape.277.refs_6_
  95.3 0.6 pad.104.refs_1_
  96.1 0.6 pad.102.refs_0_
  97.0 0.6 copy.177
  97.6 0.6 broadcast_in_dim.113.refs_3_
  98.2 0.6 broadcast_in_dim.111.refs_2_
  98.8 3.6 %prepare_weights.1 = (bf16[544,256]{1,0:T(8,128)(2,1)}, bf16[352,256]{1,0:T(8,128)(2,1)}, bf16[8,1536]{1,0:T(8,128)(2,1)}, bf16[8,1536]{1,0:T(8,128)(2,1)}, bf16...) custom-call(bf16[32,256]{1,0:T(8,128)(2,1)} %pad.102.refs_0_, ...), custom_call_target="tpu_custom_call" | custom-call | tf_op jit(solution)/shard_map/prepare_weights/pallas_call | solution.py:322
  102.5 0.6 pad_add_fusion.refs_0_
  103.1 0.6 copy.178
  103.9 0.7 copy.173
  104.7 0.6 copy.174
  105.3 42.7 %network.1 = (f32[3,256]{1,0:T(4,128)}, f32[3,256]{1,0:T(4,128)}, f32[768,128]{1,0:T(8,128)}) custom-call(s32[2]{0:T(128)} %pad_add_fusion.refs_0_, bf16[24,2304]{1,0:T(8,128)(2,1)} %bitcast.135, bf16[24,1536]{1,0:T(8,128)(2,1)} %bitcast.140, f32[3,256]{1,0:T(4,128)} %bitcast.155, f32[3,256]{1,0:T(4,128)} %bitcast.154, ...), custom_call_target="tpu_custom_call" | custom-call | tf_op jit(solution)/shard_map/network/pallas_call | solution.py:350
  148.0 6.5 %all-to-all-start.4 = ((f32[16,48,128]{2,1,0:T(8,128)}), f32[16,48,128]{2,1,0:T(8,128)S(1)}, u32[]{:S(2)}, u32[]{:S(2)}) async-start(f32[16,48,128]{2,1,0:T(8,128)} %bitcast.136), calls=%async_computation.4 | async-start | bytes 786432 | tf_op jit(solution)/shard_map/all_to_all | solution.py:408
  154.5 8.1 %all-to-all-done.4 = f32[16,48,128]{2,1,0:T(8,128)S(1)} async-done(((f32[16,48,128]{2,1,0:T(8,128)}), f32[16,48,128]{2,1,0:T(8,128)S(1)}, u32[]{:S(2)}, u32[]{:S(2)}) %all-to-all-start.4) | async-done | bytes 393248 | tf_op jit(solution)/shard_map/all_to_all | solution.py:408
  162.7 4.1 %all-gather.2 = f32[96,128]{1,0:T(8,128)S(1)} all-gather(f32[48,128]{1,0:T(8,128)S(1)} %reduce_sum.18), channel_id=4, replica_groups={{0,16},{32,48},{64,80},{96,112},{128,144},{160,176},{192,208},{224,240}..., dimensions={0}, use_global_device_ids=true | all-gather | bytes 73728 | tf_op jit(solution)/shard_map/all_gather | solution.py:400
  166.9 18.0 %all_to_all.35 = f32[16,24,128]{2,1,0:T(8,128)S(1)} all-to-all(f32[16,24,128]{2,1,0:T(8,128)S(1)} %broadcast_in_dim.114), channel_id=1, replica_groups={{0,32,64,96,128,160,192,224,256,288,320,352,384,416,448,480},{16,48,80,..., dimensions={0} | all-to-all | bytes 393216 | tf_op jit(solution)/shard_map/all_to_all | solution.py:396
  184.9 0.7 broadcast_in_dim.115
  185.6 3.5 %all-to-all-start.6 = ((f32[16,24,128]{2,1,0:T(8,128)}), f32[16,24,128]{2,1,0:T(8,128)S(1)}, u32[]{:S(2)}, u32[]{:S(2)}) async-start(f32[16,24,128]{2,1,0:T(8,128)} %broadcast_in_dim.115), calls=%async_computation.6 | async-start | bytes 393216 | tf_op jit(solution)/shard_map/all_to_all | solution.py:396
  190.3 5.7 %all-to-all-done.6 = f32[16,24,128]{2,1,0:T(8,128)S(1)} async-done(((f32[16,24,128]{2,1,0:T(8,128)}), f32[16,24,128]{2,1,0:T(8,128)S(1)}, u32[]{:S(2)}, u32[]{:S(2)}) %all-to-all-start.6) | async-done | bytes 196640 | tf_op jit(solution)/shard_map/all_to_all | solution.py:396
  196.0 6.3 %all-gather.3 = f32[32,24,128]{2,1,0:T(8,128)S(1)} all-gather(f32[16,24,128]{2,1,0:T(8,128)S(1)} %all-to-all-done.6), channel_id=5, replica_groups={{0,16},{32,48},{64,80},{96,112},{128,144},{160,176},{192,208},{224,240}..., dimensions={0}, use_global_device_ids=true | all-gather | bytes 589824 | tf_op jit(solution)/shard_map/all_gather | solution.py:400
  203.2 1.2 slice.149
  204.6 0.6 copy.139
  205.2 0.6 copy.176
  (120 shorter events, 10.4 us)
Async XLA Ops:
  0.6 39.3 %copy-start = (bf16[1,12,104,256]{3,2,1,0:T(8,128)(2,1)S(1)}, bf16[1,12,104,256]{3,2,1,0:T(8,128)(2,1)}, u32[]{:S(2)}) copy-start(bf16[1,12,104,256]{3,2,1,0:T(8,128)(2,1)} %param.14) | copy-start | bytes 1916932
  0.6 22.6 %copy-start.9 = (s32[1,12]{1,0:T(1,128)S(1)}, s32[1,12]{1,0:T(1,128)}, u32[]{:S(2)}) copy-start(s32[1,12]{1,0:T(1,128)} %param.15) | copy-start | bytes 148
  4.2 28.3 %all-to-all-start = ((f32[16,24,128]{2,1,0:T(8,128)}), f32[16,24,128]{2,1,0:T(8,128)S(1)}, u32[]{:S(2)}, u32[]{:S(2)}) async-start(f32[16,24,128]{2,1,0:T(8,128)} %broadcast_in_dim.59), calls=%async_computation | async-start | bytes 393216 | tf_op jit(solution)/shard_map/all_to_all | solution.py:396
  39.0 15.7 %copy-start.4 = (f32[1,32,104]{2,1,0:T(8,128)S(1)}, f32[1,32,104]{2,1,0:T(8,128)}, u32[]{:S(2)}) copy-start(f32[1,32,104]{2,1,0:T(8,128)} %param.19) | copy-start | bytes 39940
  39.0 15.7 %copy-start.5 = (f32[1,32,104]{2,1,0:T(8,128)S(1)}, f32[1,32,104]{2,1,0:T(8,128)}, u32[]{:S(2)}) copy-start(f32[1,32,104]{2,1,0:T(8,128)} %param.18) | copy-start | bytes 39940
  40.2 21.0 %copy-start.1 = (bf16[3,32,32,3,3,3]{2,1,5,4,3,0:T(8,128)(2,1)S(1)}, bf16[3,32,32,3,3,3]{2,1,5,4,3,0:T(8,128)(2,1)}, u32[]{:S(2)}) copy-start(bf16[3,32,32,3,3,3]{2,1,5,4,3,0:T(8,128)(2,1)} %param.21) | copy-start | bytes 497668
  41.0 13.5 %all-to-all-start.1 = ((f32[16,12,128]{2,1,0:T(8,128)}), f32[16,12,128]{2,1,0:T(8,128)S(1)}, u32[]{:S(2)}, u32[]{:S(2)}) async-start(f32[16,12,128]{2,1,0:T(8,128)} %broadcast_in_dim.62), calls=%async_computation.1 | async-start | bytes 262144 | tf_op jit(solution)/shard_map/all_to_all | solution.py:396
  56.5 17.4 %all-to-all-start.2 = ((f32[16,12,256]{2,1,0:T(8,128)}), f32[16,12,256]{2,1,0:T(8,128)S(1)}, u32[]{:S(2)}, u32[]{:S(2)}) async-start(f32[16,12,256]{2,1,0:T(8,128)} %broadcast_in_dim.63), calls=%async_computation.2 | async-start | bytes 524288 | tf_op jit(solution)/shard_map/all_to_all | solution.py:396
  83.3 20.3 %all-to-all-start.3 = ((bf16[16,3,30,128]{3,2,1,0:T(8,128)(2,1)}), bf16[16,3,30,128]{3,2,1,0:T(8,128)(2,1)S(1)}, u32[]{:S(2)}, u32[]{:S(2)}) async-start(bf16[16,3,30,128]{3,2,1,0:T(8,128)(2,1)} %broadcast_in_dim.64), calls=%async_computation.3 | async-start | bytes 786432 | tf_op jit(solution)/shard_map/all_to_all | solution.py:396
  93.2 2.0 copy-start.3
  93.2 2.8 %copy-start.2 = (bf16[32,1,3,3,3]{0,4,3,2,1:T(4,128)(2,1)S(1)}, bf16[32,1,3,3,3]{0,4,3,2,1:T(4,128)(2,1)}, u32[]{:S(2)}) copy-start(bf16[32,1,3,3,3]{0,4,3,2,1:T(4,128)(2,1)} %param.20) | copy-start | bytes 5188
  93.9 3.1 %copy-start.6 = (f32[3,2,128]{2,1,0:T(2,128)S(1)}, f32[3,2,128]{2,1,0:T(2,128)}, u32[]{:S(2)}) copy-start(f32[3,2,128]{2,1,0:T(2,128)} %param.23) | copy-start | bytes 9220
  148.0 41.1 %copy-start.8 = (f32[3,256]{1,0:T(4,128)S(1)}, f32[3,256]{1,0:T(4,128)}, u32[]{:S(2)}) copy-start(f32[3,256]{1,0:T(4,128)} %get-tuple-element.28) | copy-start | bytes 9220
  148.0 41.7 %copy-start.7 = (f32[3,256]{1,0:T(4,128)S(1)}, f32[3,256]{1,0:T(4,128)}, u32[]{:S(2)}) copy-start(f32[3,256]{1,0:T(4,128)} %get-tuple-element.29) | copy-start | bytes 9220
  148.0 14.7 %all-to-all-start.4 = ((f32[16,48,128]{2,1,0:T(8,128)}), f32[16,48,128]{2,1,0:T(8,128)S(1)}, u32[]{:S(2)}, u32[]{:S(2)}) async-start(f32[16,48,128]{2,1,0:T(8,128)} %bitcast.136), calls=%async_computation.4 | async-start | bytes 786432 | tf_op jit(solution)/shard_map/all_to_all | solution.py:408
  185.6 10.4 %all-to-all-start.6 = ((f32[16,24,128]{2,1,0:T(8,128)}), f32[16,24,128]{2,1,0:T(8,128)S(1)}, u32[]{:S(2)}, u32[]{:S(2)}) async-start(f32[16,24,128]{2,1,0:T(8,128)} %broadcast_in_dim.115), calls=%async_computation.6 | async-start | bytes 393216 | tf_op jit(solution)/shard_map/all_to_all | solution.py:396

commit v3 on v2

--- a/solution.py
+++ b/solution.py
@@ -30,7 +30,7 @@
         return self.xs + 2 * halo
 
     def starts(self, planes):
-        count = -(-planes // 6)
+        count = -(-planes // 4)
         size = -(-planes // count)
         return size, [min(k * size, planes - size) for k in range(count)]
 
@@ -46,32 +46,66 @@
     return low, rows, high
 
 
-def prepare_kernel(plan, base_in, base_last, base_out, base_back, *refs):
-    mids = 2 * (plan.layers - 1)
-    bases, outs = refs[:mids], refs[mids:]
-    w_first, w_top, w_out, w_back = outs[:4]
+def prepare_kernel(plan, w_in, w_mid, w_out, *outs):
+    w_first, w_top, w_last, w_back = outs[:4]
     toeplitz = outs[4:]
-    c = plan.c
-    for base, out, step, planes in (
-        (base_in, w_first, 1, plan.z(plan.halo_u[1])),
-        (base_last, w_top, 1, plan.z(plan.halo_c[-1])),
-    ):
-        rows = base[...].astype(jnp.float32)
+    c, zs, mids = plan.c, plan.zs, plan.layers - 1
+    f32, bf16 = jnp.float32, jnp.bfloat16
+
+    def rolled(rows, out, step, planes):
         for k in range(planes):
             moved = rows if k == 0 else pltpu.roll(rows, k * step, 1)
-            out[k * c : (k + 1) * c, :] = moved.astype(jnp.bfloat16)
-    for base, out in ((base_out, w_out), (base_back, w_back)):
-        rows = base[...].astype(jnp.float32)
+            out[k * c : (k + 1) * c, :] = moved.astype(bf16)
+
+    for weights, out, rows, lead, planes, mirrored in (
+        (w_in, w_first, plan.rows_in, plan.lead_in, plan.z(plan.halo_u[1]), False),
+        (w_out, w_top, plan.rows_last, plan.lead_last, plan.z(plan.halo_c[-1]), True),
+    ):
+        tap = lax.broadcasted_iota(jnp.int32, (27, out.shape[1]), 0)
+        tap = 26 - tap if mirrored else tap
+        at = lax.rem(tap, 9) * rows + lead + lax.div(tap, 9)
+        lane = lax.broadcasted_iota(jnp.int32, at.shape, 1)
+        chosen = jnp.where(lane == at, 1.0, 0.0).astype(bf16)
+        base = lax.dot_general(
+            weights[...], chosen, (((0,), (0,)), ((), ())), preferred_element_type=f32
+        )
+        rolled(base, out, 1, planes)
+
+    def spread(tile, planes, width):
+        pieces = []
+        for k in range(9):
+            pieces += [tile(0, k), tile(1, k), tile(2, k)]
+            lines = pieces[0].shape[0]
+            pieces.append(jnp.zeros((lines, (planes - 3) * c), f32))
+        rest = width - 9 * planes * c
+        if rest:
+            pieces.append(jnp.zeros((lines, rest), f32))
+        return jnp.concatenate(pieces, axis=1)
+
+    for weights, out, mirrored in ((w_out, w_last, False), (w_in, w_back, True)):
+        lines = weights[...].astype(f32)
+
+        def row(dz, k, lines=lines, mirrored=mirrored):
+            tap = 26 - dz * 9 - k if mirrored else dz * 9 + k
+            return lines[tap : tap + 1, :]
+
+        rows = jnp.broadcast_to(spread(row, zs + 2, out.shape[1]), out.shape)
         line = lax.broadcasted_iota(jnp.int32, rows.shape, 0)
         total = jnp.where(line == 0, rows, 0.0)
-        for k in range(1, plan.zs):
+        for k in range(1, zs):
             total = total + jnp.where(line == k, pltpu.roll(rows, k * c, 1), 0.0)
-        out[...] = total.astype(jnp.bfloat16)
-    for base, out in zip(bases, toeplitz):
-        rows = base[...].astype(jnp.float32)
-        for k in range(out.shape[0] // c):
-            moved = rows if k == 0 else pltpu.roll(rows, k * c, 1)
-            out[k * c : (k + 1) * c, :] = moved.astype(jnp.bfloat16)
+        out[...] = total.astype(bf16)
+
+    for index, out in enumerate(toeplitz):
+        first = (index % mids) * 27
+
+        def tile(dz, k, first=first, mirrored=index >= mids):
+            if mirrored:
+                return w_mid[first + 26 - dz * 9 - k].astype(f32).T
+            return w_mid[first + dz * 9 + k].astype(f32)
+
+        size = out.shape[0] // c
+        rolled(spread(tile, size + 2, out.shape[1]), out, c, size)
 
 
 def inside(first, count, c, bound):
@@ -108,11 +142,11 @@
             good = jnp.logical_and(x_at + half >= 0, x_at + half < grid[1])
             part = jnp.where(jnp.logical_and(keep, good), part, 0.0)
             for dy, moved in enumerate(shifts(part)):
-                target[dy, rows, pl.ds(lane + half * LANES, LANES)] = moved.astype(bf16)
+                target[dy, rows, lane + half * LANES : lane + (half + 1) * LANES] = moved.astype(bf16)
 
     def one_channel(source, weight, lane):
         pieces = [
-            source[dy, :, pl.ds(lane + dx * LANES, 2 * LANES)] for dx in range(3) for dy in range(3)
+            source[dy, :, lane + dx * LANES : lane + (dx + 2) * LANES] for dx in range(3) for dy in range(3)
         ]
         stacked = jnp.concatenate(pieces, axis=0).astype(bf16)
         return jnp.dot(weight[:, : stacked.shape[0]], stacked, preferred_element_type=f32)
@@ -120,7 +154,7 @@
     def many_channels(source, weight, first_plane, planes, lane):
         rows = slice(first_plane * c, (first_plane + planes + 2) * c)
         pieces = [
-            source[dy, rows, pl.ds(lane + dx * LANES, 2 * LANES)]
+            source[dy, rows, lane + dx * LANES : lane + (dx + 2) * LANES]
             for dx in range(3)
             for dy in range(3)
         ]
@@ -130,7 +164,7 @@
     def forward_tail(value, layer, first_plane, planes, pair, lane):
         halo = plan.halo_u[layer]
         rows = slice(first_plane * c, (first_plane + planes) * c)
-        pre[layer - 1][rows, pl.ds(lane, 2 * LANES)] = value
+        pre[layer - 1][rows, lane : lane + 2 * LANES] = value
         act = value * jax.nn.sigmoid(value)
         keep = inside(z_first - halo + first_plane, planes, c, grid[0])
         store_shifted(u_sh[layer - 1], act, rows, lane, x_first - halo + 2 * pair, keep)
@@ -141,7 +175,7 @@
         from_plane = first_plane + halo_pre - halo
         preact = pre[layer - 1][
             from_plane * c : (from_plane + planes) * c,
-            pl.ds(lane + (halo_pre - halo) * LANES, 2 * LANES),
+            lane + (halo_pre - halo) * LANES : lane + (halo_pre - halo + 2) * LANES,
         ]
         sigma = jax.nn.sigmoid(preact)
         slope = sigma * (1.0 + preact * (1.0 - sigma))
@@ -151,11 +185,8 @@
         )
 
     def over_pairs(count, body):
-        def step(pair, carry):
-            body(pair, pl.multiple_of(pair * 2 * LANES, 2 * LANES))
-            return carry
-
-        lax.fori_loop(0, count, step, 0)
+        for pair in range(count):
+            body(pair, pair * 2 * LANES)
 
     halo = plan.halo_u[1]
 
@@ -276,57 +307,36 @@
         grads[used:, :] = jnp.zeros((grads.shape[0] - used, LANES), f32)
 
 
-def toeplitz_bases(plan, w_in, w_mid, w_out):
-    c, layers = plan.c, plan.layers
-    mids = w_mid.shape[0]
-
-    def spread(weights, planes, lead=0):
-        moved = jnp.transpose(weights, (0, 2, 3, 1, 4))
-        moved = jnp.pad(moved, ((0, 0), (0, 0), (0, 0), (lead, planes - 3 - lead), (0, 0)))
-        flat = moved.reshape(weights.shape[0], 9 * planes * weights.shape[4])
-        return jnp.pad(flat, ((0, 0), (0, round_up(flat.shape[1], LANES) - flat.shape[1])))
-
-    first = jnp.transpose(w_in, (0, 2, 3, 4, 1))
-    base_in = spread(first, plan.rows_in, plan.lead_in)
-    last_back = jnp.transpose(jnp.flip(w_out, (2, 3, 4)), (1, 2, 3, 4, 0))
-    base_last = spread(last_back, plan.rows_last, plan.lead_last)
-    out_fwd = jnp.transpose(w_out, (0, 2, 3, 4, 1))
-    in_back = jnp.transpose(jnp.flip(w_in, (2, 3, 4)), (1, 2, 3, 4, 0))
-    base_out = jnp.broadcast_to(spread(out_fwd, plan.zs + 2), (8, round_up(9 * (plan.zs + 2) * c, LANES)))
-    base_back = jnp.broadcast_to(spread(in_back, plan.zs + 2), base_out.shape)
-    bases, sizes = [], []
-    forward = jnp.transpose(w_mid, (0, 1, 3, 4, 5, 2))
-    backward = jnp.transpose(jnp.flip(w_mid, (3, 4, 5)), (0, 2, 3, 4, 5, 1))
-    for k in range(mids):
-        size, _ = plan.starts(plan.z(plan.halo_u[k + 2]))
-        bases.append(spread(forward[k], size + 2))
-        sizes.append(size)
-    for k in range(mids):
-        size, _ = plan.starts(plan.z(plan.halo_c[k]))
-        bases.append(spread(backward[k], size + 2))
-        sizes.append(size)
-    return (base_in, base_last, base_out, base_back, *bases), sizes
-
-
 def prepared_weights(plan, w_in, w_mid, w_out):
-    bases, sizes = toeplitz_bases(plan, w_in, w_mid, w_out)
-    c, bf16 = plan.c, jnp.bfloat16
+    c, mids = plan.c, plan.layers - 1
+    bf16 = jnp.bfloat16
+
+    def banded(halo):
+        size, _ = plan.starts(plan.z(halo))
+        return (size * c, round_up(9 * (size + 2) * c, LANES))
+
+    last = (8, round_up(9 * (plan.zs + 2) * c, LANES))
     shapes = [
-        (plan.z(plan.halo_u[1]) * c, bases[0].shape[1]),
-        (plan.z(plan.halo_c[-1]) * c, bases[1].shape[1]),
-        bases[2].shape,
-        bases[3].shape,
+        (plan.z(plan.halo_u[1]) * c, round_up(9 * plan.rows_in, LANES)),
+        (plan.z(plan.halo_c[-1]) * c, round_up(9 * plan.rows_last, LANES)),
+        last,
+        last,
     ]
-    shapes += [(size * c, base.shape[1]) for size, base in zip(sizes, bases[4:])]
+    shapes += [banded(plan.halo_u[k + 2]) for k in range(mids)]
+    shapes += [banded(plan.halo_c[k]) for k in range(mids)]
     vmem = pl.BlockSpec(memory_space=pltpu.VMEM)
     return pl.pallas_call(
         lambda *refs: prepare_kernel(plan, *refs),
         out_shape=[jax.ShapeDtypeStruct(shape, bf16) for shape in shapes],
-        in_specs=[vmem] * len(bases),
+        in_specs=[vmem] * 3,
         out_specs=[vmem] * len(shapes),
         compiler_params=pltpu.CompilerParams(vmem_limit_bytes=VMEM_BYTES),
         name="prepare_weights",
-    )(*bases)
+    )(
+        jnp.transpose(w_in, (2, 3, 4, 1, 0)).reshape(27, c),
+        jnp.transpose(w_mid, (0, 3, 4, 5, 1, 2)).reshape(mids * 27, c, c),
+        jnp.transpose(w_out, (2, 3, 4, 0, 1)).reshape(27, c),
+    )
 
 
 def network(plan, grid, z_first, x_first, u_first, c_last, em_own, cot_own, weights, packed_rows):
@@ -362,18 +372,47 @@
     return ((plan.layers - 1) * (round_up(27 * plan.c, LANES) // LANES) + 2) * plan.c
 
 
-def unpack_grads(plan, packed):
+def unpack_kernel(plan, factor, halves, grad_in, grad_mid, grad_out):
     c, mids = plan.c, plan.layers - 1
-    block = round_up(27 * c, LANES) // LANES
-    per = LANES // c
-    blocks = packed[: grad_rows(plan)].reshape(mids * block + 2, c, LANES)
-    mid = blocks[: mids * block].reshape(mids, block, c, per, c)
-    mid = jnp.transpose(mid, (0, 1, 3, 2, 4)).reshape(mids, block * per, c, c)[:, :27]
+    block, per, rows = round_up(27 * c, LANES) // LANES, LANES // c, halves.shape[2]
+
+    def packed(first):
+        pieces = []
+        for at in range(first, first + c, 8):
+            slab, inner = divmod(at, CORES * rows)
+            core, row = divmod(inner, rows)
+            pieces.append(halves[core, slab, row : row + 8, :])
+        return jnp.concatenate(pieces, axis=0) * factor
+
+    for layer in range(mids):
+        for k in range(block):
+            lanes = packed((layer * block + k) * c)
+            for tap in range(min(per, 27 - k * per)):
+                grad_mid[layer * 27 + k * per + tap] = lanes[:, tap * c : (tap + 1) * c]
+    for index, out in enumerate((grad_in, grad_out)):
+        taps = packed((mids * block + index) * c).T
+        for dz in range(3):
+            for k in range(9):
+                tap = dz * 9 + k
+                out[26 - tap if index else tap] = taps[k * 8 + dz : k * 8 + dz + 1, :]
+
+
+def unpack_grads(plan, halves, factor):
+    c, mids = plan.c, plan.layers - 1
+    f32 = jnp.float32
+    thin = jax.ShapeDtypeStruct((27, 1, c), f32)
+    vmem = pl.BlockSpec(memory_space=pltpu.VMEM)
+    grad_in, mid, grad_out = pl.pallas_call(
+        lambda *refs: unpack_kernel(plan, factor, *refs),
+        out_shape=[thin, jax.ShapeDtypeStruct((mids * 27, c, c), f32), thin],
+        in_specs=[vmem],
+        out_specs=[vmem] * 3,
+        compiler_params=pltpu.CompilerParams(vmem_limit_bytes=VMEM_BYTES),
+        name="unpack_gradients",
+    )(halves)
     mid = jnp.transpose(mid.reshape(mids, 3, 3, 3, c, c), (0, 4, 5, 1, 2, 3))
-    thin = blocks[mids * block :, :, :72].reshape(2, c, 3, 3, 8)[..., :3]
-    thin = jnp.transpose(thin, (0, 1, 4, 2, 3))
-    grad_in = thin[0][:, None]
-    grad_out = jnp.flip(thin[1], (1, 2, 3))[None]
+    grad_in = jnp.transpose(grad_in.reshape(3, 3, 3, 1, c), (4, 3, 0, 1, 2))
+    grad_out = jnp.transpose(grad_out.reshape(3, 3, 3, 1, c), (3, 4, 0, 1, 2))
     return grad_in, mid, grad_out
 
 
@@ -409,9 +448,9 @@
     both = pair_gather(own)
     own = both[0] + both[1]
     half = lax.dynamic_slice_in_dim(own, core * (share // CORES), share // CORES, 0)
-    half = jnp.sum(to_all(half, "sector", chips), axis=0)
-    halves = to_all(half, "slab")
-    return jnp.transpose(pair_gather(halves), (1, 0, 2, 3)).reshape(packed.shape)
+    half = to_all(half.astype(jnp.bfloat16), "sector", chips)
+    half = jnp.sum(half.astype(jnp.float32), axis=0)
+    return pair_gather(to_all(half, "slab"))
 
 
 def shards(
@@ -439,23 +478,29 @@
     plan = Plan(zs, xs, w_in.shape[0], w_mid.shape[0] + 1)
     grid = (zs * slabs, xs * sectors)
 
-    weights = prepared_weights(plan, w_in, w_mid, w_out)
-
     cells = zs * xs
-    sent = [image, sensitivity, cotangent]
-    sent = jnp.concatenate([field.reshape(cells, ys) for field in sent], axis=0)
-    cols_row = jnp.pad(tile_cols.astype(f32), ((0, round_up(3 * cells + 1, 8) - 3 * cells - 1), (0, ys - slots)))
-    sent = jnp.concatenate([sent, cols_row], axis=0)
-    from_chips = to_all(sent, "sector", along_chips("sector"))
-    every_cols = from_chips[:, 3 * cells, :slots].reshape(-1)
-    got = jnp.transpose(pair_gather(from_chips)[:, :, : 3 * cells], (2, 1, 0, 3))
-    got = got.reshape(3, zs, xs, sectors, ys)
-    got = jnp.transpose(got, (0, 1, 3, 2, 4)).reshape(3, zs, sectors * xs, ys)
-    image_slab, sens_slab, cot_slab = got[0], got[1], got[2]
+    chips = along_chips("sector")
+    cols_row = jnp.pad(tile_cols.astype(bf16), ((0, round_up(cells + 1, 8) - cells - 1), (0, ys - slots)))
+    sent = jnp.concatenate([image.astype(bf16).reshape(cells, ys), cols_row], axis=0)
+    from_chips = to_all(sent, "sector", chips)
+    every_cols = from_chips[:, cells, :slots].astype(f32).reshape(-1)
+    got = pair_gather(from_chips[:, :cells])
+    got = jnp.transpose(got.reshape(CORES, len(chips[0]), zs, xs, ys), (2, 1, 0, 3, 4))
+    blocks = got.reshape(zs * sectors, block_len)
+
+    fields = jnp.concatenate([field.reshape(cells, ys) for field in (image, sensitivity, cotangent)], axis=0)
+    fields = jnp.pad(fields, ((0, round_up(3 * cells, 8) - 3 * cells), (0, 0)))
+    fields, from_chips = lax.optimization_barrier((fields, from_chips))
+    reach = -(-plan.halo_in // (xs * CORES))
+    near_fields = []
+    for chip in range(-reach, reach + 1):
+        step = chip * CORES
+        pairs = [(k + step, k) for k in range(sectors) if 0 <= k + step < sectors]
+        near_fields.append(lax.ppermute(fields, "sector", pairs) if chip else fields)
+    near_fields = jnp.concatenate([field[: 3 * cells] for field in near_fields], axis=0)
 
     values = tile_values[0]
     weight = (jnp.arange(slots) < tile_count[0, 0]).astype(f32) / block_len
-    blocks = image_slab.astype(bf16).reshape(zs * sectors, block_len)
     forward = jnp.einsum("krv,kv->kr", values, blocks[tile_cols[0]], preferred_element_type=f32)
     forward = forward * weight[:, None]
     lined = jnp.concatenate([forward, tile_rows[0].astype(f32)[:, None]], axis=1)
@@ -468,30 +513,35 @@
 
     backward = jnp.einsum("krv,kr->kv", values, ratio[tile_rows[0]], preferred_element_type=f32)
     backward = backward * weight[:, None]
-    every_back = to_all(backward, "sector", along_chips("sector")).reshape(-1, block_len)
+    every_back = to_all(backward, "sector", chips).reshape(-1, block_len)
+    weights = prepared_weights(plan, w_in, w_mid, w_out)
+    every_back, weights = lax.optimization_barrier((every_back, weights))
     halo = plan.halo_in
-    reach = -(-halo // xs)
     core = lax.rem(sector, CORES)
-    span = 2 * reach + CORES
-    near = sector - core - reach + jnp.arange(span)
+    span = (2 * reach + 1) * CORES
+    near = sector - core - reach * CORES + jnp.arange(span)
     wanted = (jnp.arange(zs)[:, None] * sectors + near[None, :]).astype(f32)
     good = jnp.logical_and(near >= 0, near < sectors)
     wanted = jnp.where(good[None, :], wanted, -1.0).reshape(-1)
     owning = (every_cols[None, :] == wanted[:, None]).astype(f32)
-    of_core = jnp.dot(owning, every_back, precision=highest)
-    of_cores = pair_gather(of_core)
-    back = (of_cores[0] + of_cores[1]).reshape(zs, span * xs, ys)
-    back = lax.dynamic_slice_in_dim(back, core * xs + reach * xs - halo, xs + 2 * halo, 1)
-
-    def window(field, halo, fill):
-        padded = jnp.pad(field, ((0, 0), (halo, halo), (0, 0)), constant_values=fill)
-        return lax.dynamic_slice_in_dim(padded, sector * xs, xs + 2 * halo, 1)
-
-    em = window(image_slab, halo, 0.0) * back / window(sens_slab, halo, 1.0)
-    em_own = em[:, halo : halo + xs]
-
-    cot_wide = window(cot_slab, plan.halo_last, 0.0).astype(bf16)
-    both = jnp.concatenate([em.astype(bf16), cot_wide], axis=1)
+    of_core = jnp.dot(owning, every_back, precision=highest).reshape(-1, ys)
+    of_cores = pair_gather(jnp.concatenate([of_core, near_fields], axis=0))
+    back = of_cores[:, : of_core.shape[0]]
+    back = (back[0] + back[1]).reshape(zs, span * xs, ys)
+    near_fields = of_cores[:, of_core.shape[0] :].reshape(CORES, 2 * reach + 1, 3, zs, xs, ys)
+    near_fields = jnp.transpose(near_fields, (2, 3, 1, 0, 4, 5)).reshape(3, zs, span * xs, ys)
+    row = (sector - core - reach * CORES) * xs + jnp.arange(span * xs)
+    good = jnp.logical_and(row >= 0, row < grid[1])[None, :, None]
+    em = jnp.where(good, near_fields[0] * back / near_fields[1], 0.0)
+    cot_near = jnp.where(good, near_fields[2], 0.0)
+
+    def window(field, halo):
+        return lax.dynamic_slice_in_dim(field, (core + reach * CORES) * xs - halo, xs + 2 * halo, 1)
+
+    em_own = window(em, 0)
+
+    both = [window(em, halo).astype(bf16), window(cot_near, plan.halo_last).astype(bf16)]
+    both = jnp.concatenate(both, axis=1)
     every_plane = to_all(both, "slab").reshape(zs * slabs, both.shape[1], ys)
 
     def planes(lo, count, halo, lead, rows):
@@ -517,8 +567,9 @@
         weights,
         round_up(grad_rows(plan), slabs * CORES * 8),
     )
-    packed = summed_everywhere(packed, slabs) * (1.0 / math.sqrt(grid[0] * grid[1] * ys))
-    grad_in, grad_mid, grad_out = unpack_grads(plan, packed)
+    halves = summed_everywhere(packed, slabs)
+    factor = 1.0 / math.sqrt(grid[0] * grid[1] * ys)
+    grad_in, grad_mid, grad_out = unpack_grads(plan, halves, factor)
     return (
         new_image.reshape(zs, xs, ys),
         em_grad.reshape(zs, xs, ys),

time: 207 us -> 174 us (0.84)
  Pallas kernels: 46.3 us -> 25.4 us
  local copies, waits for them, and re-layouts: 27.4 us -> 11.8 us
  starting transfers between devices: 40.9 us -> 48.4 us
  waiting for transfers between devices: 41.9 us -> 36.2 us
    pallas_call x1, Pallas kernels: 42.7 us -> 19.1 us  [network(): pl.pallas_call(lambda *refs: network_kernel(plan, grid, *refs), out_shape...]
    ppermute x0 -> x4, starting transfers between devices: none -> 11.5 us  [shards(): lax.ppermute(fields, 'sector', pairs)]
    all_to_all x1, blocking collectives: 18 us -> 25.5 us  [to_all(): lax.all_to_all(copies, axis, 0, 0, tiled=True, axis_index_groups=groups)]
    all_gather x4, blocking collectives: 25.3 us -> 18.6 us  [pair_gather(): lax.all_gather(value, 'sector', axis_index_groups=within_chip('sector'))]
    all_to_all x5, waiting for transfers between devices: 33.7 us -> 27.7 us  [to_all(): lax.all_to_all(copies, axis, 0, 0, tiled=True, axis_index_groups=groups)]
    pad x19 -> x0, local copies, waits for them, and re-layouts: 5.64 us -> none  [the longest x9 4.65 us: spread(): jnp.pad(flat, ((0, 0), (0, round_up(flat.shape[1], LANES) - flat.shape[1])))]
    reshape x15 -> x8, local copies, waits for them, and re-layouts: 5.72 us -> 1.99 us  [the longest x3 0.71 us: shards(): field.reshape(cells, ys)]
    all_to_all x1, starting transfers between devices: 6.53 us -> 3.61 us  [summed_everywhere(): own = jnp.sum(lax.all_to_all(parts, 'slab', 0, 0, tiled=True), axis=0)]
  transfers between devices with their start and end apart: 6 -> 10, of which waited for: 5 -> 6; matrix products, arithmetic and copies ran while one was open for 8% -> 4% of each run, Pallas kernels for 2% -> 2%
where the time goes in v3:
time: 174 us; the launch traced here: 173 us
  starting transfers between devices  48.4 us (28%)
  blocking collectives  44.1 us (25%)
  waiting for transfers between devices  36.2 us (21%)
  Pallas kernels  25.4 us (15%)
  local copies, waits for them, and re-layouts  11.8 us (7%)
  other arithmetic  4.9 us (3%)
  between operations  1.76 us (1%)
    all_to_all x5, starting transfers between devices, to_all(): lax.all_to_all(copies, axis, 0, 0, tiled=True, axis_index_groups=groups)  33.3 us
    all_to_all x5, waiting for transfers between devices, to_all(): lax.all_to_all(copies, axis, 0, 0, tiled=True, axis_index_groups=groups)  27.7 us
    all_to_all x1, blocking collectives, to_all(): lax.all_to_all(copies, axis, 0, 0, tiled=True, axis_index_groups=groups)  25.5 us
    pallas_call x1, Pallas kernels, network(): pl.pallas_call(lambda *refs: network_kernel(plan, grid, *refs), out_shape...  19.1 us
    all_gather x4, blocking collectives, pair_gather(): lax.all_gather(value, 'sector', axis_index_groups=within_chip('sector'))  18.6 us
    ppermute x4, starting transfers between devices, shards(): lax.ppermute(fields, 'sector', pairs)  11.5 us
    all_to_all x1, waiting for transfers between devices, summed_everywhere(): own = jnp.sum(lax.all_to_all(parts, 'slab', 0, 0, tiled=True), axis=0)  8.13 us
    pallas_call x1, Pallas kernels, prepared_weights(): pl.pallas_call(lambda *refs: prepare_kernel(plan, *refs), out_shape=[jax....  3.98 us
  transfers between devices with their start and end apart: 10, of which 6 were waited for; matrix products, arithmetic and copies ran while one was open for 4% of the time, Pallas kernels for 2%

profile of v3, /device:TPU:1, one launch (start us, length us, event | category | flops | bytes accessed | tf_op | source)
XLA Modules:
  0.0 173.4 jit_solution(17324950290762044390)
XLA Ops:
  0.7 0.7 convert_element_type.71
  1.4 0.7 convert_element_type.70
  2.1 0.6 broadcast_in_dim.66
  2.7 15.7 %all-to-all-start = ((bf16[16,8,128]{2,1,0:T(8,128)(2,1)}), bf16[16,8,128]{2,1,0:T(8,128)(2,1)S(1)}, u32[]{:S(2)}, u32[]{:S(2)}) async-start(bf16[16,8,128]{2,1,0:T(8,128)(2,1)} %broadcast_in_dim.66), calls=%async_computation | async-start | bytes 65536 | tf_op jit(solution)/shard_map/all_to_all | solution.py:435
  18.5 0.7 fusion.22
  19.1 0.7 bitcast_convert_fusion
  19.8 0.7 fusion.21
  21.1 0.7 reshape.258
  21.9 8.0 %all-to-all-done = bf16[16,8,128]{2,1,0:T(8,128)(2,1)S(1)} async-done(((bf16[16,8,128]{2,1,0:T(8,128)(2,1)}), bf16[16,8,128]{2,1,0:T(8,128)(2,1)S(1)}, u32[]{:S(2)}, u32[]{:S(2)}) %all-to-all-start) | async-done | bytes 32800 | tf_op jit(solution)/shard_map/all_to_all | solution.py:435
  30.0 3.5 %all-gather = bf16[32,6,128]{2,0,1:T(8,128)(2,1)S(1)} all-gather(bf16[16,6,128]{2,0,1:T(8,128)(2,1)S(1)} %copy.46), channel_id=2, replica_groups={{0,16},{32,48},{64,80},{96,112},{128,144},{160,176},{192,208},{224,240}..., dimensions={0}, use_global_device_ids=true | all-gather | bytes 73728 | tf_op jit(solution)/shard_map/all_gather | solution.py:439
  33.6 0.6 gather_fusion
  34.1 0.3 fusion.4
  34.6 0.7 broadcast_in_dim.105
  35.3 6.8 %all-to-all-start.1 = ((f32[16,12,128]{2,1,0:T(8,128)}), f32[16,12,128]{2,1,0:T(8,128)S(1)}, u32[]{:S(2)}, u32[]{:S(2)}) async-start(f32[16,12,128]{2,1,0:T(8,128)} %broadcast_in_dim.105), calls=%async_computation.1 | async-start | bytes 262144 | tf_op jit(solution)/shard_map/all_to_all | solution.py:435
  42.0 6.7 %all-to-all-done.1 = f32[16,12,128]{2,1,0:T(8,128)S(1)} async-done(((f32[16,12,128]{2,1,0:T(8,128)}), f32[16,12,128]{2,1,0:T(8,128)S(1)}, u32[]{:S(2)}, u32[]{:S(2)}) %all-to-all-start.1) | async-done | bytes 98336 | tf_op jit(solution)/shard_map/all_to_all | solution.py:435
  49.1 0.6 gather_fusion.1
  50.0 0.7 broadcast_in_dim.106
  50.7 3.5 %all-to-all-start.2 = ((f32[16,12,256]{2,1,0:T(8,128)}), f32[16,12,256]{2,1,0:T(8,128)S(1)}, u32[]{:S(2)}, u32[]{:S(2)}) async-start(f32[16,12,256]{2,1,0:T(8,128)} %broadcast_in_dim.106), calls=%async_computation.2 | async-start | bytes 524288 | tf_op jit(solution)/shard_map/all_to_all | solution.py:435
  54.4 0.6 reshape.254.refs_0_
  55.1 0.6 reshape.256.refs_2_
  55.8 4.0 %prepare_weights.1 = (bf16[544,256]{1,0:T(8,128)(2,1)}, bf16[352,256]{1,0:T(8,128)(2,1)}, bf16[8,1536]{1,0:T(8,128)(2,1)}, bf16[8,1536]{1,0:T(8,128)(2,1)}, bf16...) custom-call(bf16[27,32]{1,0:T(8,128)(2,1)} %reshape.254.refs_0_, ...), custom_call_target="tpu_custom_call" | custom-call | tf_op jit(solution)/shard_map/prepare_weights/pallas_call | solution.py:328
  59.8 1.3 collective-permute-start.3
  61.1 1.3 collective-permute-start.2
  62.4 4.0 %collective-permute-start.1 = (f32[24,128]{1,0:T(8,128)S(1)}, f32[24,128]{1,0:T(8,128)S(1)}, u32[]{:S(2)}, u32[]{:S(2)}) collective-permute-start(f32[24,128]{1,0:T(8,128)S(1)} %select_maximum_fusion), channel_id=1, source_target_pairs={{0,32},{16,48},{32,64},{48,80},{64,96},{80,112},{96,128},{112,144}... | collective-permute-start | bytes 36872 | tf_op jit(solution)/shard_map/ppermute | solution.py:499
  66.4 4.9 %collective-permute-start = (f32[24,128]{1,0:T(8,128)S(1)}, f32[24,128]{1,0:T(8,128)S(1)}, u32[]{:S(2)}, u32[]{:S(2)}) collective-permute-start(f32[24,128]{1,0:T(8,128)S(1)} %select_maximum_fusion), channel_id=1, source_target_pairs={{0,64},{16,80},{32,96},{48,112},{64,128},{80,144},{96,160},{112,17... | collective-permute-start | bytes 36872 | tf_op jit(solution)/shard_map/ppermute | solution.py:499
  71.7 0.4 collective-permute-done
  72.1 0.5 concatenate.18
  72.6 5.0 %all-gather.4 = f32[2,150,128]{2,1,0:T(8,128)S(1)} all-gather(f32[1,150,128]{2,1,0:T(8,128)S(1)} %bitcast.93), channel_id=3, replica_groups={{0,16},{32,48},{64,80},{96,112},{128,144},{160,176},{192,208},{224,240}..., dimensions={0}, use_global_device_ids=true | all-gather | bytes 230400 | tf_op jit(solution)/shard_map/all_gather | solution.py:439
  78.1 0.8 broadcast_in_dim.108
  78.9 3.7 %all-to-all-start.3 = ((bf16[16,3,30,128]{3,2,1,0:T(8,128)(2,1)}), bf16[16,3,30,128]{3,2,1,0:T(8,128)(2,1)S(1)}, u32[]{:S(2)}, u32[]{:S(2)}) async-start(bf16[16,3,30,128]{3,2,1,0:T(8,128)(2,1)} %broadcast_in_dim.108), calls=%async_computation.3 | async-start | bytes 786432 | tf_op jit(solution)/shard_map/all_to_all | solution.py:435
  82.7 0.6 copy.66
  83.3 0.7 pad_add_fusion.refs_0_
  83.9 0.6 copy.67
  84.5 7.2 %all-to-all-done.3 = bf16[16,3,30,128]{3,2,1,0:T(8,128)(2,1)S(1)} async-done(((bf16[16,3,30,128]{3,2,1,0:T(8,128)(2,1)}), bf16[16,3,30,128]{3,2,1,0:T(8,128)(2,1)S(1)}, u32[]{:S(2)}, u32[]{:S(2)}) %all-to-all-start.3) | async-done | bytes 368672 | tf_op jit(solution)/shard_map/all_to_all | solution.py:435
  92.0 0.7 copy.63
  92.8 0.6 copy.64
  93.5 19.1 %network.1 = (f32[3,256]{1,0:T(4,128)}, f32[3,256]{1,0:T(4,128)}, f32[768,128]{1,0:T(8,128)}) custom-call(s32[2]{0:T(128)} %pad_add_fusion.refs_0_, bf16[24,2304]{1,0:T(8,128)(2,1)} %bitcast.90, bf16[24,1536]{1,0:T(8,128)(2,1)} %bitcast.96, f32[3,256]{1,0:T(4,128)} %bitcast.105, f32[3,256]{1,0:T(4,128)} %bitcast.104, ...), custom_call_target="tpu_custom_call" | custom-call | tf_op jit(solution)/shard_map/network/pallas_call | solution.py:360
  112.5 3.6 %all-to-all-start.4 = ((f32[16,48,128]{2,1,0:T(8,128)}), f32[16,48,128]{2,1,0:T(8,128)S(1)}, u32[]{:S(2)}, u32[]{:S(2)}) async-start(f32[16,48,128]{2,1,0:T(8,128)} %bitcast.91), calls=%async_computation.4 | async-start | bytes 786432 | tf_op jit(solution)/shard_map/all_to_all | solution.py:447
  116.2 8.1 %all-to-all-done.4 = f32[16,48,128]{2,1,0:T(8,128)S(1)} async-done(((f32[16,48,128]{2,1,0:T(8,128)}), f32[16,48,128]{2,1,0:T(8,128)S(1)}, u32[]{:S(2)}, u32[]{:S(2)}) %all-to-all-start.4) | async-done | bytes 393248 | tf_op jit(solution)/shard_map/all_to_all | solution.py:447
  124.3 4.1 %all-gather.2 = f32[96,128]{1,0:T(8,128)S(1)} all-gather(f32[48,128]{1,0:T(8,128)S(1)} %reduce_sum.18), channel_id=4, replica_groups={{0,16},{32,48},{64,80},{96,112},{128,144},{160,176},{192,208},{224,240}..., dimensions={0}, use_global_device_ids=true | all-gather | bytes 73728 | tf_op jit(solution)/shard_map/all_gather | solution.py:439
  128.5 25.5 %all_to_all.35 = bf16[16,24,128]{2,1,0:T(8,128)(2,1)S(1)} all-to-all(bf16[16,24,128]{2,1,0:T(8,128)(2,1)S(1)} %broadcast_in_dim.112), channel_id=1, replica_groups={{0,32,64,96,128,160,192,224,256,288,320,352,384,416,448,480},{16,48,80,..., dimensions={0} | all-to-all | bytes 196608 | tf_op jit(solution)/shard_map/all_to_all | solution.py:435
  154.1 0.7 broadcast_in_dim.113
  154.7 3.5 %all-to-all-start.6 = ((f32[16,24,128]{2,1,0:T(8,128)}), f32[16,24,128]{2,1,0:T(8,128)S(1)}, u32[]{:S(2)}, u32[]{:S(2)}) async-start(f32[16,24,128]{2,1,0:T(8,128)} %broadcast_in_dim.113), calls=%async_computation.6 | async-start | bytes 393216 | tf_op jit(solution)/shard_map/all_to_all | solution.py:435
  158.3 0.6 reshape.267
  158.9 0.6 reshape.268
  159.5 5.7 %all-to-all-done.6 = f32[16,24,128]{2,1,0:T(8,128)S(1)} async-done(((f32[16,24,128]{2,1,0:T(8,128)}), f32[16,24,128]{2,1,0:T(8,128)S(1)}, u32[]{:S(2)}, u32[]{:S(2)}) %all-to-all-start.6) | async-done | bytes 196640 | tf_op jit(solution)/shard_map/all_to_all | solution.py:435
  165.2 5.9 %all-gather.3 = f32[32,24,128]{2,1,0:T(8,128)} all-gather(f32[16,24,128]{2,1,0:T(8,128)S(1)} %all-to-all-done.6), channel_id=5, replica_groups={{0,16},{32,48},{64,80},{96,112},{128,144},{160,176},{192,208},{224,240}..., dimensions={0}, use_global_device_ids=true | all-gather | bytes 589824 | tf_op jit(solution)/shard_map/all_gather | solution.py:439
  171.0 2.4 %unpack_gradients.1 = (f32[27,1,32]{2,1,0:T(1,128)}, f32[81,32,32]{2,1,0:T(8,128)}, f32[27,1,32]{2,1,0:T(1,128)}) custom-call(f32[2,16,24,128]{3,2,1,0:T(8,128)} %bitcast.87), custom_call_target="tpu_custom_call" | custom-call | tf_op jit(solution)/shard_map/unpack_gradients/pallas_call | solution.py:405
  (81 shorter events, 2.5 us)
Async XLA Ops:
  0.6 33.5 %copy-start = (bf16[1,12,104,256]{3,2,1,0:T(8,128)(2,1)S(1)}, bf16[1,12,104,256]{3,2,1,0:T(8,128)(2,1)}, u32[]{:S(2)}) copy-start(bf16[1,12,104,256]{3,2,1,0:T(8,128)(2,1)} %param.14) | copy-start | bytes 1916932
  0.6 48.3 %copy-start.1 = (f32[1,32,104]{2,1,0:T(8,128)S(1)}, f32[1,32,104]{2,1,0:T(8,128)}, u32[]{:S(2)}) copy-start(f32[1,32,104]{2,1,0:T(8,128)} %param.19) | copy-start | bytes 39940
  0.7 48.3 %copy-start.2 = (f32[1,32,104]{2,1,0:T(8,128)S(1)}, f32[1,32,104]{2,1,0:T(8,128)}, u32[]{:S(2)}) copy-start(f32[1,32,104]{2,1,0:T(8,128)} %param.18) | copy-start | bytes 39940
  2.7 27.2 %all-to-all-start = ((bf16[16,8,128]{2,1,0:T(8,128)(2,1)}), bf16[16,8,128]{2,1,0:T(8,128)(2,1)S(1)}, u32[]{:S(2)}, u32[]{:S(2)}) async-start(bf16[16,8,128]{2,1,0:T(8,128)(2,1)} %broadcast_in_dim.66), calls=%async_computation | async-start | bytes 65536 | tf_op jit(solution)/shard_map/all_to_all | solution.py:435
  34.4 20.0 %copy-start.8 = (f32[3,2,128]{2,1,0:T(2,128)S(1)}, f32[3,2,128]{2,1,0:T(2,128)}, u32[]{:S(2)}) copy-start(f32[3,2,128]{2,1,0:T(2,128)} %param.13) | copy-start | bytes 9220
  34.4 20.0 %copy-start.3 = (f32[3,2,128]{2,1,0:T(2,128)S(1)}, f32[3,2,128]{2,1,0:T(2,128)}, u32[]{:S(2)}) copy-start(f32[3,2,128]{2,1,0:T(2,128)} %param.23) | copy-start | bytes 9220
  34.4 20.0 %copy-start.4 = (bf16[32,1,3,3,3]{0,4,3,2,1:T(4,128)(2,1)S(1)}, bf16[32,1,3,3,3]{0,4,3,2,1:T(4,128)(2,1)}, u32[]{:S(2)}) copy-start(bf16[32,1,3,3,3]{0,4,3,2,1:T(4,128)(2,1)} %param.20) | copy-start | bytes 5188
  34.4 20.6 %copy-start.5 = (bf16[1,32,3,3,3]{1,4,3,2,0:T(4,128)(2,1)S(1)}, bf16[1,32,3,3,3]{1,4,3,2,0:T(4,128)(2,1)}, u32[]{:S(2)}) copy-start(bf16[1,32,3,3,3]{1,4,3,2,0:T(4,128)(2,1)} %param.22) | copy-start | bytes 5188
  35.3 13.5 %all-to-all-start.1 = ((f32[16,12,128]{2,1,0:T(8,128)}), f32[16,12,128]{2,1,0:T(8,128)S(1)}, u32[]{:S(2)}, u32[]{:S(2)}) async-start(f32[16,12,128]{2,1,0:T(8,128)} %broadcast_in_dim.105), calls=%async_computation.1 | async-start | bytes 262144 | tf_op jit(solution)/shard_map/all_to_all | solution.py:435
  50.7 20.7 %all-to-all-start.2 = ((f32[16,12,256]{2,1,0:T(8,128)}), f32[16,12,256]{2,1,0:T(8,128)S(1)}, u32[]{:S(2)}, u32[]{:S(2)}) async-start(f32[16,12,256]{2,1,0:T(8,128)} %broadcast_in_dim.106), calls=%async_computation.2 | async-start | bytes 524288 | tf_op jit(solution)/shard_map/all_to_all | solution.py:435
  59.8 11.9 %collective-permute-start.3 = (f32[24,128]{1,0:T(8,128)S(1)}, f32[24,128]{1,0:T(8,128)S(1)}, u32[]{:S(2)}, u32[]{:S(2)}) collective-permute-start(f32[24,128]{1,0:T(8,128)S(1)} %select_maximum_fusion), channel_id=1, source_target_pairs={{64,0},{80,16},{96,32},{112,48},{128,64},{144,80},{160,96},{176,11... | collective-permute-start | bytes 36872 | tf_op jit(solution)/shard_map/ppermute | solution.py:499
  61.1 10.6 %collective-permute-start.2 = (f32[24,128]{1,0:T(8,128)S(1)}, f32[24,128]{1,0:T(8,128)S(1)}, u32[]{:S(2)}, u32[]{:S(2)}) collective-permute-start(f32[24,128]{1,0:T(8,128)S(1)} %select_maximum_fusion), channel_id=1, source_target_pairs={{32,0},{48,16},{64,32},{80,48},{96,64},{112,80},{128,96},{144,112}... | collective-permute-start | bytes 36872 | tf_op jit(solution)/shard_map/ppermute | solution.py:499
  62.4 9.3 %collective-permute-start.1 = (f32[24,128]{1,0:T(8,128)S(1)}, f32[24,128]{1,0:T(8,128)S(1)}, u32[]{:S(2)}, u32[]{:S(2)}) collective-permute-start(f32[24,128]{1,0:T(8,128)S(1)} %select_maximum_fusion), channel_id=1, source_target_pairs={{0,32},{16,48},{32,64},{48,80},{64,96},{80,112},{96,128},{112,144}... | collective-permute-start | bytes 36872 | tf_op jit(solution)/shard_map/ppermute | solution.py:499
  66.4 5.7 %collective-permute-start = (f32[24,128]{1,0:T(8,128)S(1)}, f32[24,128]{1,0:T(8,128)S(1)}, u32[]{:S(2)}, u32[]{:S(2)}) collective-permute-start(f32[24,128]{1,0:T(8,128)S(1)} %select_maximum_fusion), channel_id=1, source_target_pairs={{0,64},{16,80},{32,96},{48,112},{64,128},{80,144},{96,160},{112,17... | collective-permute-start | bytes 36872 | tf_op jit(solution)/shard_map/ppermute | solution.py:499
  78.9 12.9 %all-to-all-start.3 = ((bf16[16,3,30,128]{3,2,1,0:T(8,128)(2,1)}), bf16[16,3,30,128]{3,2,1,0:T(8,128)(2,1)S(1)}, u32[]{:S(2)}, u32[]{:S(2)}) async-start(bf16[16,3,30,128]{3,2,1,0:T(8,128)(2,1)} %broadcast_in_dim.108), calls=%async_computation.3 | async-start | bytes 786432 | tf_op jit(solution)/shard_map/all_to_all | solution.py:435
  112.5 45.7 %copy-start.7 = (f32[3,256]{1,0:T(4,128)S(1)}, f32[3,256]{1,0:T(4,128)}, u32[]{:S(2)}) copy-start(f32[3,256]{1,0:T(4,128)} %get-tuple-element.55) | copy-start | bytes 9220
  112.5 46.3 %copy-start.6 = (f32[3,256]{1,0:T(4,128)S(1)}, f32[3,256]{1,0:T(4,128)}, u32[]{:S(2)}) copy-start(f32[3,256]{1,0:T(4,128)} %get-tuple-element.56) | copy-start | bytes 9220
  112.5 11.8 %all-to-all-start.4 = ((f32[16,48,128]{2,1,0:T(8,128)}), f32[16,48,128]{2,1,0:T(8,128)S(1)}, u32[]{:S(2)}, u32[]{:S(2)}) async-start(f32[16,48,128]{2,1,0:T(8,128)} %bitcast.91), calls=%async_computation.4 | async-start | bytes 786432 | tf_op jit(solution)/shard_map/all_to_all | solution.py:447
  154.7 10.4 %all-to-all-start.6 = ((f32[16,24,128]{2,1,0:T(8,128)}), f32[16,24,128]{2,1,0:T(8,128)S(1)}, u32[]{:S(2)}, u32[]{:S(2)}) async-start(f32[16,24,128]{2,1,0:T(8,128)} %broadcast_in_dim.113), calls=%async_computation.6 | async-start | bytes 393216 | tf_op jit(solution)/shard_map/all_to_all | solution.py:435

commit v4 on v3

--- a/solution.py
+++ b/solution.py
@@ -30,7 +30,7 @@
         return self.xs + 2 * halo
 
     def starts(self, planes):
-        count = -(-planes // 4)
+        count = -(-planes // 2)
         size = -(-planes // count)
         return size, [min(k * size, planes - size) for k in range(count)]
 
@@ -52,10 +52,10 @@
     c, zs, mids = plan.c, plan.zs, plan.layers - 1
     f32, bf16 = jnp.float32, jnp.bfloat16
 
-    def rolled(rows, out, step, planes):
+    def rolled(rows, out, step, planes, first=0):
         for k in range(planes):
             moved = rows if k == 0 else pltpu.roll(rows, k * step, 1)
-            out[k * c : (k + 1) * c, :] = moved.astype(bf16)
+            out[(first + k) * c : (first + k + 1) * c, :] = moved.astype(bf16)
 
     for weights, out, rows, lead, planes, mirrored in (
         (w_in, w_first, plan.rows_in, plan.lead_in, plan.z(plan.halo_u[1]), False),
@@ -71,13 +71,13 @@
         )
         rolled(base, out, 1, planes)
 
-    def spread(tile, planes, width):
+    def spread(tile, taps, planes, width):
         pieces = []
-        for k in range(9):
+        for k in taps:
             pieces += [tile(0, k), tile(1, k), tile(2, k)]
             lines = pieces[0].shape[0]
             pieces.append(jnp.zeros((lines, (planes - 3) * c), f32))
-        rest = width - 9 * planes * c
+        rest = width - len(taps) * planes * c
         if rest:
             pieces.append(jnp.zeros((lines, rest), f32))
         return jnp.concatenate(pieces, axis=1)
@@ -89,7 +89,7 @@
             tap = 26 - dz * 9 - k if mirrored else dz * 9 + k
             return lines[tap : tap + 1, :]
 
-        rows = jnp.broadcast_to(spread(row, zs + 2, out.shape[1]), out.shape)
+        rows = jnp.broadcast_to(spread(row, range(9), zs + 2, out.shape[1]), out.shape)
         line = lax.broadcasted_iota(jnp.int32, rows.shape, 0)
         total = jnp.where(line == 0, rows, 0.0)
         for k in range(1, zs):
@@ -104,8 +104,10 @@
                 return w_mid[first + 26 - dz * 9 - k].astype(f32).T
             return w_mid[first + dz * 9 + k].astype(f32)
 
-        size = out.shape[0] // c
-        rolled(spread(tile, size + 2, out.shape[1]), out, c, size)
+        size = out.shape[0] // (3 * c)
+        for dx in range(3):
+            rows = spread(tile, range(dx * 3, dx * 3 + 3), size + 2, out.shape[1])
+            rolled(rows, out, c, size, dx * size)
 
 
 def inside(first, count, c, bound):
@@ -114,7 +116,7 @@
     return jnp.logical_and(plane >= 0, plane < bound)
 
 
-def network_kernel(plan, grid, pos, u_first, c_last, em_own, cot_own, w_first, w_top, w_out, w_back, *refs):
+def network_kernel(plan, grid, pos, received, em_own, cot_own, w_first, w_top, w_out, w_back, *refs):
     layers, c, zs, xs = plan.layers, plan.c, plan.zs, plan.xs
     mids = layers - 1
     w_fwd, w_bwd = refs[:mids], refs[mids : 2 * mids]
@@ -127,13 +129,23 @@
     z_first, x_first = pos[0], pos[1]
     f32, bf16 = jnp.float32, jnp.bfloat16
 
-    for source, target, count in (
-        (u_first, first_sh, plan.x(plan.halo_in)),
-        (c_last, last_sh, plan.x(plan.halo_last)),
+    wide = plan.x(plan.halo_in)
+    for target, gathered, halo, lead, first_row in (
+        (first_sh, scratch[-2], plan.halo_in, plan.lead_in, 0),
+        (last_sh, scratch[-1], plan.halo_last, plan.lead_last, wide),
     ):
-        for k in range(count):
-            span = slice(k * LANES, (k + 1) * LANES)
-            for dy, rows in enumerate(shifts(source[:, span].astype(f32))):
+        gathered[...] = jnp.zeros(gathered.shape, f32)
+        for k in range(plan.z(halo)):
+            plane = z_first - halo + k
+            inner = jnp.logical_and(plane >= 0, plane < grid[0])
+            rows = received[jnp.clip(plane, 0, grid[0] - 1)].astype(f32)
+            rows = jnp.where(inner, rows, 0.0)
+            for x in range(plan.x(halo)):
+                span = slice(x * LANES, (x + 1) * LANES)
+                gathered[lead + k : lead + k + 1, span] = rows[first_row + x : first_row + x + 1, :]
+        for x in range(plan.x(halo)):
+            span = slice(x * LANES, (x + 1) * LANES)
+            for dy, rows in enumerate(shifts(gathered[:, span])):
                 target[dy, :, span] = rows
 
     def store_shifted(target, value, rows, lane, x_at, keep):
@@ -151,15 +163,21 @@
         stacked = jnp.concatenate(pieces, axis=0).astype(bf16)
         return jnp.dot(weight[:, : stacked.shape[0]], stacked, preferred_element_type=f32)
 
-    def many_channels(source, weight, first_plane, planes, lane):
+    def many_channels(source, weight, first_plane, planes, count):
         rows = slice(first_plane * c, (first_plane + planes + 2) * c)
-        pieces = [
-            source[dy, rows, lane + dx * LANES : lane + (dx + 2) * LANES]
-            for dx in range(3)
-            for dy in range(3)
-        ]
-        stacked = jnp.concatenate(pieces, axis=0)
-        return jnp.dot(weight[:, : stacked.shape[0]], stacked, preferred_element_type=f32)
+        lines = planes * c
+
+        def product(pair):
+            span = slice(pair * 2 * LANES, (pair + 1) * 2 * LANES)
+            stacked = jnp.concatenate([source[dy, rows, span] for dy in range(3)], axis=0)
+            return jnp.dot(weight[:, : stacked.shape[0]], stacked, preferred_element_type=f32)
+
+        left = product(0)
+        for pair in range(count):
+            right = product(pair + 1)
+            middle = [left[lines : 2 * lines, LANES:], right[lines : 2 * lines, :LANES]]
+            yield left[:lines] + jnp.concatenate(middle, axis=1) + right[2 * lines :]
+            left = right
 
     def forward_tail(value, layer, first_plane, planes, pair, lane):
         halo = plan.halo_u[layer]
@@ -184,27 +202,19 @@
             c_sh[layer - 1], slope * value, rows, lane, x_first - halo + 2 * pair, keep
         )
 
-    def over_pairs(count, body):
-        for pair in range(count):
-            body(pair, pair * 2 * LANES)
-
     halo = plan.halo_u[1]
-
-    def first_layer(pair, lane):
-        value = one_channel(first_sh, w_first, lane)
-        forward_tail(value, 1, 0, plan.z(halo), pair, lane)
-
-    over_pairs(plan.x(halo) // 2, first_layer)
+    for pair in range(plan.x(halo) // 2):
+        lane = pair * 2 * LANES
+        forward_tail(one_channel(first_sh, w_first, lane), 1, 0, plan.z(halo), pair, lane)
     for layer in range(2, layers + 1):
         halo = plan.halo_u[layer]
         size, starts = plan.starts(plan.z(halo))
         for start in starts:
-
-            def middle(pair, lane, layer=layer, size=size, start=start):
-                value = many_channels(u_sh[layer - 2], w_fwd[layer - 2], start, size, lane)
-                forward_tail(value, layer, start, size, pair, lane)
-
-            over_pairs(plan.x(halo) // 2, middle)
+            values = many_channels(
+                u_sh[layer - 2], w_fwd[layer - 2], start, size, plan.x(halo) // 2
+            )
+            for pair, value in enumerate(values):
+                forward_tail(value, layer, start, size, pair, pair * 2 * LANES)
 
     def own_taps(source, halo):
         rows = slice((halo - 1) * c, (halo + zs + 1) * c)
@@ -222,21 +232,16 @@
 
     halo = plan.halo_c[-1]
 
-    def top_layer(pair, lane):
-        value = one_channel(last_sh, w_top, lane)
-        backward_tail(value, layers, 0, plan.z(halo), pair, lane)
-
-    over_pairs(plan.x(halo) // 2, top_layer)
+    for pair in range(plan.x(halo) // 2):
+        lane = pair * 2 * LANES
+        backward_tail(one_channel(last_sh, w_top, lane), layers, 0, plan.z(halo), pair, lane)
     for layer in range(layers - 1, 0, -1):
         halo = plan.halo_c[layer - 1]
         size, starts = plan.starts(plan.z(halo))
         for start in starts:
-
-            def middle_back(pair, lane, layer=layer, size=size, start=start):
-                value = many_channels(c_sh[layer], w_bwd[layer - 1], start, size, lane)
-                backward_tail(value, layer, start, size, pair, lane)
-
-            over_pairs(plan.x(halo) // 2, middle_back)
+            values = many_channels(c_sh[layer], w_bwd[layer - 1], start, size, plan.x(halo) // 2)
+            for pair, value in enumerate(values):
+                backward_tail(value, layer, start, size, pair, pair * 2 * LANES)
     taps = own_taps(c_sh[0], plan.halo_c[0])
     down = jnp.dot(w_back[:, : taps.shape[0]], taps, preferred_element_type=f32)
     em_grad[...] = cot_own[...] + down[:zs, :]
@@ -313,7 +318,7 @@
 
     def banded(halo):
         size, _ = plan.starts(plan.z(halo))
-        return (size * c, round_up(9 * (size + 2) * c, LANES))
+        return (3 * size * c, round_up(3 * (size + 2) * c, LANES))
 
     last = (8, round_up(9 * (plan.zs + 2) * c, LANES))
     shapes = [
@@ -339,7 +344,7 @@
     )
 
 
-def network(plan, grid, z_first, x_first, u_first, c_last, em_own, cot_own, weights, packed_rows):
+def network(plan, grid, position, received, em_own, cot_own, weights, packed_rows):
     layers, c = plan.layers, plan.c
     f32, bf16 = jnp.float32, jnp.bfloat16
     own = jax.ShapeDtypeStruct((plan.zs, plan.xs * LANES), f32)
@@ -355,8 +360,11 @@
     scratch += [pltpu.VMEM(region(plan.halo_u[l]), f32) for l in range(1, layers + 1)]
     scratch += [pltpu.VMEM(region(plan.halo_c[l - 1], (3,)), bf16) for l in range(1, layers + 1)]
     vmem = pl.BlockSpec(memory_space=pltpu.VMEM)
-    position = jnp.stack([z_first, x_first]).astype(jnp.int32)
-    operands = (position, u_first, c_last, em_own, cot_own, *weights)
+    scratch += [
+        pltpu.VMEM((plan.rows_in, plan.x(plan.halo_in) * LANES), f32),
+        pltpu.VMEM((plan.rows_last, plan.x(plan.halo_last) * LANES), f32),
+    ]
+    operands = (position, received, em_own, cot_own, *weights)
     return pl.pallas_call(
         lambda *refs: network_kernel(plan, grid, *refs),
         out_shape=[own, own, jax.ShapeDtypeStruct((packed_rows, LANES), f32)],
@@ -366,6 +374,60 @@
         compiler_params=pltpu.CompilerParams(vmem_limit_bytes=VMEM_BYTES),
         name="network",
     )(*operands)
+
+
+def image_kernel(plan, grid, copies, pos, parts, sent, em_own, cot_own):
+    zs, xs, halo, outer = plan.zs, plan.xs, plan.halo_in, plan.halo_last
+    reach = -(-halo // (xs * CORES))
+    span = (2 * reach + 1) * CORES * xs
+    x_first = pos[1]
+    core = lax.rem(lax.div(x_first, xs), CORES)
+    row = x_first - (core + reach * CORES) * xs + lax.broadcasted_iota(jnp.int32, (span, LANES), 0)
+    good = jnp.logical_and(row >= 0, row < grid[1])
+
+    def near(field, z):
+        pieces = []
+        for chip in range(2 * reach + 1):
+            at = zs * span + (chip * 3 + field) * zs * xs + z * xs
+            pieces += [parts[k, at : at + xs, :] for k in range(CORES)]
+        return jnp.concatenate(pieces, axis=0)
+
+    def window(rows, halo):
+        first = reach * CORES * xs - halo
+        count = xs + 2 * halo
+        taken = rows[first : first + count]
+        for k in range(1, CORES):
+            taken = jnp.where(core == k, rows[first + k * xs : first + k * xs + count], taken)
+        return taken
+
+    for z in range(zs):
+        back = parts[0, z * span : (z + 1) * span, :]
+        for k in range(1, CORES):
+            back = back + parts[k, z * span : (z + 1) * span, :]
+        em = window(jnp.where(good, near(0, z) * back / near(1, z), 0.0), halo)
+        cot = window(jnp.where(good, near(2, z), 0.0), outer)
+        both = jnp.concatenate([em, cot], axis=0).astype(jnp.bfloat16)
+        for k in range(copies):
+            sent[k, z] = both
+        for x in range(xs):
+            lanes = slice(x * LANES, (x + 1) * LANES)
+            em_own[z : z + 1, lanes] = em[halo + x : halo + x + 1, :]
+            cot_own[z : z + 1, lanes] = cot[outer + x : outer + x + 1, :]
+
+
+def image_and_halo(plan, grid, copies, position, parts):
+    f32 = jnp.float32
+    rows = plan.x(plan.halo_in) + plan.x(plan.halo_last)
+    own = jax.ShapeDtypeStruct((plan.zs, plan.xs * LANES), f32)
+    vmem = pl.BlockSpec(memory_space=pltpu.VMEM)
+    return pl.pallas_call(
+        lambda *refs: image_kernel(plan, grid, copies, *refs),
+        out_shape=[jax.ShapeDtypeStruct((copies, plan.zs, rows, LANES), jnp.bfloat16), own, own],
+        in_specs=[pl.BlockSpec(memory_space=pltpu.SMEM), vmem],
+        out_specs=[vmem] * 3,
+        compiler_params=pltpu.CompilerParams(vmem_limit_bytes=VMEM_BYTES),
+        name="image_and_halo",
+    )(position, parts)
 
 
 def grad_rows(plan):
@@ -439,7 +501,7 @@
     return lax.all_gather(value, "sector", axis_index_groups=within_chip("sector"))
 
 
-def summed_everywhere(packed, slabs):
+def summed_everywhere(packed, slabs, beside):
     chips = along_chips("sector")
     core = lax.rem(lax.axis_index("sector"), CORES)
     share = packed.shape[0] // slabs
@@ -449,8 +511,9 @@
     own = both[0] + both[1]
     half = lax.dynamic_slice_in_dim(own, core * (share // CORES), share // CORES, 0)
     half = to_all(half.astype(jnp.bfloat16), "sector", chips)
+    half, beside = lax.optimization_barrier((half, beside))
     half = jnp.sum(half.astype(jnp.float32), axis=0)
-    return pair_gather(to_all(half, "slab"))
+    return pair_gather(to_all(half, "slab")), beside
 
 
 def shards(
@@ -505,6 +568,8 @@
     forward = forward * weight[:, None]
     lined = jnp.concatenate([forward, tile_rows[0].astype(f32)[:, None]], axis=1)
     lined = jnp.pad(lined, ((0, 0), (0, LANES - row_len - 1)))
+    lined, *kernels = lax.optimization_barrier((lined, w_in, w_mid, w_out))
+    weights = prepared_weights(plan, *kernels)
     every = to_all(lined, "slab").reshape(slabs * slots, LANES)
     every_rows = every[:, row_len]
     placing = (every_rows[None, :] == jnp.arange(line_blocks, dtype=f32)[:, None]).astype(f32)
@@ -513,10 +578,8 @@
 
     backward = jnp.einsum("krv,kr->kv", values, ratio[tile_rows[0]], preferred_element_type=f32)
     backward = backward * weight[:, None]
+    backward, weights = lax.optimization_barrier((backward, weights))
     every_back = to_all(backward, "sector", chips).reshape(-1, block_len)
-    weights = prepared_weights(plan, w_in, w_mid, w_out)
-    every_back, weights = lax.optimization_barrier((every_back, weights))
-    halo = plan.halo_in
     core = lax.rem(sector, CORES)
     span = (2 * reach + 1) * CORES
     near = sector - core - reach * CORES + jnp.arange(span)
@@ -526,53 +589,29 @@
     owning = (every_cols[None, :] == wanted[:, None]).astype(f32)
     of_core = jnp.dot(owning, every_back, precision=highest).reshape(-1, ys)
     of_cores = pair_gather(jnp.concatenate([of_core, near_fields], axis=0))
-    back = of_cores[:, : of_core.shape[0]]
-    back = (back[0] + back[1]).reshape(zs, span * xs, ys)
-    near_fields = of_cores[:, of_core.shape[0] :].reshape(CORES, 2 * reach + 1, 3, zs, xs, ys)
-    near_fields = jnp.transpose(near_fields, (2, 3, 1, 0, 4, 5)).reshape(3, zs, span * xs, ys)
-    row = (sector - core - reach * CORES) * xs + jnp.arange(span * xs)
-    good = jnp.logical_and(row >= 0, row < grid[1])[None, :, None]
-    em = jnp.where(good, near_fields[0] * back / near_fields[1], 0.0)
-    cot_near = jnp.where(good, near_fields[2], 0.0)
-
-    def window(field, halo):
-        return lax.dynamic_slice_in_dim(field, (core + reach * CORES) * xs - halo, xs + 2 * halo, 1)
-
-    em_own = window(em, 0)
-
-    both = [window(em, halo).astype(bf16), window(cot_near, plan.halo_last).astype(bf16)]
-    both = jnp.concatenate(both, axis=1)
-    every_plane = to_all(both, "slab").reshape(zs * slabs, both.shape[1], ys)
-
-    def planes(lo, count, halo, lead, rows):
-        field = every_plane[:, lo : lo + count]
-        padded = jnp.pad(field, ((halo + lead, rows), (0, 0), (0, 0)))
-        taken = lax.dynamic_slice_in_dim(padded, slab * zs, rows, 0)
-        line = jnp.arange(rows)[:, None, None]
-        taken = jnp.where(jnp.logical_and(line >= lead, line < lead + plan.z(halo)), taken, 0)
-        return taken.reshape(rows, count * ys)
-
-    wide = plan.x(halo)
-    u_first = planes(0, wide, halo, plan.lead_in, plan.rows_in)
-    c_last = planes(wide, plan.x(plan.halo_last), plan.halo_last, plan.lead_last, plan.rows_last)
+    position = jnp.stack([slab * zs, sector * xs]).astype(jnp.int32)
+    to_send, em_own, cot_own = image_and_halo(plan, grid, slabs, position, of_cores)
+
+    received = lax.all_to_all(to_send, "slab", 0, 0, tiled=True)
+    received = received.reshape(zs * slabs, *received.shape[2:])
     new_image, em_grad, packed = network(
         plan,
         grid,
-        slab * zs,
-        sector * xs,
-        u_first,
-        c_last,
-        em_own.reshape(zs, xs * ys),
-        cotangent.reshape(zs, xs * ys),
+        position,
+        received,
+        em_own,
+        cot_own,
         weights,
         round_up(grad_rows(plan), slabs * CORES * 8),
     )
-    halves = summed_everywhere(packed, slabs)
+    new_image = new_image.reshape(zs, xs, ys)
+    em_grad = em_grad.reshape(zs, xs, ys)
+    halves, new_image = summed_everywhere(packed, slabs, new_image)
     factor = 1.0 / math.sqrt(grid[0] * grid[1] * ys)
     grad_in, grad_mid, grad_out = unpack_grads(plan, halves, factor)
     return (
-        new_image.reshape(zs, xs, ys),
-        em_grad.reshape(zs, xs, ys),
+        new_image,
+        em_grad,
         grad_in,
         grad_mid,
         grad_out,

time: 174 us -> 170 us (0.977)
  blocking collectives: 44.1 us -> 37 us
  starting transfers between devices: 48.4 us -> 54.6 us
  local copies, waits for them, and re-layouts: 11.8 us -> 8.83 us
    all_to_all x1, blocking collectives: 25.5 us -> 15 us  [shards(): received = lax.all_to_all(to_send, 'slab', 0, 0, tiled=True)]
    all_to_all x5, starting transfers between devices: 33.3 us -> 39.5 us  [to_all(): lax.all_to_all(copies, axis, 0, 0, tiled=True, axis_index_groups=groups)]
    all_gather x4, blocking collectives: 18.6 us -> 22 us  [pair_gather(): lax.all_gather(value, 'sector', axis_index_groups=within_chip('sector'))]
    unnamed x25 -> x20, local copies, waits for them, and re-layouts: 2.58 us -> 0.06 us
    broadcast_in_dim x6 -> x5, local copies, waits for them, and re-layouts: 3.55 us -> 3.4 us  [to_all(): copies = jnp.broadcast_to(value[None], (count, *value.shape))]
  transfers between devices with their start and end apart: 10 -> 10, of which waited for: 6 -> 6; matrix products, arithmetic and copies ran while one was open for 4% -> 4% of each run, Pallas kernels for 2% -> 3%
where the time goes in v4:
time: 170 us; the launch traced here: 169 us
  starting transfers between devices  54.6 us (32%)
  blocking collectives  37 us (22%)
  waiting for transfers between devices  34.8 us (20%)
  Pallas kernels  27 us (16%)
  local copies, waits for them, and re-layouts  8.83 us (5%)
  other arithmetic  4.4 us (3%)
    all_to_all x5, starting transfers between devices, to_all(): lax.all_to_all(copies, axis, 0, 0, tiled=True, axis_index_groups=groups)  39.5 us
    all_to_all x5, waiting for transfers between devices, to_all(): lax.all_to_all(copies, axis, 0, 0, tiled=True, axis_index_groups=groups)  26.8 us
    all_gather x4, blocking collectives, pair_gather(): lax.all_gather(value, 'sector', axis_index_groups=within_chip('sector'))  22 us
    pallas_call x1, Pallas kernels, network(): pl.pallas_call(lambda *refs: network_kernel(plan, grid, *refs), out_shape...  18.2 us
    all_to_all x1, blocking collectives, shards(): received = lax.all_to_all(to_send, 'slab', 0, 0, tiled=True)  15 us
    ppermute x4, starting transfers between devices, shards(): lax.ppermute(fields, 'sector', pairs)  11.5 us
    all_to_all x1, waiting for transfers between devices, summed_everywhere(): own = jnp.sum(lax.all_to_all(parts, 'slab', 0, 0, tiled=True), axis=0)  8 us
    pallas_call x1, Pallas kernels, prepared_weights(): pl.pallas_call(lambda *refs: prepare_kernel(plan, *refs), out_shape=[jax....  4.63 us
  transfers between devices with their start and end apart: 10, of which 6 were waited for; matrix products, arithmetic and copies ran while one was open for 4% of the time, Pallas kernels for 3%

profile of v4, /device:TPU:1, one launch (start us, length us, event | category | flops | bytes accessed | tf_op | source)
XLA Modules:
  0.0 169.0 jit_solution(7629012482318347819)
XLA Ops:
  0.7 0.7 convert_element_type.57
  1.4 0.7 convert_element_type.56
  2.1 0.6 broadcast_in_dim.18
  2.7 15.7 %all-to-all-start = ((bf16[16,8,128]{2,1,0:T(8,128)(2,1)}), bf16[16,8,128]{2,1,0:T(8,128)(2,1)S(1)}, u32[]{:S(2)}, u32[]{:S(2)}) async-start(bf16[16,8,128]{2,1,0:T(8,128)(2,1)} %broadcast_in_dim.18), calls=%async_computation | async-start | bytes 65536 | tf_op jit(solution)/shard_map/all_to_all | solution.py:497
  18.5 0.7 fusion.19
  19.2 0.7 bitcast_convert_fusion
  19.8 0.7 fusion.18
  21.2 0.7 reshape.202
  22.0 8.0 %all-to-all-done = bf16[16,8,128]{2,1,0:T(8,128)(2,1)S(1)} async-done(((bf16[16,8,128]{2,1,0:T(8,128)(2,1)}), bf16[16,8,128]{2,1,0:T(8,128)(2,1)S(1)}, u32[]{:S(2)}, u32[]{:S(2)}) %all-to-all-start) | async-done | bytes 32800 | tf_op jit(solution)/shard_map/all_to_all | solution.py:497
  30.0 3.5 %all-gather = bf16[32,6,128]{2,0,1:T(8,128)(2,1)S(1)} all-gather(bf16[16,6,128]{2,0,1:T(8,128)(2,1)S(1)} %copy.30), channel_id=2, replica_groups={{0,16},{32,48},{64,80},{96,112},{128,144},{160,176},{192,208},{224,240}..., dimensions={0}, use_global_device_ids=true | all-gather | bytes 73728 | tf_op jit(solution)/shard_map/all_gather | solution.py:501
  33.6 0.6 gather_fusion
  34.1 0.3 fusion.4
  34.6 0.7 broadcast_in_dim.21
  35.3 6.8 %all-to-all-start.1 = ((f32[16,12,128]{2,1,0:T(8,128)}), f32[16,12,128]{2,1,0:T(8,128)S(1)}, u32[]{:S(2)}, u32[]{:S(2)}) async-start(f32[16,12,128]{2,1,0:T(8,128)} %broadcast_in_dim.21), calls=%async_computation.1 | async-start | bytes 262144 | tf_op jit(solution)/shard_map/all_to_all | solution.py:497
  42.0 0.6 reshape.197.refs_0_
  42.7 0.6 reshape.199.refs_2_
  43.3 4.6 %prepare_weights.1 = (bf16[544,256]{1,0:T(8,128)(2,1)}, bf16[352,256]{1,0:T(8,128)(2,1)}, bf16[8,1536]{1,0:T(8,128)(2,1)}, bf16[8,1536]{1,0:T(8,128)(2,1)}, bf16...) custom-call(bf16[27,32]{1,0:T(8,128)(2,1)} %reshape.197.refs_0_, ...), custom_call_target="tpu_custom_call" | custom-call | tf_op jit(solution)/shard_map/prepare_weights/pallas_call | solution.py:333
  47.9 0.8 all-to-all-done.1
  48.9 0.2 fusion.1
  49.1 0.6 gather_fusion.1
  49.7 0.2 fusion.2
  50.0 0.7 broadcast_in_dim.22
  50.7 3.5 %all-to-all-start.2 = ((f32[16,12,256]{2,1,0:T(8,128)}), f32[16,12,256]{2,1,0:T(8,128)S(1)}, u32[]{:S(2)}, u32[]{:S(2)}) async-start(f32[16,12,256]{2,1,0:T(8,128)} %broadcast_in_dim.22), calls=%async_computation.2 | async-start | bytes 524288 | tf_op jit(solution)/shard_map/all_to_all | solution.py:497
  54.5 0.6 pad_add_fusion.refs_0_
  55.0 1.3 collective-permute-start.3
  56.3 1.3 collective-permute-start.2
  57.6 4.0 %collective-permute-start.1 = (f32[24,128]{1,0:T(8,128)S(1)}, f32[24,128]{1,0:T(8,128)S(1)}, u32[]{:S(2)}, u32[]{:S(2)}) collective-permute-start(f32[24,128]{1,0:T(8,128)S(1)} %select_maximum_fusion), channel_id=1, source_target_pairs={{0,32},{16,48},{32,64},{48,80},{64,96},{80,112},{96,128},{112,144}... | collective-permute-start | bytes 36872 | tf_op jit(solution)/shard_map/ppermute | solution.py:562
  61.6 4.9 %collective-permute-start = (f32[24,128]{1,0:T(8,128)S(1)}, f32[24,128]{1,0:T(8,128)S(1)}, u32[]{:S(2)}, u32[]{:S(2)}) collective-permute-start(f32[24,128]{1,0:T(8,128)S(1)} %select_maximum_fusion), channel_id=1, source_target_pairs={{0,64},{16,80},{32,96},{48,112},{64,128},{80,144},{96,160},{112,17... | collective-permute-start | bytes 36872 | tf_op jit(solution)/shard_map/ppermute | solution.py:562
  66.6 0.4 all-to-all-done.2
  67.1 0.2 fusion.7
  67.3 0.6 concatenate.15
  67.9 8.3 %all-gather.4.refs_1_ = f32[2,150,128]{2,1,0:T(8,128)} all-gather(f32[1,150,128]{2,1,0:T(8,128)S(1)} %bitcast.69), channel_id=3, replica_groups={{0,16},{32,48},{64,80},{96,112},{128,144},{160,176},{192,208},{224,240}..., dimensions={0}, use_global_device_ids=true | all-gather | bytes 230400 | tf_op jit(solution)/shard_map/all_gather | solution.py:501
  76.2 1.7 %image_and_halo.1 = (bf16[16,3,30,128]{3,2,1,0:T(8,128)(2,1)}, f32[3,256]{1,0:T(4,128)}, f32[3,256]{1,0:T(4,128)}) custom-call(s32[2]{0:T(128)} %pad_add_fusion.refs_0_, f32[2,150,128]{2,1,0:T(8,128)} %all-gather.4.refs_1_), custom_call_target="tpu_custom_call" | custom-call | tf_op jit(solution)/shard_map/image_and_halo/pallas_call | solution.py:423
  78.0 15.0 %all_to_all.35 = bf16[16,3,30,128]{3,2,1,0:T(8,128)(2,1)} all-to-all(bf16[16,3,30,128]{3,2,1,0:T(8,128)(2,1)} %get-tuple-element.58), channel_id=1, replica_groups=mesh['sector'=32,'slab'=16] {'slab'}, dimensions={0} | all-to-all | bytes 737280 | tf_op jit(solution)/shard_map/all_to_all | solution.py:595
  92.9 18.2 %network.1 = (f32[3,256]{1,0:T(4,128)}, f32[3,256]{1,0:T(4,128)}, f32[768,128]{1,0:T(8,128)}) custom-call(s32[2]{0:T(128)} %pad_add_fusion.refs_0_, bf16[48,30,128]{2,1,0:T(8,128)(2,1)} %bitcast.66, f32[3,256]{1,0:T(4,128)} %get-tuple-element.59.refs_2_, f32[3,256]{1,0:T(4,128)} %get-tuple-element.60.refs_3_, bf16[544,256]{1,0:T(8,128)(2,1)} %get-tuple-element.61.refs_4_, ...), custom_call_target="tpu_custom_call" | custom-call | tf_op jit(solution)/shard_map/network/pallas_call | solution.py:368
  111.2 3.6 %all-to-all-start.4 = ((f32[16,48,128]{2,1,0:T(8,128)}), f32[16,48,128]{2,1,0:T(8,128)S(1)}, u32[]{:S(2)}, u32[]{:S(2)}) async-start(f32[16,48,128]{2,1,0:T(8,128)} %bitcast.68), calls=%async_computation.4 | async-start | bytes 786432 | tf_op jit(solution)/shard_map/all_to_all | solution.py:509
  114.7 8.0 %all-to-all-done.4 = f32[16,48,128]{2,1,0:T(8,128)S(1)} async-done(((f32[16,48,128]{2,1,0:T(8,128)}), f32[16,48,128]{2,1,0:T(8,128)S(1)}, u32[]{:S(2)}, u32[]{:S(2)}) %all-to-all-start.4) | async-done | bytes 393248 | tf_op jit(solution)/shard_map/all_to_all | solution.py:509
  122.8 4.3 %all-gather.2 = f32[96,128]{1,0:T(8,128)S(1)} all-gather(f32[48,128]{1,0:T(8,128)S(1)} %reduce_sum.18), channel_id=4, replica_groups={{0,16},{32,48},{64,80},{96,112},{128,144},{160,176},{192,208},{224,240}..., dimensions={0}, use_global_device_ids=true | all-gather | bytes 73728 | tf_op jit(solution)/shard_map/all_gather | solution.py:501
  127.1 0.7 broadcast_in_dim.23
  127.7 10.0 %all-to-all-start.5 = ((bf16[16,24,128]{2,1,0:T(8,128)(2,1)}), bf16[16,24,128]{2,1,0:T(8,128)(2,1)S(1)}, u32[]{:S(2)}, u32[]{:S(2)}) async-start(bf16[16,24,128]{2,1,0:T(8,128)(2,1)} %broadcast_in_dim.23), calls=%async_computation.5 | async-start | bytes 196608 | tf_op jit(solution)/shard_map/all_to_all | solution.py:497
  137.7 0.6 reshape.207
  138.3 11.3 %all-to-all-done.5 = bf16[16,24,128]{2,1,0:T(8,128)(2,1)S(1)} async-done(((bf16[16,24,128]{2,1,0:T(8,128)(2,1)}), bf16[16,24,128]{2,1,0:T(8,128)(2,1)S(1)}, u32[]{:S(2)}, u32[]{:S(2)}) %all-to-all-start.5) | async-done | bytes 98336 | tf_op jit(solution)/shard_map/all_to_all | solution.py:497
  149.6 0.7 broadcast_in_dim.24
  150.3 3.5 %all-to-all-start.6 = ((f32[16,24,128]{2,1,0:T(8,128)}), f32[16,24,128]{2,1,0:T(8,128)S(1)}, u32[]{:S(2)}, u32[]{:S(2)}) async-start(f32[16,24,128]{2,1,0:T(8,128)} %broadcast_in_dim.24), calls=%async_computation.6 | async-start | bytes 393216 | tf_op jit(solution)/shard_map/all_to_all | solution.py:497
  153.9 0.6 reshape.208
  154.5 6.3 %all-to-all-done.6 = f32[16,24,128]{2,1,0:T(8,128)S(1)} async-done(((f32[16,24,128]{2,1,0:T(8,128)}), f32[16,24,128]{2,1,0:T(8,128)S(1)}, u32[]{:S(2)}, u32[]{:S(2)}) %all-to-all-start.6) | async-done | bytes 196640 | tf_op jit(solution)/shard_map/all_to_all | solution.py:497
  160.8 5.9 %all-gather.3 = f32[32,24,128]{2,1,0:T(8,128)} all-gather(f32[16,24,128]{2,1,0:T(8,128)S(1)} %all-to-all-done.6), channel_id=5, replica_groups={{0,16},{32,48},{64,80},{96,112},{128,144},{160,176},{192,208},{224,240}..., dimensions={0}, use_global_device_ids=true | all-gather | bytes 589824 | tf_op jit(solution)/shard_map/all_gather | solution.py:501
  166.6 2.4 %unpack_gradients.1 = (f32[27,1,32]{2,1,0:T(1,128)}, f32[81,32,32]{2,1,0:T(8,128)}, f32[27,1,32]{2,1,0:T(1,128)}) custom-call(f32[2,16,24,128]{3,2,1,0:T(8,128)} %bitcast.65), custom_call_target="tpu_custom_call" | custom-call | tf_op jit(solution)/shard_map/unpack_gradients/pallas_call | solution.py:467
  (52 shorter events, 1.1 us)
Async XLA Ops:
  0.6 33.5 %copy-start = (bf16[1,12,104,256]{3,2,1,0:T(8,128)(2,1)S(1)}, bf16[1,12,104,256]{3,2,1,0:T(8,128)(2,1)}, u32[]{:S(2)}) copy-start(bf16[1,12,104,256]{3,2,1,0:T(8,128)(2,1)} %param.14) | copy-start | bytes 1916932
  0.6 42.0 %copy-start.4 = (bf16[1,32,3,3,3]{1,4,3,2,0:T(4,128)(2,1)S(1)}, bf16[1,32,3,3,3]{1,4,3,2,0:T(4,128)(2,1)}, u32[]{:S(2)}) copy-start(bf16[1,32,3,3,3]{1,4,3,2,0:T(4,128)(2,1)} %param.22) | copy-start | bytes 5188
  0.7 41.4 %copy-start.3 = (bf16[32,1,3,3,3]{0,4,3,2,1:T(4,128)(2,1)S(1)}, bf16[32,1,3,3,3]{0,4,3,2,1:T(4,128)(2,1)}, u32[]{:S(2)}) copy-start(bf16[32,1,3,3,3]{0,4,3,2,1:T(4,128)(2,1)} %param.20) | copy-start | bytes 5188
  2.7 27.2 %all-to-all-start = ((bf16[16,8,128]{2,1,0:T(8,128)(2,1)}), bf16[16,8,128]{2,1,0:T(8,128)(2,1)S(1)}, u32[]{:S(2)}, u32[]{:S(2)}) async-start(bf16[16,8,128]{2,1,0:T(8,128)(2,1)} %broadcast_in_dim.18), calls=%async_computation | async-start | bytes 65536 | tf_op jit(solution)/shard_map/all_to_all | solution.py:497
  18.5 30.4 %copy-start.1 = (f32[1,32,104]{2,1,0:T(8,128)S(1)}, f32[1,32,104]{2,1,0:T(8,128)}, u32[]{:S(2)}) copy-start(f32[1,32,104]{2,1,0:T(8,128)} %param.19) | copy-start | bytes 39940
  18.5 30.4 %copy-start.2 = (f32[1,32,104]{2,1,0:T(8,128)S(1)}, f32[1,32,104]{2,1,0:T(8,128)}, u32[]{:S(2)}) copy-start(f32[1,32,104]{2,1,0:T(8,128)} %param.18) | copy-start | bytes 39940
  35.3 13.5 %all-to-all-start.1 = ((f32[16,12,128]{2,1,0:T(8,128)}), f32[16,12,128]{2,1,0:T(8,128)S(1)}, u32[]{:S(2)}, u32[]{:S(2)}) async-start(f32[16,12,128]{2,1,0:T(8,128)} %broadcast_in_dim.21), calls=%async_computation.1 | async-start | bytes 262144 | tf_op jit(solution)/shard_map/all_to_all | solution.py:497
  43.3 11.1 %copy-start.7 = (f32[3,2,128]{2,1,0:T(2,128)S(1)}, f32[3,2,128]{2,1,0:T(2,128)}, u32[]{:S(2)}) copy-start(f32[3,2,128]{2,1,0:T(2,128)} %param.13) | copy-start | bytes 9220
  43.3 11.2 %copy-start.8 = (f32[3,2,128]{2,1,0:T(2,128)S(1)}, f32[3,2,128]{2,1,0:T(2,128)}, u32[]{:S(2)}) copy-start(f32[3,2,128]{2,1,0:T(2,128)} %param.23) | copy-start | bytes 9220
  50.7 16.3 %all-to-all-start.2 = ((f32[16,12,256]{2,1,0:T(8,128)}), f32[16,12,256]{2,1,0:T(8,128)S(1)}, u32[]{:S(2)}, u32[]{:S(2)}) async-start(f32[16,12,256]{2,1,0:T(8,128)} %broadcast_in_dim.22), calls=%async_computation.2 | async-start | bytes 524288 | tf_op jit(solution)/shard_map/all_to_all | solution.py:497
  55.0 12.3 %collective-permute-start.3 = (f32[24,128]{1,0:T(8,128)S(1)}, f32[24,128]{1,0:T(8,128)S(1)}, u32[]{:S(2)}, u32[]{:S(2)}) collective-permute-start(f32[24,128]{1,0:T(8,128)S(1)} %select_maximum_fusion), channel_id=1, source_target_pairs={{64,0},{80,16},{96,32},{112,48},{128,64},{144,80},{160,96},{176,11... | collective-permute-start | bytes 36872 | tf_op jit(solution)/shard_map/ppermute | solution.py:562
  56.3 11.0 %collective-permute-start.2 = (f32[24,128]{1,0:T(8,128)S(1)}, f32[24,128]{1,0:T(8,128)S(1)}, u32[]{:S(2)}, u32[]{:S(2)}) collective-permute-start(f32[24,128]{1,0:T(8,128)S(1)} %select_maximum_fusion), channel_id=1, source_target_pairs={{32,0},{48,16},{64,32},{80,48},{96,64},{112,80},{128,96},{144,112}... | collective-permute-start | bytes 36872 | tf_op jit(solution)/shard_map/ppermute | solution.py:562
  57.6 9.7 %collective-permute-start.1 = (f32[24,128]{1,0:T(8,128)S(1)}, f32[24,128]{1,0:T(8,128)S(1)}, u32[]{:S(2)}, u32[]{:S(2)}) collective-permute-start(f32[24,128]{1,0:T(8,128)S(1)} %select_maximum_fusion), channel_id=1, source_target_pairs={{0,32},{16,48},{32,64},{48,80},{64,96},{80,112},{96,128},{112,144}... | collective-permute-start | bytes 36872 | tf_op jit(solution)/shard_map/ppermute | solution.py:562
  61.6 5.7 %collective-permute-start = (f32[24,128]{1,0:T(8,128)S(1)}, f32[24,128]{1,0:T(8,128)S(1)}, u32[]{:S(2)}, u32[]{:S(2)}) collective-permute-start(f32[24,128]{1,0:T(8,128)S(1)} %select_maximum_fusion), channel_id=1, source_target_pairs={{0,64},{16,80},{32,96},{48,112},{64,128},{80,144},{96,160},{112,17... | collective-permute-start | bytes 36872 | tf_op jit(solution)/shard_map/ppermute | solution.py:562
  111.2 26.6 %copy-start.6 = (f32[3,256]{1,0:T(4,128)S(1)}, f32[3,256]{1,0:T(4,128)}, u32[]{:S(2)}) copy-start(f32[3,256]{1,0:T(4,128)} %get-tuple-element.72) | copy-start | bytes 9220
  111.2 42.7 %copy-start.5 = (f32[3,256]{1,0:T(4,128)S(1)}, f32[3,256]{1,0:T(4,128)}, u32[]{:S(2)}) copy-start(f32[3,256]{1,0:T(4,128)} %get-tuple-element.74) | copy-start | bytes 9220
  111.2 11.6 %all-to-all-start.4 = ((f32[16,48,128]{2,1,0:T(8,128)}), f32[16,48,128]{2,1,0:T(8,128)S(1)}, u32[]{:S(2)}, u32[]{:S(2)}) async-start(f32[16,48,128]{2,1,0:T(8,128)} %bitcast.68), calls=%async_computation.4 | async-start | bytes 786432 | tf_op jit(solution)/shard_map/all_to_all | solution.py:509
  127.7 21.9 %all-to-all-start.5 = ((bf16[16,24,128]{2,1,0:T(8,128)(2,1)}), bf16[16,24,128]{2,1,0:T(8,128)(2,1)S(1)}, u32[]{:S(2)}, u32[]{:S(2)}) async-start(bf16[16,24,128]{2,1,0:T(8,128)(2,1)} %broadcast_in_dim.23), calls=%async_computation.5 | async-start | bytes 196608 | tf_op jit(solution)/shard_map/all_to_all | solution.py:497
  150.3 10.4 %all-to-all-start.6 = ((f32[16,24,128]{2,1,0:T(8,128)}), f32[16,24,128]{2,1,0:T(8,128)S(1)}, u32[]{:S(2)}, u32[]{:S(2)}) async-start(f32[16,24,128]{2,1,0:T(8,128)} %broadcast_in_dim.24), calls=%async_computation.6 | async-start | bytes 393216 | tf_op jit(solution)/shard_map/all_to_all | solution.py:497

commit v5 on v4

--- a/solution.py
+++ b/solution.py
@@ -8,7 +8,8 @@
 from jax.sharding import PartitionSpec as P
 
 LANES = 128
-VMEM_BYTES = 56 * 1024 * 1024
+VMEM_BYTES = 36 * 1024 * 1024
+SMALL_VMEM_BYTES = 12 * 1024 * 1024
 
 
 class Plan:
@@ -41,8 +42,8 @@
 
 def shifts(rows):
     lane = lax.broadcasted_iota(jnp.int32, rows.shape, 1)
-    low = jnp.where(lane == 0, 0.0, pltpu.roll(rows, 1, 1))
-    high = jnp.where(lane == LANES - 1, 0.0, pltpu.roll(rows, LANES - 1, 1))
+    low = jnp.where(lane == 0, jnp.zeros_like(rows), pltpu.roll(rows, 1, 1))
+    high = jnp.where(lane == LANES - 1, jnp.zeros_like(rows), pltpu.roll(rows, LANES - 1, 1))
     return low, rows, high
 
 
@@ -152,9 +153,9 @@
         for half in range(2):
             part = value[:, half * LANES : (half + 1) * LANES]
             good = jnp.logical_and(x_at + half >= 0, x_at + half < grid[1])
-            part = jnp.where(jnp.logical_and(keep, good), part, 0.0)
+            part = jnp.where(jnp.logical_and(keep, good), part, 0.0).astype(bf16)
             for dy, moved in enumerate(shifts(part)):
-                target[dy, rows, lane + half * LANES : lane + (half + 1) * LANES] = moved.astype(bf16)
+                target[dy, rows, lane + half * LANES : lane + (half + 1) * LANES] = moved
 
     def one_channel(source, weight, lane):
         pieces = [
@@ -182,19 +183,21 @@
     def forward_tail(value, layer, first_plane, planes, pair, lane):
         halo = plan.halo_u[layer]
         rows = slice(first_plane * c, (first_plane + planes) * c)
-        pre[layer - 1][rows, lane : lane + 2 * LANES] = value
+        near = plan.halo_c[layer - 1]
+        edge = halo - near
+        low, high = max(first_plane, edge), min(first_plane + planes, edge + plan.z(near))
+        at = lane - edge * LANES
+        if low < high and 0 <= at < plan.x(near) * LANES:
+            kept = value[(low - first_plane) * c : (high - first_plane) * c]
+            pre[layer - 1][(low - edge) * c : (high - edge) * c, at : at + 2 * LANES] = kept
         act = value * jax.nn.sigmoid(value)
         keep = inside(z_first - halo + first_plane, planes, c, grid[0])
         store_shifted(u_sh[layer - 1], act, rows, lane, x_first - halo + 2 * pair, keep)
 
     def backward_tail(value, layer, first_plane, planes, pair, lane):
-        halo, halo_pre = plan.halo_c[layer - 1], plan.halo_u[layer]
+        halo = plan.halo_c[layer - 1]
         rows = slice(first_plane * c, (first_plane + planes) * c)
-        from_plane = first_plane + halo_pre - halo
-        preact = pre[layer - 1][
-            from_plane * c : (from_plane + planes) * c,
-            lane + (halo_pre - halo) * LANES : lane + (halo_pre - halo + 2) * LANES,
-        ]
+        preact = pre[layer - 1][rows, lane : lane + 2 * LANES]
         sigma = jax.nn.sigmoid(preact)
         slope = sigma * (1.0 + preact * (1.0 - sigma))
         keep = inside(z_first - halo + first_plane, planes, c, grid[0])
@@ -335,7 +338,7 @@
         out_shape=[jax.ShapeDtypeStruct(shape, bf16) for shape in shapes],
         in_specs=[vmem] * 3,
         out_specs=[vmem] * len(shapes),
-        compiler_params=pltpu.CompilerParams(vmem_limit_bytes=VMEM_BYTES),
+        compiler_params=pltpu.CompilerParams(vmem_limit_bytes=SMALL_VMEM_BYTES),
         name="prepare_weights",
     )(
         jnp.transpose(w_in, (2, 3, 4, 1, 0)).reshape(27, c),
@@ -357,7 +360,7 @@
         return (*lead, plan.z(halo) * c, plan.x(halo) * LANES)
 
     scratch += [pltpu.VMEM(region(plan.halo_u[l], (3,)), bf16) for l in range(1, layers + 1)]
-    scratch += [pltpu.VMEM(region(plan.halo_u[l]), f32) for l in range(1, layers + 1)]
+    scratch += [pltpu.VMEM(region(plan.halo_c[l - 1]), f32) for l in range(1, layers + 1)]
     scratch += [pltpu.VMEM(region(plan.halo_c[l - 1], (3,)), bf16) for l in range(1, layers + 1)]
     vmem = pl.BlockSpec(memory_space=pltpu.VMEM)
     scratch += [
@@ -425,7 +428,7 @@
         out_shape=[jax.ShapeDtypeStruct((copies, plan.zs, rows, LANES), jnp.bfloat16), own, own],
         in_specs=[pl.BlockSpec(memory_space=pltpu.SMEM), vmem],
         out_specs=[vmem] * 3,
-        compiler_params=pltpu.CompilerParams(vmem_limit_bytes=VMEM_BYTES),
+        compiler_params=pltpu.CompilerParams(vmem_limit_bytes=SMALL_VMEM_BYTES),
         name="image_and_halo",
     )(position, parts)
 
@@ -469,7 +472,7 @@
         out_shape=[thin, jax.ShapeDtypeStruct((mids * 27, c, c), f32), thin],
         in_specs=[vmem],
         out_specs=[vmem] * 3,
-        compiler_params=pltpu.CompilerParams(vmem_limit_bytes=VMEM_BYTES),
+        compiler_params=pltpu.CompilerParams(vmem_limit_bytes=SMALL_VMEM_BYTES),
         name="unpack_gradients",
     )(halves)
     mid = jnp.transpose(mid.reshape(mids, 3, 3, 3, c, c), (0, 4, 5, 1, 2, 3))

time: 170 us -> 164 us (0.965)
  Pallas kernels: 27 us -> 22 us
  waiting for transfers between devices: 34.8 us -> 38.3 us
  blocking collectives: 37 us -> 34.8 us
    all_to_all x5, waiting for transfers between devices: 26.8 us -> 30.2 us  [to_all(): lax.all_to_all(copies, axis, 0, 0, tiled=True, axis_index_groups=groups)]
    all_to_all x1, blocking collectives: 15 us -> 13 us  [shards(): received = lax.all_to_all(to_send, 'slab', 0, 0, tiled=True)]
    pallas_call x1, Pallas kernels: 4.63 us -> 2.81 us  [prepared_weights(): pl.pallas_call(lambda *refs: prepare_kernel(plan, *refs), out_shape=[jax....]
  transfers between devices with their start and end apart: 10 -> 10, of which waited for: 6 -> 6; matrix products, arithmetic and copies ran while one was open for 4% -> 3% of each run, Pallas kernels for 3% -> 2%
where the time goes in v5:
time: 164 us; the launch traced here: 163 us
  starting transfers between devices  54 us (33%)
  waiting for transfers between devices  38.3 us (23%)
  blocking collectives  34.8 us (21%)
  Pallas kernels  22 us (13%)
  local copies, waits for them, and re-layouts  7.63 us (5%)
  other arithmetic  3.96 us (2%)
  between operations  1.67 us (1%)
    all_to_all x5, starting transfers between devices, to_all(): lax.all_to_all(copies, axis, 0, 0, tiled=True, axis_index_groups=groups)  39 us
    all_to_all x5, waiting for transfers between devices, to_all(): lax.all_to_all(copies, axis, 0, 0, tiled=True, axis_index_groups=groups)  30.2 us
    all_gather x4, blocking collectives, pair_gather(): lax.all_gather(value, 'sector', axis_index_groups=within_chip('sector'))  21.8 us
    pallas_call x1, Pallas kernels, network(): pl.pallas_call(lambda *refs: network_kernel(plan, grid, *refs), out_shape...  17.2 us
    all_to_all x1, blocking collectives, shards(): received = lax.all_to_all(to_send, 'slab', 0, 0, tiled=True)  13 us
    ppermute x4, starting transfers between devices, shards(): lax.ppermute(fields, 'sector', pairs)  11.5 us
    all_to_all x1, waiting for transfers between devices, summed_everywhere(): own = jnp.sum(lax.all_to_all(parts, 'slab', 0, 0, tiled=True), axis=0)  8 us
    all_to_all x1, starting transfers between devices, summed_everywhere(): own = jnp.sum(lax.all_to_all(parts, 'slab', 0, 0, tiled=True), axis=0)  3.55 us
  transfers between devices with their start and end apart: 10, of which 6 were waited for; matrix products, arithmetic and copies ran while one was open for 3% of the time, Pallas kernels for 2%

profile of v5, /device:TPU:1, one launch (start us, length us, event | category | flops | bytes accessed | tf_op | source)
XLA Modules:
  0.0 163.2 jit_solution(6210965354298661705)
XLA Ops:
  0.7 0.8 convert_element_type.57
  1.4 0.7 convert_element_type.56
  2.2 0.6 broadcast_in_dim.18
  2.8 15.7 %all-to-all-start = ((bf16[16,8,128]{2,1,0:T(8,128)(2,1)}), bf16[16,8,128]{2,1,0:T(8,128)(2,1)S(1)}, u32[]{:S(2)}, u32[]{:S(2)}) async-start(bf16[16,8,128]{2,1,0:T(8,128)(2,1)} %broadcast_in_dim.18), calls=%async_computation | async-start | bytes 65536 | tf_op jit(solution)/shard_map/all_to_all | solution.py:500
  18.6 0.7 fusion.19
  19.2 0.7 bitcast_convert_fusion
  19.9 0.7 fusion.18
  21.2 0.7 reshape.202
  21.9 0.1 copy.25
  22.0 8.0 %all-to-all-done = bf16[16,8,128]{2,1,0:T(8,128)(2,1)S(1)} async-done(((bf16[16,8,128]{2,1,0:T(8,128)(2,1)}), bf16[16,8,128]{2,1,0:T(8,128)(2,1)S(1)}, u32[]{:S(2)}, u32[]{:S(2)}) %all-to-all-start) | async-done | bytes 32800 | tf_op jit(solution)/shard_map/all_to_all | solution.py:500
  30.0 3.5 %all-gather = bf16[32,6,128]{2,0,1:T(8,128)(2,1)S(1)} all-gather(bf16[16,6,128]{2,0,1:T(8,128)(2,1)S(1)} %copy.30), channel_id=2, replica_groups={{0,16},{32,48},{64,80},{96,112},{128,144},{160,176},{192,208},{224,240}..., dimensions={0}, use_global_device_ids=true | all-gather | bytes 73728 | tf_op jit(solution)/shard_map/all_gather | solution.py:504
  33.6 0.6 gather_fusion
  34.2 0.3 fusion.4
  34.6 0.7 broadcast_in_dim.21
  35.3 6.8 %all-to-all-start.1 = ((f32[16,12,128]{2,1,0:T(8,128)}), f32[16,12,128]{2,1,0:T(8,128)S(1)}, u32[]{:S(2)}, u32[]{:S(2)}) async-start(f32[16,12,128]{2,1,0:T(8,128)} %broadcast_in_dim.21), calls=%async_computation.1 | async-start | bytes 262144 | tf_op jit(solution)/shard_map/all_to_all | solution.py:500
  42.2 2.8 %prepare_weights.1 = (bf16[544,256]{1,0:T(8,128)(2,1)S(1)}, bf16[352,256]{1,0:T(8,128)(2,1)S(1)}, bf16[8,1536]{1,0:T(8,128)(2,1)S(1)}, bf16[8,1536]{1,0:T(8,128)...) custom-call(bf16[27,32]{1,0:T(8,128)(2,1)S(1)} %reshape.197.refs_0_,, ...), custom_call_target="tpu_custom_call" | custom-call | tf_op jit(solution)/shard_map/prepare_weights/pallas_call | solution.py:336
  45.0 3.8 %all-to-all-done.1 = f32[16,12,128]{2,1,0:T(8,128)S(1)} async-done(((f32[16,12,128]{2,1,0:T(8,128)}), f32[16,12,128]{2,1,0:T(8,128)S(1)}, u32[]{:S(2)}, u32[]{:S(2)}) %all-to-all-start.1) | async-done | bytes 98336 | tf_op jit(solution)/shard_map/all_to_all | solution.py:500
  48.8 0.2 slice_reduce_fusion
  49.0 0.2 fusion.1
  49.2 0.6 gather_fusion.1
  49.7 0.2 fusion.2
  50.0 0.7 broadcast_in_dim.22
  50.7 3.5 %all-to-all-start.2 = ((f32[16,12,256]{2,1,0:T(8,128)}), f32[16,12,256]{2,1,0:T(8,128)S(1)}, u32[]{:S(2)}, u32[]{:S(2)}) async-start(f32[16,12,256]{2,1,0:T(8,128)} %broadcast_in_dim.22), calls=%async_computation.2 | async-start | bytes 524288 | tf_op jit(solution)/shard_map/all_to_all | solution.py:500
  54.4 0.1 select_n.35
  54.6 1.3 collective-permute-start.3
  55.9 1.3 collective-permute-start.2
  57.2 4.0 %collective-permute-start.1 = (f32[24,128]{1,0:T(8,128)S(1)}, f32[24,128]{1,0:T(8,128)S(1)}, u32[]{:S(2)}, u32[]{:S(2)}) collective-permute-start(f32[24,128]{1,0:T(8,128)S(1)} %select_maximum_fusion), channel_id=1, source_target_pairs={{0,32},{16,48},{32,64},{48,80},{64,96},{80,112},{96,128},{112,144}... | collective-permute-start | bytes 36872 | tf_op jit(solution)/shard_map/ppermute | solution.py:565
  61.2 4.9 %collective-permute-start = (f32[24,128]{1,0:T(8,128)S(1)}, f32[24,128]{1,0:T(8,128)S(1)}, u32[]{:S(2)}, u32[]{:S(2)}) collective-permute-start(f32[24,128]{1,0:T(8,128)S(1)} %select_maximum_fusion), channel_id=1, source_target_pairs={{0,64},{16,80},{32,96},{48,112},{64,128},{80,144},{96,160},{112,17... | collective-permute-start | bytes 36872 | tf_op jit(solution)/shard_map/ppermute | solution.py:565
  66.2 0.9 all-to-all-done.2
  67.1 0.2 fusion.7
  67.4 0.6 concatenate.15
  68.0 8.2 %all-gather.4.refs_1_ = f32[2,150,128]{2,1,0:T(8,128)S(1)} all-gather(f32[1,150,128]{2,1,0:T(8,128)S(1)} %bitcast.68), channel_id=3, replica_groups={{0,16},{32,48},{64,80},{96,112},{128,144},{160,176},{192,208},{224,240}..., dimensions={0}, use_global_device_ids=true | all-gather | bytes 230400 | tf_op jit(solution)/shard_map/all_gather | solution.py:504
  76.2 0.6 image_and_halo.1
  76.8 13.0 %all_to_all.35 = bf16[16,3,30,128]{3,2,1,0:T(8,128)(2,1)S(1)} all-to-all(bf16[16,3,30,128]{3,2,1,0:T(8,128)(2,1)S(1)} %get-tuple-element.58), channel_id=1, replica_groups=mesh['sector'=32,'slab'=16] {'slab'}, dimensions={0} | all-to-all | bytes 737280 | tf_op jit(solution)/shard_map/all_to_all | solution.py:598
  89.8 17.2 %network.1 = (f32[3,256]{1,0:T(4,128)S(1)}, f32[3,256]{1,0:T(4,128)S(1)}, f32[768,128]{1,0:T(8,128)}) custom-call(s32[2]{0:T(128)S(1)} %pad_add_fusion.refs_0_, bf16[48,30,128]{2,1,0:T(8,128)(2,1)S(1)} %bitcast.66, f32[3,256]{1,0:T(4,128)S(1)} %get-tuple-element.59.refs_2_, f32[3,256]{1,0:T(4,128)S(1)} %get-tuple-element.60.refs_3_, ...), custom_call_target="tpu_custom_call" | custom-call | tf_op jit(solution)/shard_map/network/pallas_call | solution.py:371
  107.0 3.6 %all-to-all-start.4 = ((f32[16,48,128]{2,1,0:T(8,128)}), f32[16,48,128]{2,1,0:T(8,128)S(1)}, u32[]{:S(2)}, u32[]{:S(2)}) async-start(f32[16,48,128]{2,1,0:T(8,128)} %bitcast.22), calls=%async_computation.4 | async-start | bytes 786432 | tf_op jit(solution)/shard_map/all_to_all | solution.py:512
  110.6 8.0 %all-to-all-done.4 = f32[16,48,128]{2,1,0:T(8,128)S(1)} async-done(((f32[16,48,128]{2,1,0:T(8,128)}), f32[16,48,128]{2,1,0:T(8,128)S(1)}, u32[]{:S(2)}, u32[]{:S(2)}) %all-to-all-start.4) | async-done | bytes 393248 | tf_op jit(solution)/shard_map/all_to_all | solution.py:512
  118.6 4.3 %all-gather.2 = f32[96,128]{1,0:T(8,128)S(1)} all-gather(f32[48,128]{1,0:T(8,128)S(1)} %reduce_sum.18), channel_id=4, replica_groups={{0,16},{32,48},{64,80},{96,112},{128,144},{160,176},{192,208},{224,240}..., dimensions={0}, use_global_device_ids=true | all-gather | bytes 73728 | tf_op jit(solution)/shard_map/all_gather | solution.py:504
  122.9 0.7 broadcast_in_dim.23
  123.6 9.4 %all-to-all-start.5 = ((bf16[16,24,128]{2,1,0:T(8,128)(2,1)}), bf16[16,24,128]{2,1,0:T(8,128)(2,1)S(1)}, u32[]{:S(2)}, u32[]{:S(2)}) async-start(bf16[16,24,128]{2,1,0:T(8,128)(2,1)} %broadcast_in_dim.23), calls=%async_computation.5 | async-start | bytes 196608 | tf_op jit(solution)/shard_map/all_to_all | solution.py:500
  133.0 0.6 reshape.207
  133.6 11.3 %all-to-all-done.5 = bf16[16,24,128]{2,1,0:T(8,128)(2,1)S(1)} async-done(((bf16[16,24,128]{2,1,0:T(8,128)(2,1)}), bf16[16,24,128]{2,1,0:T(8,128)(2,1)S(1)}, u32[]{:S(2)}, u32[]{:S(2)}) %all-to-all-start.5) | async-done | bytes 98336 | tf_op jit(solution)/shard_map/all_to_all | solution.py:500
  145.0 0.7 broadcast_in_dim.24
  145.6 3.5 %all-to-all-start.6 = ((f32[16,24,128]{2,1,0:T(8,128)}), f32[16,24,128]{2,1,0:T(8,128)S(1)}, u32[]{:S(2)}, u32[]{:S(2)}) async-start(f32[16,24,128]{2,1,0:T(8,128)} %broadcast_in_dim.24), calls=%async_computation.6 | async-start | bytes 393216 | tf_op jit(solution)/shard_map/all_to_all | solution.py:500
  149.2 0.6 reshape.208
  149.8 6.3 %all-to-all-done.6 = f32[16,24,128]{2,1,0:T(8,128)S(1)} async-done(((f32[16,24,128]{2,1,0:T(8,128)}), f32[16,24,128]{2,1,0:T(8,128)S(1)}, u32[]{:S(2)}, u32[]{:S(2)}) %all-to-all-start.6) | async-done | bytes 196640 | tf_op jit(solution)/shard_map/all_to_all | solution.py:500
  156.1 5.7 %all-gather.3 = f32[32,24,128]{2,1,0:T(8,128)S(1)} all-gather(f32[16,24,128]{2,1,0:T(8,128)S(1)} %all-to-all-done.6), channel_id=5, replica_groups={{0,16},{32,48},{64,80},{96,112},{128,144},{160,176},{192,208},{224,240}..., dimensions={0}, use_global_device_ids=true | all-gather | bytes 589824 | tf_op jit(solution)/shard_map/all_gather | solution.py:504
  161.8 1.4 unpack_gradients.1
  (50 shorter events, 0.8 us)
Async XLA Ops:
  0.6 33.6 %copy-start = (bf16[1,12,104,256]{3,2,1,0:T(8,128)(2,1)S(1)}, bf16[1,12,104,256]{3,2,1,0:T(8,128)(2,1)}, u32[]{:S(2)}) copy-start(bf16[1,12,104,256]{3,2,1,0:T(8,128)(2,1)} %param.14) | copy-start | bytes 1916932
  0.6 41.5 %copy-start.5 = (bf16[1,32,3,3,3]{1,4,3,2,0:T(4,128)(2,1)S(1)}, bf16[1,32,3,3,3]{1,4,3,2,0:T(4,128)(2,1)}, u32[]{:S(2)}) copy-start(bf16[1,32,3,3,3]{1,4,3,2,0:T(4,128)(2,1)} %param.22) | copy-start | bytes 5188
  0.7 41.5 %copy-start.1 = (bf16[3,32,32,3,3,3]{2,1,5,4,3,0:T(8,128)(2,1)S(1)}, bf16[3,32,32,3,3,3]{2,1,5,4,3,0:T(8,128)(2,1)}, u32[]{:S(2)}) copy-start(bf16[3,32,32,3,3,3]{2,1,5,4,3,0:T(8,128)(2,1)} %param.21) | copy-start | bytes 497668
  0.7 41.4 %copy-start.4 = (bf16[32,1,3,3,3]{0,4,3,2,1:T(4,128)(2,1)S(1)}, bf16[32,1,3,3,3]{0,4,3,2,1:T(4,128)(2,1)}, u32[]{:S(2)}) copy-start(bf16[32,1,3,3,3]{0,4,3,2,1:T(4,128)(2,1)} %param.20) | copy-start | bytes 5188
  2.8 27.2 %all-to-all-start = ((bf16[16,8,128]{2,1,0:T(8,128)(2,1)}), bf16[16,8,128]{2,1,0:T(8,128)(2,1)S(1)}, u32[]{:S(2)}, u32[]{:S(2)}) async-start(bf16[16,8,128]{2,1,0:T(8,128)(2,1)} %broadcast_in_dim.18), calls=%async_computation | async-start | bytes 65536 | tf_op jit(solution)/shard_map/all_to_all | solution.py:500
  18.5 30.4 %copy-start.2 = (f32[1,32,104]{2,1,0:T(8,128)S(1)}, f32[1,32,104]{2,1,0:T(8,128)}, u32[]{:S(2)}) copy-start(f32[1,32,104]{2,1,0:T(8,128)} %param.19) | copy-start | bytes 39940
  18.5 30.4 %copy-start.3 = (f32[1,32,104]{2,1,0:T(8,128)S(1)}, f32[1,32,104]{2,1,0:T(8,128)}, u32[]{:S(2)}) copy-start(f32[1,32,104]{2,1,0:T(8,128)} %param.18) | copy-start | bytes 39940
  35.3 13.5 %all-to-all-start.1 = ((f32[16,12,128]{2,1,0:T(8,128)}), f32[16,12,128]{2,1,0:T(8,128)S(1)}, u32[]{:S(2)}, u32[]{:S(2)}) async-start(f32[16,12,128]{2,1,0:T(8,128)} %broadcast_in_dim.21), calls=%async_computation.1 | async-start | bytes 262144 | tf_op jit(solution)/shard_map/all_to_all | solution.py:500
  42.1 12.3 %copy-start.6 = (f32[3,2,128]{2,1,0:T(2,128)S(1)}, f32[3,2,128]{2,1,0:T(2,128)}, u32[]{:S(2)}) copy-start(f32[3,2,128]{2,1,0:T(2,128)} %param.13) | copy-start | bytes 9220
  42.2 12.3 %copy-start.7 = (f32[3,2,128]{2,1,0:T(2,128)S(1)}, f32[3,2,128]{2,1,0:T(2,128)}, u32[]{:S(2)}) copy-start(f32[3,2,128]{2,1,0:T(2,128)} %param.23) | copy-start | bytes 9220
  50.7 16.3 %all-to-all-start.2 = ((f32[16,12,256]{2,1,0:T(8,128)}), f32[16,12,256]{2,1,0:T(8,128)S(1)}, u32[]{:S(2)}, u32[]{:S(2)}) async-start(f32[16,12,256]{2,1,0:T(8,128)} %broadcast_in_dim.22), calls=%async_computation.2 | async-start | bytes 524288 | tf_op jit(solution)/shard_map/all_to_all | solution.py:500
  54.6 12.8 %collective-permute-start.3 = (f32[24,128]{1,0:T(8,128)S(1)}, f32[24,128]{1,0:T(8,128)S(1)}, u32[]{:S(2)}, u32[]{:S(2)}) collective-permute-start(f32[24,128]{1,0:T(8,128)S(1)} %select_maximum_fusion), channel_id=1, source_target_pairs={{64,0},{80,16},{96,32},{112,48},{128,64},{144,80},{160,96},{176,11... | collective-permute-start | bytes 36872 | tf_op jit(solution)/shard_map/ppermute | solution.py:565
  55.9 11.5 %collective-permute-start.2 = (f32[24,128]{1,0:T(8,128)S(1)}, f32[24,128]{1,0:T(8,128)S(1)}, u32[]{:S(2)}, u32[]{:S(2)}) collective-permute-start(f32[24,128]{1,0:T(8,128)S(1)} %select_maximum_fusion), channel_id=1, source_target_pairs={{32,0},{48,16},{64,32},{80,48},{96,64},{112,80},{128,96},{144,112}... | collective-permute-start | bytes 36872 | tf_op jit(solution)/shard_map/ppermute | solution.py:565
  57.2 10.2 %collective-permute-start.1 = (f32[24,128]{1,0:T(8,128)S(1)}, f32[24,128]{1,0:T(8,128)S(1)}, u32[]{:S(2)}, u32[]{:S(2)}) collective-permute-start(f32[24,128]{1,0:T(8,128)S(1)} %select_maximum_fusion), channel_id=1, source_target_pairs={{0,32},{16,48},{32,64},{48,80},{64,96},{80,112},{96,128},{112,144}... | collective-permute-start | bytes 36872 | tf_op jit(solution)/shard_map/ppermute | solution.py:565
  61.2 6.2 %collective-permute-start = (f32[24,128]{1,0:T(8,128)S(1)}, f32[24,128]{1,0:T(8,128)S(1)}, u32[]{:S(2)}, u32[]{:S(2)}) collective-permute-start(f32[24,128]{1,0:T(8,128)S(1)} %select_maximum_fusion), channel_id=1, source_target_pairs={{0,64},{16,80},{32,96},{48,112},{64,128},{80,144},{96,160},{112,17... | collective-permute-start | bytes 36872 | tf_op jit(solution)/shard_map/ppermute | solution.py:565
  107.0 11.6 %all-to-all-start.4 = ((f32[16,48,128]{2,1,0:T(8,128)}), f32[16,48,128]{2,1,0:T(8,128)S(1)}, u32[]{:S(2)}, u32[]{:S(2)}) async-start(f32[16,48,128]{2,1,0:T(8,128)} %bitcast.22), calls=%async_computation.4 | async-start | bytes 786432 | tf_op jit(solution)/shard_map/all_to_all | solution.py:512
  123.6 21.3 %all-to-all-start.5 = ((bf16[16,24,128]{2,1,0:T(8,128)(2,1)}), bf16[16,24,128]{2,1,0:T(8,128)(2,1)S(1)}, u32[]{:S(2)}, u32[]{:S(2)}) async-start(bf16[16,24,128]{2,1,0:T(8,128)(2,1)} %broadcast_in_dim.23), calls=%async_computation.5 | async-start | bytes 196608 | tf_op jit(solution)/shard_map/all_to_all | solution.py:500
  145.6 10.4 %all-to-all-start.6 = ((f32[16,24,128]{2,1,0:T(8,128)}), f32[16,24,128]{2,1,0:T(8,128)S(1)}, u32[]{:S(2)}, u32[]{:S(2)}) async-start(f32[16,24,128]{2,1,0:T(8,128)} %broadcast_in_dim.24), calls=%async_computation.6 | async-start | bytes 393216 | tf_op jit(solution)/shard_map/all_to_all | solution.py:500

commit v6 on v5

--- a/solution.py
+++ b/solution.py
@@ -519,6 +519,69 @@
     return pair_gather(to_all(half, "slab")), beside
 
 
+def small_call(kernel, name, shapes, operands, scalars):
+    vmem = pl.BlockSpec(memory_space=pltpu.VMEM)
+    smem = pl.BlockSpec(memory_space=pltpu.SMEM)
+    return pl.pallas_call(
+        kernel,
+        out_shape=shapes,
+        in_specs=[smem] * scalars + [vmem] * (len(operands) - scalars),
+        out_specs=vmem,
+        compiler_params=pltpu.CompilerParams(vmem_limit_bytes=SMALL_VMEM_BYTES),
+        name=name,
+    )(*operands)
+
+
+def message_kernel(image, cols, out):
+    f32 = jnp.float32
+    zs = image.shape[0]
+    rows = [image[z] for z in range(zs)]
+    numbers = cols[...].astype(f32)
+    rows.append(jnp.concatenate([numbers, jnp.zeros((1, LANES - numbers.shape[1]), f32)], axis=1))
+    used = sum(part.shape[0] for part in rows)
+    if out.shape[1] > used:
+        rows.append(jnp.zeros((out.shape[1] - used, LANES), f32))
+    message = jnp.concatenate(rows, axis=0).astype(out.dtype)
+    for k in range(out.shape[0]):
+        out[k] = message
+
+
+def padded_rows(rows):
+    short = round_up(rows.shape[0], 16) - rows.shape[0]
+    if short:
+        rows = jnp.concatenate([rows, jnp.zeros((short, rows.shape[1]), rows.dtype)], axis=0)
+    return rows
+
+
+def backward_kernel(block_len, rows, count, every, measured, background, values, out):
+    f32, bf16 = jnp.float32, jnp.bfloat16
+    slots, row_len, _ = values.shape
+    line_blocks = measured.shape[1]
+    terms = jnp.concatenate([every[k] for k in range(every.shape[0])], axis=0)
+    number = lax.broadcasted_iota(jnp.int32, (terms.shape[0], line_blocks), 1).astype(f32)
+    placing = jnp.where(terms[:, row_len : row_len + 1] == number, 1.0, 0.0)
+    projection = lax.dot_general(
+        placing,
+        terms,
+        (((0,), (0,)), ((), ())),
+        precision=lax.Precision.HIGHEST,
+        preferred_element_type=f32,
+    )[:, :row_len]
+    ratio = (measured[0] / (projection + background[0])).astype(bf16)
+    number = lax.broadcasted_iota(jnp.int32, (1, line_blocks), 1)
+    chosen = [jnp.where(number == rows[0, k], 1.0, 0.0) for k in range(slots)]
+    chosen = padded_rows(jnp.concatenate(chosen, axis=0)).astype(bf16)
+    ratios = jnp.dot(chosen, ratio, preferred_element_type=f32).astype(bf16)
+    lines = []
+    for k in range(slots):
+        sums = jnp.dot(ratios, values[k], preferred_element_type=f32)
+        weight = jnp.where(k < count[0, 0], 1.0 / block_len, 0.0)
+        lines.append(sums[k : k + 1] * weight)
+    lines = jnp.concatenate(lines, axis=0)
+    for k in range(out.shape[0]):
+        out[k] = lines
+
+
 def shards(
     image,
     sensitivity,
@@ -539,16 +602,16 @@
     sector, slab = lax.axis_index("sector"), lax.axis_index("slab")
     zs, xs, ys = image.shape
     block_len = xs * ys
-    line_blocks, row_len = measured.shape[1:]
+    row_len = measured.shape[2]
     slots = tile_rows.shape[1]
     plan = Plan(zs, xs, w_in.shape[0], w_mid.shape[0] + 1)
     grid = (zs * slabs, xs * sectors)
 
     cells = zs * xs
     chips = along_chips("sector")
-    cols_row = jnp.pad(tile_cols.astype(bf16), ((0, round_up(cells + 1, 8) - cells - 1), (0, ys - slots)))
-    sent = jnp.concatenate([image.astype(bf16).reshape(cells, ys), cols_row], axis=0)
-    from_chips = to_all(sent, "sector", chips)
+    message = jax.ShapeDtypeStruct((len(chips[0]), round_up(cells + 1, 8), ys), bf16)
+    message = small_call(message_kernel, "first_message", message, (image, tile_cols), 0)
+    from_chips = lax.all_to_all(message, "sector", 0, 0, tiled=True, axis_index_groups=chips)
     every_cols = from_chips[:, cells, :slots].astype(f32).reshape(-1)
     got = pair_gather(from_chips[:, :cells])
     got = jnp.transpose(got.reshape(CORES, len(chips[0]), zs, xs, ys), (2, 1, 0, 3, 4))
@@ -573,16 +636,18 @@
     lined = jnp.pad(lined, ((0, 0), (0, LANES - row_len - 1)))
     lined, *kernels = lax.optimization_barrier((lined, w_in, w_mid, w_out))
     weights = prepared_weights(plan, *kernels)
-    every = to_all(lined, "slab").reshape(slabs * slots, LANES)
-    every_rows = every[:, row_len]
-    placing = (every_rows[None, :] == jnp.arange(line_blocks, dtype=f32)[:, None]).astype(f32)
-    projection = jnp.dot(placing, every[:, :row_len], precision=highest)
-    ratio = (measured[0] / (projection + background[0])).astype(bf16)
-
-    backward = jnp.einsum("krv,kr->kv", values, ratio[tile_rows[0]], preferred_element_type=f32)
-    backward = backward * weight[:, None]
+    every = to_all(lined, "slab")
+
+    backward = small_call(
+        lambda *refs: backward_kernel(block_len, *refs),
+        "back_terms",
+        jax.ShapeDtypeStruct((len(chips[0]), slots, block_len), f32),
+        (tile_rows, tile_count, every, measured, background, values),
+        2,
+    )
     backward, weights = lax.optimization_barrier((backward, weights))
-    every_back = to_all(backward, "sector", chips).reshape(-1, block_len)
+    every_back = lax.all_to_all(backward, "sector", 0, 0, tiled=True, axis_index_groups=chips)
+    every_back = every_back.reshape(-1, block_len)
     core = lax.rem(sector, CORES)
     span = (2 * reach + 1) * CORES
     near = sector - core - reach * CORES + jnp.arange(span)

time: 164 us -> 165 us (level)
  other arithmetic: 3.96 us -> 1.09 us
  Pallas kernels: 22 us -> 24.5 us
  waiting for transfers between devices: 38.3 us -> 40.3 us
    all_to_all x0 -> x2, starting transfers between devices: none -> 19.3 us  [the longest x1 15.7 us: shards(): lax.all_to_all(message, 'sector', 0, 0, tiled=True, axis_index_groups=chips)]
    all_to_all x5 -> x3, starting transfers between devices: 39 us -> 19.8 us  [to_all(): lax.all_to_all(copies, axis, 0, 0, tiled=True, axis_index_groups=groups)]
    all_to_all x0 -> x2, waiting for transfers between devices: none -> 10.9 us  [the longest x1 10 us: shards(): lax.all_to_all(message, 'sector', 0, 0, tiled=True, axis_index_groups=chips)]
    all_to_all x5 -> x3, waiting for transfers between devices: 30.2 us -> 21.4 us  [to_all(): lax.all_to_all(copies, axis, 0, 0, tiled=True, axis_index_groups=groups)]
    pallas_call x0 -> x2, Pallas kernels: none -> 2.53 us  [small_call(): pl.pallas_call(kernel, out_shape=shapes, in_specs=[smem] * scalars + [vme...]
    broadcast_in_dim x5 -> x3, local copies, waits for them, and re-layouts: 3.4 us -> 2.03 us  [to_all(): copies = jnp.broadcast_to(value[None], (count, *value.shape))]
  transfers between devices with their start and end apart: 10 -> 10, of which waited for: 6 -> 6; matrix products, arithmetic and copies ran while one was open for 3% -> 2% of each run, Pallas kernels for 2% -> 2%
where the time goes in v6:
time: 165 us; the launch traced here: 164 us
  starting transfers between devices  54.1 us (33%)
  waiting for transfers between devices  40.3 us (24%)
  blocking collectives  34.8 us (21%)
  Pallas kernels  24.5 us (15%)
  local copies, waits for them, and re-layouts  6.23 us (4%)
    all_gather x4, blocking collectives, pair_gather(): lax.all_gather(value, 'sector', axis_index_groups=within_chip('sector'))  21.8 us
    all_to_all x3, waiting for transfers between devices, to_all(): lax.all_to_all(copies, axis, 0, 0, tiled=True, axis_index_groups=groups)  21.4 us
    all_to_all x3, starting transfers between devices, to_all(): lax.all_to_all(copies, axis, 0, 0, tiled=True, axis_index_groups=groups)  19.8 us
    pallas_call x1, Pallas kernels, network(): pl.pallas_call(lambda *refs: network_kernel(plan, grid, *refs), out_shape...  17.2 us
    all_to_all x1, starting transfers between devices, shards(): lax.all_to_all(message, 'sector', 0, 0, tiled=True, axis_index_groups=chips)  15.7 us
    all_to_all x1, blocking collectives, shards(): received = lax.all_to_all(to_send, 'slab', 0, 0, tiled=True)  13 us
    ppermute x4, starting transfers between devices, shards(): lax.ppermute(fields, 'sector', pairs)  11.5 us
    all_to_all x1, waiting for transfers between devices, shards(): lax.all_to_all(message, 'sector', 0, 0, tiled=True, axis_index_groups=chips)  10 us
  transfers between devices with their start and end apart: 10, of which 6 were waited for; matrix products, arithmetic and copies ran while one was open for 2% of the time, Pallas kernels for 2%

profile of v6, /device:TPU:1, one launch (start us, length us, event | category | flops | bytes accessed | tf_op | source)
XLA Modules:
  0.0 164.3 jit_solution(15761705634032865910)
XLA Ops:
  0.6 0.0 copy-start
  0.7 0.8 copy-done.4
  1.5 0.7 copy-done.6
  2.1 0.6 first_message.1
  2.7 15.7 %all-to-all-start = ((bf16[16,8,128]{2,1,0:T(8,128)(2,1)}), bf16[16,8,128]{2,1,0:T(8,128)(2,1)S(1)}, u32[]{:S(2)}, u32[]{:S(2)}) async-start(bf16[16,8,128]{2,1,0:T(8,128)(2,1)} %first_message.1), calls=%async_computation | async-start | bytes 65536 | tf_op jit(solution)/shard_map/all_to_all | solution.py:614
  19.2 0.7 convert_bitcast_fusion
  19.8 0.1 copy.27
  19.9 10.0 %all-to-all-done = bf16[16,8,128]{2,1,0:T(8,128)(2,1)S(1)} async-done(((bf16[16,8,128]{2,1,0:T(8,128)(2,1)}), bf16[16,8,128]{2,1,0:T(8,128)(2,1)S(1)}, u32[]{:S(2)}, u32[]{:S(2)}) %all-to-all-start) | async-done | bytes 32800 | tf_op jit(solution)/shard_map/all_to_all | solution.py:614
  30.0 3.5 %all-gather = bf16[32,6,128]{2,0,1:T(8,128)(2,1)S(1)} all-gather(bf16[16,6,128]{2,0,1:T(8,128)(2,1)S(1)} %copy.25), channel_id=2, replica_groups={{0,16},{32,48},{64,80},{96,112},{128,144},{160,176},{192,208},{224,240}..., dimensions={0}, use_global_device_ids=true | all-gather | bytes 73728 | tf_op jit(solution)/shard_map/all_gather | solution.py:504
  33.6 0.6 gather_fusion
  34.1 1.3 fusion.5
  35.5 0.1 bitcast_multiply_fusion
  35.6 0.1 select_maximum_fusion.2
  35.6 0.7 broadcast_in_dim.20
  36.3 6.9 %all-to-all-start.1 = ((f32[16,12,128]{2,1,0:T(8,128)}), f32[16,12,128]{2,1,0:T(8,128)S(1)}, u32[]{:S(2)}, u32[]{:S(2)}) async-start(f32[16,12,128]{2,1,0:T(8,128)} %broadcast_in_dim.20), calls=%async_computation.1 | async-start | bytes 262144 | tf_op jit(solution)/shard_map/all_to_all | solution.py:500
  43.3 2.8 %prepare_weights.1 = (bf16[544,256]{1,0:T(8,128)(2,1)S(1)}, bf16[352,256]{1,0:T(8,128)(2,1)S(1)}, bf16[8,1536]{1,0:T(8,128)(2,1)S(1)}, bf16[8,1536]{1,0:T(8,128)...) custom-call(bf16[27,32]{1,0:T(8,128)(2,1)S(1)} %reshape.159.refs_0_,, ...), custom_call_target="tpu_custom_call" | custom-call | tf_op jit(solution)/shard_map/prepare_weights/pallas_call | solution.py:336
  46.1 3.8 %all-to-all-done.1.refs_2_ = f32[16,12,128]{2,1,0:T(8,128)S(1)} async-done(((f32[16,12,128]{2,1,0:T(8,128)}), f32[16,12,128]{2,1,0:T(8,128)S(1)}, u32[]{:S(2)}, u32[]{:S(2)}) %all-to-all-start.1) | async-done | bytes 98336 | tf_op jit(solution)/shard_map/all_to_all | solution.py:500
  49.9 1.9 %back_terms.1 = f32[16,12,256]{2,1,0:T(8,128)} custom-call(s32[1,12]{1,0:T(1,128)S(1)} %copy-done.5, s32[1,1]{1,0:T(1,128)} %copy.36.refs_1_, f32[16,12,128]{2,1,0:T(8,128)S(1)} %all-to-all-done.1.refs_2_, f32[1,32,104]{2,1,0:T(8,128)S(1)} %copy-done.2, f32[1,32,104]{2,1,0:T(8,128)S(1)} %copy-done.3, bf16[12,104,256]{2,1,0:T(8,128)(2,1)S(1)} %bitcast.53), custom_call_target="tpu_custom_call" | custom-call | tf_op jit(solution)/shard_map/back_terms/pallas_call | solution.py:525
  51.8 3.5 %all-to-all-start.2 = ((f32[16,12,256]{2,1,0:T(8,128)}), f32[16,12,256]{2,1,0:T(8,128)S(1)}, u32[]{:S(2)}, u32[]{:S(2)}) async-start(f32[16,12,256]{2,1,0:T(8,128)} %back_terms.1), calls=%async_computation.2 | async-start | bytes 524288 | tf_op jit(solution)/shard_map/all_to_all | solution.py:649
  55.4 0.1 convert_select_fusion
  55.5 0.1 select_n.25
  55.6 0.1 pad_add_fusion.refs_0_
  55.7 1.3 collective-permute-start.3
  57.0 1.3 collective-permute-start.2
  58.3 4.0 %collective-permute-start.1 = (f32[24,128]{1,0:T(8,128)S(1)}, f32[24,128]{1,0:T(8,128)S(1)}, u32[]{:S(2)}, u32[]{:S(2)}) collective-permute-start(f32[24,128]{1,0:T(8,128)S(1)} %select_maximum_fusion), channel_id=1, source_target_pairs={{0,32},{16,48},{32,64},{48,80},{64,96},{80,112},{96,128},{112,144}... | collective-permute-start | bytes 36872 | tf_op jit(solution)/shard_map/ppermute | solution.py:628
  62.3 4.9 %collective-permute-start = (f32[24,128]{1,0:T(8,128)S(1)}, f32[24,128]{1,0:T(8,128)S(1)}, u32[]{:S(2)}, u32[]{:S(2)}) collective-permute-start(f32[24,128]{1,0:T(8,128)S(1)} %select_maximum_fusion), channel_id=1, source_target_pairs={{0,64},{16,80},{32,96},{48,112},{64,128},{80,144},{96,160},{112,17... | collective-permute-start | bytes 36872 | tf_op jit(solution)/shard_map/ppermute | solution.py:628
  67.2 0.1 reshape.174
  67.3 0.9 all-to-all-done.2
  68.2 0.2 fusion
  68.5 0.0 collective-permute-done.3
  68.5 0.6 concatenate.11
  69.1 8.2 %all-gather.4.refs_1_ = f32[2,150,128]{2,1,0:T(8,128)S(1)} all-gather(f32[1,150,128]{2,1,0:T(8,128)S(1)} %bitcast.57), channel_id=3, replica_groups={{0,16},{32,48},{64,80},{96,112},{128,144},{160,176},{192,208},{224,240}..., dimensions={0}, use_global_device_ids=true | all-gather | bytes 230400 | tf_op jit(solution)/shard_map/all_gather | solution.py:504
  77.3 0.6 image_and_halo.1
  77.9 13.0 %all_to_all.35 = bf16[16,3,30,128]{3,2,1,0:T(8,128)(2,1)S(1)} all-to-all(bf16[16,3,30,128]{3,2,1,0:T(8,128)(2,1)S(1)} %get-tuple-element.58), channel_id=1, replica_groups=mesh['sector'=32,'slab'=16] {'slab'}, dimensions={0} | all-to-all | bytes 737280 | tf_op jit(solution)/shard_map/all_to_all | solution.py:663
  90.9 17.2 %network.1 = (f32[3,256]{1,0:T(4,128)S(1)}, f32[3,256]{1,0:T(4,128)S(1)}, f32[768,128]{1,0:T(8,128)}) custom-call(s32[2]{0:T(128)S(1)} %pad_add_fusion.refs_0_, bf16[48,30,128]{2,1,0:T(8,128)(2,1)S(1)} %bitcast.55, f32[3,256]{1,0:T(4,128)S(1)} %get-tuple-element.59.refs_2_, f32[3,256]{1,0:T(4,128)S(1)} %get-tuple-element.60.refs_3_, ...), custom_call_target="tpu_custom_call" | custom-call | tf_op jit(solution)/shard_map/network/pallas_call | solution.py:371
  108.1 3.6 %all-to-all-start.4 = ((f32[16,48,128]{2,1,0:T(8,128)}), f32[16,48,128]{2,1,0:T(8,128)S(1)}, u32[]{:S(2)}, u32[]{:S(2)}) async-start(f32[16,48,128]{2,1,0:T(8,128)} %bitcast.17), calls=%async_computation.4 | async-start | bytes 786432 | tf_op jit(solution)/shard_map/all_to_all | solution.py:512
  111.7 8.0 %all-to-all-done.4 = f32[16,48,128]{2,1,0:T(8,128)S(1)} async-done(((f32[16,48,128]{2,1,0:T(8,128)}), f32[16,48,128]{2,1,0:T(8,128)S(1)}, u32[]{:S(2)}, u32[]{:S(2)}) %all-to-all-start.4) | async-done | bytes 393248 | tf_op jit(solution)/shard_map/all_to_all | solution.py:512
  119.7 4.3 %all-gather.2 = f32[96,128]{1,0:T(8,128)S(1)} all-gather(f32[48,128]{1,0:T(8,128)S(1)} %reduce_sum.18), channel_id=4, replica_groups={{0,16},{32,48},{64,80},{96,112},{128,144},{160,176},{192,208},{224,240}..., dimensions={0}, use_global_device_ids=true | all-gather | bytes 73728 | tf_op jit(solution)/shard_map/all_gather | solution.py:504
  124.1 0.7 broadcast_in_dim.21
  124.7 9.4 %all-to-all-start.5 = ((bf16[16,24,128]{2,1,0:T(8,128)(2,1)}), bf16[16,24,128]{2,1,0:T(8,128)(2,1)S(1)}, u32[]{:S(2)}, u32[]{:S(2)}) async-start(bf16[16,24,128]{2,1,0:T(8,128)(2,1)} %broadcast_in_dim.21), calls=%async_computation.5 | async-start | bytes 196608 | tf_op jit(solution)/shard_map/all_to_all | solution.py:500
  134.1 0.6 reshape.169
  134.7 11.3 %all-to-all-done.5 = bf16[16,24,128]{2,1,0:T(8,128)(2,1)S(1)} async-done(((bf16[16,24,128]{2,1,0:T(8,128)(2,1)}), bf16[16,24,128]{2,1,0:T(8,128)(2,1)S(1)}, u32[]{:S(2)}, u32[]{:S(2)}) %all-to-all-start.5) | async-done | bytes 98336 | tf_op jit(solution)/shard_map/all_to_all | solution.py:500
  146.1 0.7 broadcast_in_dim.22
  146.7 3.5 %all-to-all-start.6 = ((f32[16,24,128]{2,1,0:T(8,128)}), f32[16,24,128]{2,1,0:T(8,128)S(1)}, u32[]{:S(2)}, u32[]{:S(2)}) async-start(f32[16,24,128]{2,1,0:T(8,128)} %broadcast_in_dim.22), calls=%async_computation.6 | async-start | bytes 393216 | tf_op jit(solution)/shard_map/all_to_all | solution.py:500
  150.3 0.6 reshape.170
  150.9 6.3 %all-to-all-done.6 = f32[16,24,128]{2,1,0:T(8,128)S(1)} async-done(((f32[16,24,128]{2,1,0:T(8,128)}), f32[16,24,128]{2,1,0:T(8,128)S(1)}, u32[]{:S(2)}, u32[]{:S(2)}) %all-to-all-start.6) | async-done | bytes 196640 | tf_op jit(solution)/shard_map/all_to_all | solution.py:500
  157.2 5.7 %all-gather.3 = f32[32,24,128]{2,1,0:T(8,128)S(1)} all-gather(f32[16,24,128]{2,1,0:T(8,128)S(1)} %all-to-all-done.6), channel_id=5, replica_groups={{0,16},{32,48},{64,80},{96,112},{128,144},{160,176},{192,208},{224,240}..., dimensions={0}, use_global_device_ids=true | all-gather | bytes 589824 | tf_op jit(solution)/shard_map/all_gather | solution.py:504
  162.9 1.4 unpack_gradients.1
  (44 shorter events, 0.3 us)
Async XLA Ops:
  0.6 49.3 %copy-start = (bf16[1,12,104,256]{3,2,1,0:T(8,128)(2,1)S(1)}, bf16[1,12,104,256]{3,2,1,0:T(8,128)(2,1)}, u32[]{:S(2)}) copy-start(bf16[1,12,104,256]{3,2,1,0:T(8,128)(2,1)} %param.14) | copy-start | bytes 1916932
  0.6 42.7 %copy-start.1 = (bf16[3,32,32,3,3,3]{2,1,5,4,3,0:T(8,128)(2,1)S(1)}, bf16[3,32,32,3,3,3]{2,1,5,4,3,0:T(8,128)(2,1)}, u32[]{:S(2)}) copy-start(bf16[3,32,32,3,3,3]{2,1,5,4,3,0:T(8,128)(2,1)} %param.21) | copy-start | bytes 497668
  0.7 49.3 %copy-start.3 = (f32[1,32,104]{2,1,0:T(8,128)S(1)}, f32[1,32,104]{2,1,0:T(8,128)}, u32[]{:S(2)}) copy-start(f32[1,32,104]{2,1,0:T(8,128)} %refs_4_.1) | copy-start | bytes 39940
  0.7 49.3 %copy-start.2 = (f32[1,32,104]{2,1,0:T(8,128)S(1)}, f32[1,32,104]{2,1,0:T(8,128)}, u32[]{:S(2)}) copy-start(f32[1,32,104]{2,1,0:T(8,128)} %refs_3_.1) | copy-start | bytes 39940
  0.7 0.8 copy-start.4
  1.5 0.7 copy-start.6
  2.1 41.1 %copy-start.7 = (bf16[32,1,3,3,3]{0,4,3,2,1:T(4,128)(2,1)S(1)}, bf16[32,1,3,3,3]{0,4,3,2,1:T(4,128)(2,1)}, u32[]{:S(2)}) copy-start(bf16[32,1,3,3,3]{0,4,3,2,1:T(4,128)(2,1)} %param.20) | copy-start | bytes 5188
  2.1 41.2 %copy-start.8 = (bf16[1,32,3,3,3]{1,4,3,2,0:T(4,128)(2,1)S(1)}, bf16[1,32,3,3,3]{1,4,3,2,0:T(4,128)(2,1)}, u32[]{:S(2)}) copy-start(bf16[1,32,3,3,3]{1,4,3,2,0:T(4,128)(2,1)} %param.22) | copy-start | bytes 5188
  2.1 47.8 %copy-start.5 = (s32[1,12]{1,0:T(1,128)S(1)}, s32[1,12]{1,0:T(1,128)}, u32[]{:S(2)}) copy-start(s32[1,12]{1,0:T(1,128)} %refs_0_.1) | copy-start | bytes 148
  2.7 27.2 %all-to-all-start = ((bf16[16,8,128]{2,1,0:T(8,128)(2,1)}), bf16[16,8,128]{2,1,0:T(8,128)(2,1)S(1)}, u32[]{:S(2)}, u32[]{:S(2)}) async-start(bf16[16,8,128]{2,1,0:T(8,128)(2,1)} %first_message.1), calls=%async_computation | async-start | bytes 65536 | tf_op jit(solution)/shard_map/all_to_all | solution.py:614
  36.3 19.2 %copy-start.9 = (f32[3,2,128]{2,1,0:T(2,128)S(1)}, f32[3,2,128]{2,1,0:T(2,128)}, u32[]{:S(2)}) copy-start(f32[3,2,128]{2,1,0:T(2,128)} %param.13) | copy-start | bytes 9220
  36.3 19.3 %copy-start.10 = (f32[3,2,128]{2,1,0:T(2,128)S(1)}, f32[3,2,128]{2,1,0:T(2,128)}, u32[]{:S(2)}) copy-start(f32[3,2,128]{2,1,0:T(2,128)} %param.23) | copy-start | bytes 9220
  36.3 13.6 %all-to-all-start.1 = ((f32[16,12,128]{2,1,0:T(8,128)}), f32[16,12,128]{2,1,0:T(8,128)S(1)}, u32[]{:S(2)}, u32[]{:S(2)}) async-start(f32[16,12,128]{2,1,0:T(8,128)} %broadcast_in_dim.20), calls=%async_computation.1 | async-start | bytes 262144 | tf_op jit(solution)/shard_map/all_to_all | solution.py:500
  51.8 16.3 %all-to-all-start.2 = ((f32[16,12,256]{2,1,0:T(8,128)}), f32[16,12,256]{2,1,0:T(8,128)S(1)}, u32[]{:S(2)}, u32[]{:S(2)}) async-start(f32[16,12,256]{2,1,0:T(8,128)} %back_terms.1), calls=%async_computation.2 | async-start | bytes 524288 | tf_op jit(solution)/shard_map/all_to_all | solution.py:649
  55.7 12.8 %collective-permute-start.3 = (f32[24,128]{1,0:T(8,128)S(1)}, f32[24,128]{1,0:T(8,128)S(1)}, u32[]{:S(2)}, u32[]{:S(2)}) collective-permute-start(f32[24,128]{1,0:T(8,128)S(1)} %select_maximum_fusion), channel_id=1, source_target_pairs={{64,0},{80,16},{96,32},{112,48},{128,64},{144,80},{160,96},{176,11... | collective-permute-start | bytes 36872 | tf_op jit(solution)/shard_map/ppermute | solution.py:628
  57.0 11.5 %collective-permute-start.2 = (f32[24,128]{1,0:T(8,128)S(1)}, f32[24,128]{1,0:T(8,128)S(1)}, u32[]{:S(2)}, u32[]{:S(2)}) collective-permute-start(f32[24,128]{1,0:T(8,128)S(1)} %select_maximum_fusion), channel_id=1, source_target_pairs={{32,0},{48,16},{64,32},{80,48},{96,64},{112,80},{128,96},{144,112}... | collective-permute-start | bytes 36872 | tf_op jit(solution)/shard_map/ppermute | solution.py:628
  58.3 10.2 %collective-permute-start.1 = (f32[24,128]{1,0:T(8,128)S(1)}, f32[24,128]{1,0:T(8,128)S(1)}, u32[]{:S(2)}, u32[]{:S(2)}) collective-permute-start(f32[24,128]{1,0:T(8,128)S(1)} %select_maximum_fusion), channel_id=1, source_target_pairs={{0,32},{16,48},{32,64},{48,80},{64,96},{80,112},{96,128},{112,144}... | collective-permute-start | bytes 36872 | tf_op jit(solution)/shard_map/ppermute | solution.py:628
  62.3 6.2 %collective-permute-start = (f32[24,128]{1,0:T(8,128)S(1)}, f32[24,128]{1,0:T(8,128)S(1)}, u32[]{:S(2)}, u32[]{:S(2)}) collective-permute-start(f32[24,128]{1,0:T(8,128)S(1)} %select_maximum_fusion), channel_id=1, source_target_pairs={{0,64},{16,80},{32,96},{48,112},{64,128},{80,144},{96,160},{112,17... | collective-permute-start | bytes 36872 | tf_op jit(solution)/shard_map/ppermute | solution.py:628
  108.1 11.6 %all-to-all-start.4 = ((f32[16,48,128]{2,1,0:T(8,128)}), f32[16,48,128]{2,1,0:T(8,128)S(1)}, u32[]{:S(2)}, u32[]{:S(2)}) async-start(f32[16,48,128]{2,1,0:T(8,128)} %bitcast.17), calls=%async_computation.4 | async-start | bytes 786432 | tf_op jit(solution)/shard_map/all_to_all | solution.py:512
  124.7 21.3 %all-to-all-start.5 = ((bf16[16,24,128]{2,1,0:T(8,128)(2,1)}), bf16[16,24,128]{2,1,0:T(8,128)(2,1)S(1)}, u32[]{:S(2)}, u32[]{:S(2)}) async-start(bf16[16,24,128]{2,1,0:T(8,128)(2,1)} %broadcast_in_dim.21), calls=%async_computation.5 | async-start | bytes 196608 | tf_op jit(solution)/shard_map/all_to_all | solution.py:500
  146.7 10.4 %all-to-all-start.6 = ((f32[16,24,128]{2,1,0:T(8,128)}), f32[16,24,128]{2,1,0:T(8,128)S(1)}, u32[]{:S(2)}, u32[]{:S(2)}) async-start(f32[16,24,128]{2,1,0:T(8,128)} %broadcast_in_dim.22), calls=%async_computation.6 | async-start | bytes 393216 | tf_op jit(solution)/shard_map/all_to_all | solution.py:500
